TPU v7x, 32 devices: a whole 2x2x4 slice. The times are simulated.
32 devices in a mesh: head: 4 (over y, x), ctx: 8 (over z, core).
Axes of the slice: x: 2, y: 2, z: 4, core: 2. Of those that a mesh axis runs over, the one named last changes fastest.
Arguments:
- queries: bfloat16 [8, 512, 8192], P('ctx', 'head'), may hold values from -6 to 6
- keys: bfloat16 [8, 512, 8192], P('ctx', 'head'), may hold values from -6 to 6
- values: bfloat16 [8, 512, 8192], P('ctx', 'head'), may hold values from -6 to 6
- gate: bfloat16 [8, 512, 8192], P('ctx', 'head'), may hold values from -6 to 6
- log_decay: float32 [8, 64, 512], P('ctx', 'head'), may hold values from -1 to 0, as said below
- norm_gain: bfloat16 [8192], P('head'), may hold values from 0.099609375 to 1.8984375
Outputs:
- attended: bfloat16 [8, 512, 8192], P('ctx', 'head')
Inputs may be any that keep to these rules, and one draw needn't show every extreme that they name: `log_decay`: every entry is negative.
All inputs are finite; a program needn't handle non-finite values.
Results may differ from a plain program's by a relative error of at most 0.0048.
Values may be sent and summed in bfloat16 or wider, within the bound.
No kernel may reach another device: no remote copies, remote signals or barrier semaphores. Data moves between devices by JAX's collectives and lax.ppermute only.
A program may use at most 192 MiB of HBM per device.

v0:
```python
import functools

import jax
import jax.numpy as jnp
from jax import lax
from jax.experimental import pallas as pl
from jax.experimental.pallas import tpu as pltpu
from jax.sharding import Mesh
from jax.sharding import PartitionSpec as P

GROUPS = 2
STEP = 8
EXTRA = 16
VMEM_LIMIT = 8 * 1024 * 1024
NN = (((1,), (0,)), ((), ()))
NT = (((1,), (1,)), ((), ()))
TN = (((0,), (0,)), ((), ()))


def dot(a, b, dims, precision=None):
    return lax.dot_general(a, b, dims, precision=precision, preferred_element_type=jnp.float32)


def split(value):
    first = value.astype(jnp.bfloat16)
    left = value - first.astype(jnp.float32)
    second = left.astype(jnp.bfloat16)
    return first, second, (left - second.astype(jnp.float32)).astype(jnp.bfloat16)


def sums_over(decay, keep):
    heads, length = decay.shape
    rows = lax.broadcasted_iota(jnp.int32, (length, length), 0)
    columns = lax.broadcasted_iota(jnp.int32, (length, length), 1)
    chosen = jnp.where(keep(rows, columns), 1.0, 0.0).astype(jnp.bfloat16)
    parts = [part.astype(jnp.float32) for part in split(decay)]
    both = dot(jnp.concatenate(parts, axis=0).astype(jnp.bfloat16), chosen, NN)
    return both[:heads] + (both[heads : 2 * heads] + both[2 * heads :])


def join(rows, head):
    wide = rows.astype(jnp.float32)
    return wide[3 * head : 3 * head + 1] + (
        wide[3 * head + 1 : 3 * head + 2] + wide[3 * head + 2 : 3 * head + 3]
    )


def decay_rows(totals):
    parts = [part for total in totals for part in split(total)]
    blank = jnp.zeros((EXTRA - len(parts), totals[0].shape[1]), jnp.bfloat16)
    return jnp.concatenate(parts + [blank], axis=0)


def pack_kernel(parts, decay_ref, packed_ref):
    length = packed_ref.shape[2]
    for place in range(packed_ref.shape[0]):
        start = place % parts * length
        packed_ref[place] = decay_ref[0, :, start : start + length]


def gate_kernel(half, begin, share, dim, me_ref, gate_ref, *refs):
    *results, done_ref, copy_ref, result_ref, done = refs[-6:]
    width = share * dim
    loads, stores = [], []
    for at, out_ref in enumerate(results):
        first = (me_ref[1] if at == 0 else 1 - me_ref[1]) * half + begin
        columns = pl.ds(pl.multiple_of(first * dim, width), width)
        loads.append(pltpu.make_async_copy(gate_ref.at[0, :, columns], copy_ref.at[at], done.at[at]))
        stores.append(pltpu.make_async_copy(result_ref.at[at], out_ref, done.at[2 + at]))
        loads[-1].start()
    for at in range(len(results)):
        loads[at].wait()
        for head in range(share):
            c = slice(head * dim, (head + 1) * dim)
            turned = jnp.tanh(0.5 * copy_ref[at, :, c].astype(jnp.float32))
            result_ref[at, :, c] = 0.5 + 0.5 * turned
        stores[at].start()
    done_ref[...] = jnp.zeros_like(done_ref)
    for store in stores:
        store.wait()


def heads_at(first, head, dim):
    return pl.ds(pl.multiple_of((first + head) * dim, dim), dim)


def decays_at(decay_ref, block, first):
    local = decay_ref.shape[1]
    parts = decay_ref.shape[0] // 2
    rows = pl.ds(pl.multiple_of(first % local, STEP), STEP)
    return decay_ref[block * parts + first // local, rows, :]


def state_kernel(dim, owned, half, begin, masks, me_ref, decay_ref, *refs):
    arrays, slots = refs[:4], refs[-3 - 2 * len(masks) : -3]
    stacked_ref, copy_ref, done = refs[-3:]
    part, core = me_ref[0], me_ref[1]
    firsts = [core * half + begin + ((part >> 1) ^ mask) * STEP for mask in masks]
    width = STEP * dim
    moves = [
        [
            pltpu.make_async_copy(
                ref.at[0, :, pl.ds(pl.multiple_of(first * dim, width), width)],
                copy_ref.at[turn, at],
                done.at[turn, at],
            )
            for at, ref in enumerate(arrays)
        ]
        for turn, first in enumerate(firsts)
    ]
    for move in sum(moves, []):
        move.start()
    for turn, first in enumerate(firsts):
        for source in range(2):
            block = core if source == 0 else 1 - core
            decay = decays_at(decay_ref, block, first)
            weight = jnp.exp(sums_over(decay, lambda u, s: u > s))
            whole = jnp.broadcast_to(jnp.sum(decay, axis=1, keepdims=True), (STEP, dim))
            for move in moves[turn][2 * source : 2 * source + 2]:
                move.wait()
            states = []
            for head in range(STEP):
                c = slice(head * dim, (head + 1) * dim)
                decayed = copy_ref[turn, 2 * source, :, c].T.astype(jnp.float32)
                decayed = (decayed * weight[head : head + 1, :]).astype(jnp.bfloat16)
                states.append(dot(decayed, copy_ref[turn, 2 * source + 1, :, c], NN))
            for head in range(STEP):
                owner, spot = divmod(head, owned)
                span = slice(spot * dim, (spot + 1) * dim)
                stacked_ref[turn, owner, block, span, :] = states[head].astype(jnp.bfloat16)
            for at in range(2):
                stacked_ref[turn, at, block, owned * dim :, :] = decay_rows(
                    [whole[head : head + 1] for head in range(at * owned, (at + 1) * owned)]
                )
        for at in range(2):
            slots[2 * turn + at][...] = stacked_ref[turn, (part & 1) ^ at]


def inside_kernel(
    dim, half, begin, count, other, me_ref, queries_ref, keys_ref, values_ref, decay_ref, *rest
):
    inside_ref, down_ref, done_ref = rest[-3:]
    core = me_ref[1]
    length = decay_ref.shape[2]
    rows = lax.broadcasted_iota(jnp.int32, (length, length), 0)
    causal = rows >= lax.broadcasted_iota(jnp.int32, (length, length), 1)
    for turn in range(count // STEP):
        first = (1 - core if other else core) * half + begin + turn * STEP
        decay = decays_at(decay_ref, core, first)
        across = sums_over(decay, lambda u, s: u <= s)
        down = across.T
        down_ref[turn] = jnp.exp(down)
        columns = [heads_at(first, head, dim) for head in range(STEP)]
        scores = [dot(queries_ref[0, :, c], keys_ref[0, :, c], NT) for c in columns]
        weights = []
        for head in range(STEP):
            gap = down[:, head : head + 1] - across[head : head + 1, :]
            weight = scores[head] * jnp.exp(jnp.where(causal, gap, -jnp.inf))
            weights.append(weight.astype(jnp.bfloat16))
        for head, c in enumerate(columns):
            at = (turn * STEP + head) * dim
            inside_ref[:, at : at + dim] = dot(weights[head], values_ref[0, :, c], NN)
    done_ref[...] = jnp.zeros_like(done_ref)


def gather_states(part, slots, stacked_ref):
    parts = len(slots)
    for slot, slot_ref in enumerate(slots):
        for block in range(2):
            stacked_ref[block * parts + (part ^ slot)] = slot_ref[block]


def total_kernel(dim, owned, parts, me_ref, *refs):
    total_ref, stacked_ref = refs[-2:]
    gather_states(me_ref[0], refs[:parts], stacked_ref)
    count = 2 * parts
    extra = [stacked_ref[at, owned * dim :, :] for at in range(count)]
    sums = []
    for head in range(owned):
        span = slice(head * dim, (head + 1) * dim)
        after = jnp.zeros((1, dim), jnp.float32)
        total = stacked_ref[count - 1, span, :].astype(jnp.float32)
        for at in range(count - 2, -1, -1):
            after += join(extra[at + 1], head)
            total += jnp.exp(after) * stacked_ref[at, span, :].astype(jnp.float32)
        total_ref[span, :] = total.astype(jnp.bfloat16)
        sums.append(after + join(extra[0], head))
    total_ref[owned * dim :, :] = decay_rows(sums)


def widen_kernel(dim, owned, step, me_ref, mine_ref, other_ref, *refs):
    out_ref = refs[-1]
    later = (me_ref[2] >> step) % 2 == 1
    extra = mine_ref[owned * dim :, :], other_ref[owned * dim :, :]
    sums = []
    for head in range(owned):
        span = slice(head * dim, (head + 1) * dim)
        mine, other = join(extra[0], head), join(extra[1], head)
        total = jnp.where(later, 1.0, jnp.exp(other)) * mine_ref[span, :].astype(jnp.float32)
        total += jnp.where(later, jnp.exp(mine), 1.0) * other_ref[span, :].astype(jnp.float32)
        out_ref[span, :] = total.astype(jnp.bfloat16)
        sums.append(mine + other)
    out_ref[owned * dim :, :] = decay_rows(sums)


def prefix_kernel(dim, owned, parts, stretches, me_ref, gain_ref, *refs):
    stacked_ref, prefix_ref = refs[-2:]
    slots, totals = refs[:parts], refs[parts : parts + stretches]
    count = 2 * parts
    results = refs[-2 - parts : -2]
    gather_states(me_ref[0], slots, stacked_ref)
    extra = [stacked_ref[at, owned * dim :, :] for at in range(count)]
    more = [total_ref[owned * dim :, :] for total_ref in totals]
    earlier = [
        ((me_ref[2] >> step) % 2).astype(jnp.float32) for step in range(len(totals))
    ]
    for head in range(owned):
        span = slice(head * dim, (head + 1) * dim)
        prefix = jnp.zeros((dim, dim), jnp.float32)
        after = jnp.zeros((1, dim), jnp.float32)
        for turn, total_ref in enumerate(totals):
            factor = earlier[turn] * jnp.exp(after)
            prefix += factor * total_ref[span, :].astype(jnp.float32)
            after += earlier[turn] * join(more[turn], head)
        for at in range(count):
            prefix_ref[at, span, :] = prefix.astype(jnp.bfloat16)
            if at < count - 1:
                prefix = jnp.exp(join(extra[at], head)) * prefix
                prefix += stacked_ref[at, span, :].astype(jnp.float32)
    size = owned * dim
    for slot, result_ref in enumerate(results):
        for block in range(2):
            result_ref[block * size : (block + 1) * size, :] = prefix_ref[
                block * parts + (me_ref[0] ^ slot)
            ]
        result_ref[2 * size :, :] = gain_ref[...]


def collect(part, block, slots, prefix_ref, gain_ref):
    parts, size, _ = prefix_ref.shape
    local = gain_ref.shape[0] // parts
    for slot, slot_ref in enumerate(slots):
        owner = part ^ slot
        prefix_ref[owner] = slot_ref[pl.ds(pl.multiple_of(block * size, size), size), :]
        rows = pl.ds(pl.multiple_of(owner * local, local), local)
        gain_ref[rows, :] = slot_ref[2 * size :, :].astype(jnp.float32)


def merge_kernel(parts, me_ref, *refs):
    *others, gain_ref, prefix_ref = refs[parts:] if len(refs) == parts + 4 else refs[parts + 1 :]
    collect(me_ref[0], 1 - me_ref[1], refs[:parts], prefix_ref, gain_ref)
    each = parts // len(others)
    for turn, other_ref in enumerate(others):
        other_ref[...] = prefix_ref[turn * each : (turn + 1) * each]


def output_kernel(
    dim, owned, half, begin, count, parts, me_ref,
    queries_ref, inside_ref, down_ref, gate_ref, *refs,
):
    out_ref, done_ref, prefix_ref, gain_ref, result_ref, sent = refs[-6:]
    core = me_ref[1]
    if parts is None:
        *others, gains = refs[:3]
        each = others[0].shape[0]
        prefixes = [others[at // each].at[at % each] for at in range(each * len(others))]
    else:
        collect(me_ref[0], core, refs[:parts], prefix_ref, gain_ref)
        prefixes, gains = [prefix_ref.at[at] for at in range(parts)], gain_ref
    average = jnp.full((dim, dim), 1.0 / dim, jnp.bfloat16)
    moves = []
    for turn in range(count // STEP):
        first = (1 - core if parts is None else core) * half + begin + turn * STEP
        gain = gains[pl.ds(pl.multiple_of(first, STEP), STEP), :]
        down = down_ref[turn]
        columns = [heads_at(first, head, dim) for head in range(STEP)]
        carried = []
        for head, c in enumerate(columns):
            owner, spot = divmod(turn * STEP + head, owned)
            prefix = prefixes[owner][spot * dim : (spot + 1) * dim, :]
            carried.append(dot(queries_ref[0, :, c], prefix, NN))
        mixed, means = [], []
        for head in range(STEP):
            at = (turn * STEP + head) * dim
            mixed.append(inside_ref[:, at : at + dim] + carried[head] * down[:, head : head + 1])
            means.append(dot((mixed[head] * mixed[head]).astype(jnp.bfloat16), average, NN))
        for head in range(STEP):
            at = (turn * STEP + head) * dim
            factor = gain[head : head + 1, :] * gate_ref[:, at : at + dim]
            normed = mixed[head] * lax.rsqrt(means[head] + 1e-06) * factor
            result_ref[turn, :, head * dim : (head + 1) * dim] = normed.astype(jnp.bfloat16)
        width = STEP * dim
        moves.append(
            pltpu.make_async_copy(
                result_ref.at[turn],
                out_ref.at[0, :, pl.ds(pl.multiple_of(first * dim, width), width)],
                sent.at[turn],
            )
        )
        moves[-1].start()
    done_ref[...] = jnp.zeros_like(done_ref)
    for move in moves:
        move.wait()


def kernel_call(body, name, in_specs, out_specs, out_shape, scratch=(), aliases={}, cost=0):
    return pl.pallas_call(
        body,
        grid_spec=pltpu.PrefetchScalarGridSpec(
            num_scalar_prefetch=1,
            grid=(),
            in_specs=in_specs,
            out_specs=out_specs,
            scratch_shapes=scratch,
        ),
        out_shape=out_shape,
        input_output_aliases=aliases,
        compiler_params=pltpu.CompilerParams(vmem_limit_bytes=VMEM_LIMIT),
        cost_estimate=pl.CostEstimate(
            flops=int(1e9 * cost) + 1, transcendentals=0, bytes_accessed=1
        ),
        name=name,
    )


def on_device(parts, planes, queries, keys, values, gate, log_decay, norm_gain):
    _, length, width = queries.shape
    local = log_decay.shape[1]
    dim = width // (local * parts)
    count = 2 * parts
    half = local * parts // 2
    owned = half // (GROUPS * parts)
    rows = owned * dim + EXTRA
    me = jnp.stack([lax.axis_index(axis) for axis in ("head", "core", "z")]).astype(jnp.int32)
    swap = [(0, 1), (1, 0)]

    values_other = lax.ppermute(values, "core", swap)
    keys_other = lax.ppermute(keys, "core", swap)
    packed = pl.pallas_call(
        functools.partial(pack_kernel, parts),
        out_shape=jax.ShapeDtypeStruct((count, local, length), jnp.float32),
        name="pack",
    )(log_decay)
    decay = lax.all_to_all(packed, ("core", "head"), 0, 0, tiled=True)
    gain = norm_gain.reshape(local, dim)

    vmem = pl.BlockSpec(memory_space=pltpu.VMEM)
    hbm = pl.BlockSpec(memory_space=pl.ANY)

    def in_vmem(array):
        return pltpu.with_memory_space_constraint(array, pltpu.VMEM)

    def in_hbm(array):
        return pltpu.with_memory_space_constraint(array, pltpu.HBM)

    own = in_hbm(keys), in_hbm(values)
    share = half // GROUPS
    keys, values, queries = (in_vmem(array) for array in (keys, values, queries))

    def exchange(slots):
        arrived = list(slots)
        for slot in sorted(range(1, parts), key=lambda s: -bin(s).count("1")):
            pairs = [(at, at ^ slot) for at in range(parts)]
            arrived[slot] = lax.ppermute(slots[slot], "head", pairs)
        return arrived

    before = ()
    held = []
    state_type = jax.ShapeDtypeStruct((2, rows, dim), jnp.bfloat16)
    token = jax.ShapeDtypeStruct((8, 128), jnp.float32)
    inside = {}

    def inside_part(before, cost=0):
        group, other = divmod(len(inside), 2)
        *inside[group, other], made = kernel_call(
            functools.partial(inside_kernel, dim, half, group * share, share, other),
            f"inside{group}_{other}",
            [vmem] * 4 + [hbm] * len(before),
            [vmem] * 3,
            [
                pltpu.VMEM((length, share * dim), jnp.float32),
                jax.ShapeDtypeStruct((share // STEP, length, STEP), jnp.float32),
                token,
            ],
            cost=cost,
        )(me, queries, keys, values, decay, *before)
        return (made,)

    gate_type = jax.ShapeDtypeStruct((length, share * dim), jnp.float32)
    gates = {}

    def gates_of(group, before):
        gates[group, 0], gates[group, 1], made = kernel_call(
            functools.partial(gate_kernel, half, group * share, share, dim),
            f"gates{group}",
            [hbm] * (1 + len(before)),
            [hbm, hbm, vmem],
            [pltpu.HBM(gate_type.shape, gate_type.dtype)] * 2 + [token],
            [
                pltpu.VMEM((2, length, share * dim), jnp.bfloat16),
                pltpu.VMEM((2,) + gate_type.shape, jnp.float32),
                pltpu.SemaphoreType.DMA((4,)),
            ],
        )(me, in_hbm(gate), *before)
        return (made,)

    for group in range(GROUPS):
        slots = {}
        for masks in ((1,), (0,)) if group == 0 else ((1, 0),):
            state = kernel_call(
                functools.partial(state_kernel, dim, owned, half, group * share, masks),
                f"state{group}_{masks[0]}",
                [vmem] + [hbm] * (4 + len(before)),
                [vmem] * (2 * len(masks)),
                [state_type] * (2 * len(masks)),
                [
                    pltpu.VMEM((len(masks), 2) + state_type.shape, jnp.bfloat16),
                    pltpu.VMEM((len(masks), 4, length, STEP * dim), jnp.bfloat16),
                    pltpu.SemaphoreType.DMA((len(masks), 4)),
                ],
            )(me, decay, *own, keys_other, values_other, *before)
            before = tuple(state[:1])
            for at, array in enumerate(state):
                slots[2 * masks[at // 2] + at % 2] = array
        held.append(exchange([slots[slot] for slot in range(parts)]))
        if group == 0:
            before = inside_part(inside_part(before))

    arrived = []
    stacked = pltpu.VMEM((count, rows, dim), jnp.bfloat16)
    total_type = jax.ShapeDtypeStruct((rows, dim), jnp.bfloat16)

    def with_plane(total, step):
        pairs = [(at, at ^ (1 << step)) for at in range(planes)]
        return lax.ppermute(total, "z", pairs)

    def widen(group, step, total, other, before):
        return kernel_call(
            functools.partial(widen_kernel, dim, owned, step),
            f"widen{group}_{step}",
            [vmem] * 2 + [hbm] * len(before),
            vmem,
            total_type,
        )(me, total, other, *before)

    def prefix_of(group, before):
        stretches = arrived[group]
        return kernel_call(
            functools.partial(prefix_kernel, dim, owned, parts, len(stretches)),
            f"prefix{group}",
            [vmem] * (1 + parts + len(stretches)) + [hbm] * len(before),
            [vmem] * parts,
            [prefix_type] * parts,
            [stacked, pltpu.VMEM((count, size, dim), jnp.bfloat16)],
        )(me, gain, *held[group], *stretches, *before)

    size = owned * dim
    prefix_type = jax.ShapeDtypeStruct((2 * size + local, dim), jnp.bfloat16)
    prefixes = []
    for group in range(GROUPS):
        total = kernel_call(
            functools.partial(total_kernel, dim, owned, parts),
            f"total{group}",
            [vmem] * parts + [hbm],
            vmem,
            total_type,
            [stacked],
        )(me, *held[group], *before)
        before = (total,)
        stretches = [with_plane(total, 0)]
        arrived.append(stretches)
        if group > 0:
            prefix = prefix_of(group - 1, before)
            before = tuple(prefix[:1])
            prefixes.append(exchange(prefix))
        if group < GROUPS - 1:
            before = inside_part(before)
        for step in range(1, planes.bit_length() - 1):
            total = widen(group, step - 1, total, stretches[-1], before)
            before = (total,)
            stretches.append(with_plane(total, step))
        while group == GROUPS - 1 and len(inside) < 2 * GROUPS:
            before = inside_part(before, 2)
        before = gates_of(group, before)
    prefix = prefix_of(GROUPS - 1, before)
    before = tuple(prefix[:1])
    prefixes.append(exchange(prefix))

    part_type = jax.ShapeDtypeStruct((parts, size, dim), jnp.bfloat16)
    half_type = jax.ShapeDtypeStruct((parts // 2, size, dim), jnp.bfloat16)
    gain_type = jax.ShapeDtypeStruct((parts * local, dim), jnp.float32)

    def merge(group, before, cost):
        return kernel_call(
            functools.partial(merge_kernel, parts),
            f"merge{group}",
            [vmem] * parts + [hbm] * len(before),
            [vmem] * 3,
            [half_type, half_type, gain_type],
            [pltpu.VMEM(part_type.shape, part_type.dtype)],
            cost=cost,
        )(me, *prefixes[group], *before)

    def output(group, other, received, out, before, cost=0):
        *out, made = kernel_call(
            functools.partial(
                output_kernel, dim, owned, half, group * share, share, None if other else parts
            ),
            f"output{group}_{other}",
            [vmem] * (4 + len(received)) + [hbm] * (len(out) + len(before)),
            [hbm, vmem],
            [pltpu.HBM((1, length, width), jnp.bfloat16), token],
            [
                pltpu.VMEM(part_type.shape, part_type.dtype),
                pltpu.VMEM(gain_type.shape, gain_type.dtype),
                pltpu.VMEM((share // STEP, length, STEP * dim), jnp.bfloat16),
                pltpu.SemaphoreType.DMA((share // STEP,)),
            ],
            aliases={5 + len(received): 0} if out else {},
            cost=cost,
        )(
            me, queries, in_vmem(inside[group, other][0]), inside[group, other][1],
            in_vmem(gates[group, other]), *received, *out, *before,
        )
        return out, (made,)

    out = ()
    for group in range(GROUPS):
        last = group == GROUPS - 1
        if not last:
            out, before = output(group, 0, prefixes[group], out, before)
        *others, gains = merge(group, before, 0)
        others = [lax.ppermute(other, "core", swap) for other in others]
        before = (gains,)
        if last:
            out, before = output(group, 0, prefixes[group], out, before, cost=20)
        out, before = output(group, 1, (*others, gains), out, before)
    return out[0]


def solution(mesh):
    parts, blocks = mesh.shape["head"], mesh.shape["ctx"]
    names = mesh.axis_names
    at = names.index("ctx")
    shape = mesh.devices.shape[:at] + (blocks // 2, 2) + mesh.devices.shape[at + 1 :]
    finer = Mesh(mesh.devices.reshape(shape), names[:at] + ("z", "core") + names[at + 1 :])
    tokens = P(("z", "core"), "head", None)
    return jax.shard_map(
        functools.partial(on_device, parts, blocks // 2),
        mesh=finer,
        in_specs=(tokens,) * 5 + (P("head"),),
        out_specs=tokens,
        check_vma=False,
    )
```

profile of v0, /device:TPU:0, one launch (start us, length us, event | category | flops | bytes accessed | tf_op | source)
XLA Modules:
  0.0 75.7 jit_solution(14024002137033453169)
XLA Ops:
  0.5 1.4 %pack.1 = f32[8,16,128]{2,1,0:T(8,128)} custom-call(f32[1,16,512]{2,1,0:T(8,128)} %decay_ref.1), custom_call_target="tpu_custom_call" | custom-call | tf_op jit(solution)/shard_map/pack/pallas_call | solution.py:339
  1.9 5.2 %all-to-all-start = ((f32[8,16,128]{2,1,0:T(8,128)}), f32[8,16,128]{2,1,0:T(8,128)S(1)}, u32[]{:S(2)}, u32[]{:S(2)}) async-start(f32[8,16,128]{2,1,0:T(8,128)} %pack.1), calls=%async_computation | async-start | bytes 131072 | tf_op jit(solution)/shard_map/all_to_all | solution.py:344
  7.1 4.9 %all-to-all-done.decay_ref = f32[8,16,128]{2,1,0:T(8,128)S(1)} async-done(((f32[8,16,128]{2,1,0:T(8,128)}), f32[8,16,128]{2,1,0:T(8,128)S(1)}, u32[]{:S(2)}, u32[]{:S(2)}) %all-to-all-start) | async-done | bytes 65568 | tf_op jit(solution)/shard_map/all_to_all | solution.py:344
  12.0 2.2 %state0_1.1 = (bf16[2,528,128]{2,1,0:T(8,128)(2,1)S(1)}, bf16[2,528,128]{2,1,0:T(8,128)(2,1)S(1)}) custom-call(s32[3]{0:T(128)S(1)} %pad_add_fusion.me_ref, f32[8,16,128]{2,1,0:T(8,128)S(1)} %all-to-all-done.decay_ref, bf16[1,128,8192]{2,1,0:T(8,128)(2,1)} %keys_ref.7, bf16[1,128,8192]{2,1,0:T(8,128)(2,1)} %values_ref.7, ...), custom_call_target="tpu_custom_call" | custom-call | flops 1 | bytes 1 | tf_op jit(solution)/shard_map/state0_1/pallas_call | solution.py:410
  14.9 1.4 %collective-permute-start.6 = (bf16[2,528,128]{2,1,0:T(8,128)(2,1)S(1)}, bf16[2,528,128]{2,1,0:T(8,128)(2,1)S(1)}, u32[]{:S(2)}, u32[]{:S(2)}) collective-permute-start(bf16[2,528,128]{2,1,0:T(8,128)(2,1)S(1)} %get-tuple-element.52.refs_4_), channel_id=1, source_target_pairs={{0,16},{8,24},{16,0},{24,8},{1,17},{9,25},{17,1},{25,9},{2,18},{10... | collective-permute-start | bytes 811016 | tf_op jit(solution)/shard_map/ppermute | solution.py:364
  16.3 2.2 %state0_0.1 = (bf16[2,528,128]{2,1,0:T(8,128)(2,1)S(1)}, bf16[2,528,128]{2,1,0:T(8,128)(2,1)S(1)}) custom-call(s32[3]{0:T(128)S(1)} %pad_add_fusion.me_ref, f32[8,16,128]{2,1,0:T(8,128)S(1)} %all-to-all-done.decay_ref, bf16[1,128,8192]{2,1,0:T(8,128)(2,1)} %keys_ref.7, bf16[1,128,8192]{2,1,0:T(8,128)(2,1)} %values_ref.7, ...), custom_call_target="tpu_custom_call" | custom-call | flops 1 | bytes 1 | tf_op jit(solution)/shard_map/state0_0/pallas_call | solution.py:410
  18.5 1.5 %collective-permute-start.5 = (bf16[2,528,128]{2,1,0:T(8,128)(2,1)S(1)}, bf16[2,528,128]{2,1,0:T(8,128)(2,1)S(1)}, u32[]{:S(2)}, u32[]{:S(2)}) collective-permute-start(bf16[2,528,128]{2,1,0:T(8,128)(2,1)S(1)} %get-tuple-element.60), channel_id=1, source_target_pairs={{0,8},{8,0},{16,24},{24,16},{1,9},{9,1},{17,25},{25,17},{2,10},{10... | collective-permute-start | bytes 811016 | tf_op jit(solution)/shard_map/ppermute | solution.py:364
  20.1 1.7 %inside0_0.1 = (f32[128,2048]{1,0:T(8,128)S(1)}, f32[2,128,8]{2,1,0:T(8,128)S(1)}, f32[8,128]{1,0:T(8,128)S(1)}) custom-call(s32[3]{0:T(128)S(1)} %pad_add_fusion.me_ref, bf16[1,128,8192]{2,1,0:T(8,128)(2,1)S(1)} %copy-done, bf16[1,128,8192]{2,1,0:T(8,128)(2,1)S(1)} %copy-done.1, bf16[1,128,8192]{2,1,0:T(8,128)(2,1)S(1)} %copy-done.3, ...), custom_call_target="tpu_custom_call" | custom-call | flops 1 | bytes 1 | tf_op jit(solution)/shard_map/inside0_0/pallas_call | solution.py:375
  21.7 1.7 %inside0_1.1 = (f32[128,2048]{1,0:T(8,128)S(1)}, f32[2,128,8]{2,1,0:T(8,128)S(1)}, f32[8,128]{1,0:T(8,128)S(1)}) custom-call(s32[3]{0:T(128)S(1)} %pad_add_fusion.me_ref, bf16[1,128,8192]{2,1,0:T(8,128)(2,1)S(1)} %copy-done, bf16[1,128,8192]{2,1,0:T(8,128)(2,1)S(1)} %copy-done.1, bf16[1,128,8192]{2,1,0:T(8,128)(2,1)S(1)} %copy-done.3, ...), custom_call_target="tpu_custom_call" | custom-call | flops 1 | bytes 1 | tf_op jit(solution)/shard_map/inside0_1/pallas_call | solution.py:375
  23.5 3.5 %state1_1.1 = (bf16[2,528,128]{2,1,0:T(8,128)(2,1)S(1)}, bf16[2,528,128]{2,1,0:T(8,128)(2,1)S(1)}, bf16[2,528,128]{2,1,0:T(8,128)(2,1)S(1)}, bf16[2,528,128]{2,1,0:T(8,128)(2,1)S(1)}) custom-call(s32[3]{0:T(128)S(1)} %pad_add_fusion.me_ref, f32[8,16,128]{2,1,0:T(8,128)S(1)} %all-to-all-done.decay_ref, bf16[1,128,8192]{2,1,0:T(8,128)(2,1)} %keys_ref.7, ...), custom_call_target="tpu_custom_call" | custom-call | flops 1 | bytes 1 | tf_op jit(solution)/shard_map/state1_1/pallas_call | solution.py:410
  27.5 2.1 %collective-permute-start.4 = (bf16[2,528,128]{2,1,0:T(8,128)(2,1)S(1)}, bf16[2,528,128]{2,1,0:T(8,128)(2,1)S(1)}, u32[]{:S(2)}, u32[]{:S(2)}) collective-permute-start(bf16[2,528,128]{2,1,0:T(8,128)(2,1)S(1)} %get-tuple-element.59), channel_id=1, source_target_pairs={{0,24},{8,16},{16,8},{24,0},{1,25},{9,17},{17,9},{25,1},{2,26},{10... | collective-permute-start | bytes 811016 | tf_op jit(solution)/shard_map/ppermute | solution.py:364
  31.4 1.6 %collective-permute-start.8 = (bf16[528,128]{1,0:T(8,128)(2,1)S(1)}, bf16[528,128]{1,0:T(8,128)(2,1)S(1)}, u32[]{:S(2)}, u32[]{:S(2)}) collective-permute-start(bf16[528,128]{1,0:T(8,128)(2,1)S(1)} %total0.1.rest_0_.mine_ref), channel_id=1, source_target_pairs={{0,2},{2,0},{4,6},{6,4},{1,3},{3,1},{5,7},{7,5},{8,10},{10,8},{12,... | collective-permute-start | bytes 405512 | tf_op jit(solution)/shard_map/ppermute | solution.py:435
  33.0 1.7 %inside1_0.1 = (f32[128,2048]{1,0:T(8,128)S(1)}, f32[2,128,8]{2,1,0:T(8,128)S(1)}, f32[8,128]{1,0:T(8,128)S(1)}) custom-call(s32[3]{0:T(128)S(1)} %pad_add_fusion.me_ref, bf16[1,128,8192]{2,1,0:T(8,128)(2,1)S(1)} %copy-done, bf16[1,128,8192]{2,1,0:T(8,128)(2,1)S(1)} %copy-done.2, bf16[1,128,8192]{2,1,0:T(8,128)(2,1)S(1)} %copy-done.4, ...), custom_call_target="tpu_custom_call" | custom-call | flops 1 | bytes 1 | tf_op jit(solution)/shard_map/inside1_0/pallas_call | solution.py:375
  34.7 1.7 %collective-permute-done.8.other_ref.refs_4_ = bf16[528,128]{1,0:T(8,128)(2,1)S(1)} collective-permute-done((bf16[528,128]{1,0:T(8,128)(2,1)S(1)}, bf16[528,128]{1,0:T(8,128)(2,1)S(1)}, u32[]{:S(2)}, u32[]{:S(2)}) %collective-permute-start.8) | collective-permute-done | bytes 135200 | tf_op jit(solution)/shard_map/ppermute | solution.py:435
  37.1 2.6 %collective-permute-start.10 = (bf16[528,128]{1,0:T(8,128)(2,1)S(1)}, bf16[528,128]{1,0:T(8,128)(2,1)S(1)}, u32[]{:S(2)}, u32[]{:S(2)}) collective-permute-start(bf16[528,128]{1,0:T(8,128)(2,1)S(1)} %widen0_0.1.refs_0_), channel_id=1, source_target_pairs={{0,4},{2,6},{4,0},{6,2},{1,5},{3,7},{5,1},{7,3},{8,12},{10,14},{12... | collective-permute-start | bytes 405512 | tf_op jit(solution)/shard_map/ppermute | solution.py:435
  39.7 3.1 %gates0.1 = (f32[128,2048]{1,0:T(8,128)}, f32[128,2048]{1,0:T(8,128)}, f32[8,128]{1,0:T(8,128)S(1)}) custom-call(s32[3]{0:T(128)S(1)} %pad_add_fusion.me_ref, bf16[1,128,8192]{2,1,0:T(8,128)(2,1)} %gate_ref.3, bf16[528,128]{1,0:T(8,128)(2,1)S(1)} %widen0_0.1.refs_0_), custom_call_target="tpu_custom_call" | custom-call | flops 1 | bytes 1 | tf_op jit(solution)/shard_map/gates0/pallas_call | solution.py:393
  42.9 0.9 %total1.1.refs_6_.mine_ref = bf16[528,128]{1,0:T(8,128)(2,1)S(1)} custom-call(s32[3]{0:T(128)S(1)} %pad_add_fusion.me_ref, bf16[2,528,128]{2,1,0:T(8,128)(2,1)S(1)} %get-tuple-element.56.refs_0_, bf16[2,528,128]{2,1,0:T(8,128)(2,1)S(1)} %collective-permute-done.2.refs_1_, bf16[2,528,128]{2,1,0:T(8,128)(2,1)S(1)} %collective-permute-done.3.refs_2_, ...), custom_call_target="tpu_custom_call" | custom-call | flops 1 | bytes 1 | tf_op jit(solution)/shard_map/total1/pallas_call | solution.py:461
  43.7 1.6 %collective-permute-start.9 = (bf16[528,128]{1,0:T(8,128)(2,1)S(1)}, bf16[528,128]{1,0:T(8,128)(2,1)S(1)}, u32[]{:S(2)}, u32[]{:S(2)}) collective-permute-start(bf16[528,128]{1,0:T(8,128)(2,1)S(1)} %total1.1.refs_6_.mine_ref), channel_id=1, source_target_pairs={{0,2},{2,0},{4,6},{6,4},{1,3},{3,1},{5,7},{7,5},{8,10},{10,8},{12,... | collective-permute-start | bytes 405512 | tf_op jit(solution)/shard_map/ppermute | solution.py:435
  45.4 1.0 %prefix0.1 = (bf16[1040,128]{1,0:T(8,128)(2,1)S(1)}, bf16[1040,128]{1,0:T(8,128)(2,1)S(1)}, bf16[1040,128]{1,0:T(8,128)(2,1)S(1)}, bf16[1040,128]{1,0:T(8,128)(2,1)S(1)}) custom-call(s32[3]{0:T(128)S(1)} %pad_add_fusion.me_ref, bf16[16,128]{1,0:T(8,128)(2,1)S(1)} %bitcast.4, bf16[2,528,128]{2,1,0:T(8,128)(2,1)S(1)} %get-tuple-element.53.rest_0_.refs_0_, ...), custom_call_target="tpu_custom_call" | custom-call | flops 1 | bytes 1 | tf_op jit(solution)/shard_map/prefix0/pallas_call | solution.py:448
  47.0 1.2 %collective-permute-start.16 = (bf16[1040,128]{1,0:T(8,128)(2,1)S(1)}, bf16[1040,128]{1,0:T(8,128)(2,1)S(1)}, u32[]{:S(2)}, u32[]{:S(2)}) collective-permute-start(bf16[1040,128]{1,0:T(8,128)(2,1)S(1)} %get-tuple-element.78), channel_id=1, source_target_pairs={{0,16},{8,24},{16,0},{24,8},{1,17},{9,25},{17,1},{25,9},{2,18},{10... | collective-permute-start | bytes 798728 | tf_op jit(solution)/shard_map/ppermute | solution.py:364
  48.2 1.7 %collective-permute-start.17 = (bf16[1040,128]{1,0:T(8,128)(2,1)S(1)}, bf16[1040,128]{1,0:T(8,128)(2,1)S(1)}, u32[]{:S(2)}, u32[]{:S(2)}) collective-permute-start(bf16[1040,128]{1,0:T(8,128)(2,1)S(1)} %get-tuple-element.79), channel_id=1, source_target_pairs={{0,24},{8,16},{16,8},{24,0},{1,25},{9,17},{17,9},{25,1},{2,26},{10... | collective-permute-start | bytes 798728 | tf_op jit(solution)/shard_map/ppermute | solution.py:364
  50.6 1.9 %collective-permute-start.11 = (bf16[528,128]{1,0:T(8,128)(2,1)S(1)}, bf16[528,128]{1,0:T(8,128)(2,1)S(1)}, u32[]{:S(2)}, u32[]{:S(2)}) collective-permute-start(bf16[528,128]{1,0:T(8,128)(2,1)S(1)} %widen1_0.1.rest_0_), channel_id=1, source_target_pairs={{0,4},{2,6},{4,0},{6,2},{1,5},{3,7},{5,1},{7,3},{8,12},{10,14},{12... | collective-permute-start | bytes 405512 | tf_op jit(solution)/shard_map/ppermute | solution.py:435
  52.5 1.7 %inside1_1.1 = (f32[128,2048]{1,0:T(8,128)S(1)}, f32[2,128,8]{2,1,0:T(8,128)S(1)}, f32[8,128]{1,0:T(8,128)S(1)}) custom-call(s32[3]{0:T(128)S(1)} %pad_add_fusion.me_ref, bf16[1,128,8192]{2,1,0:T(8,128)(2,1)S(1)} %copy-done, bf16[1,128,8192]{2,1,0:T(8,128)(2,1)S(1)} %copy-done.2, bf16[1,128,8192]{2,1,0:T(8,128)(2,1)S(1)} %copy-done.4, ...), custom_call_target="tpu_custom_call" | custom-call | flops 2000000000 | bytes 1 | tf_op jit(solution)/shard_map/inside1_1/pallas_call | solution.py:375
  54.2 3.1 %gates1.1 = (f32[128,2048]{1,0:T(8,128)}, f32[128,2048]{1,0:T(8,128)}, f32[8,128]{1,0:T(8,128)S(1)}) custom-call(s32[3]{0:T(128)S(1)} %pad_add_fusion.me_ref, bf16[1,128,8192]{2,1,0:T(8,128)(2,1)} %gate_ref.3, f32[8,128]{1,0:T(8,128)S(1)} %get-tuple-element.67.refs_0_), custom_call_target="tpu_custom_call" | custom-call | flops 1 | bytes 1 | tf_op jit(solution)/shard_map/gates1/pallas_call | solution.py:393
  57.9 1.0 %prefix1.1 = (bf16[1040,128]{1,0:T(8,128)(2,1)S(1)}, bf16[1040,128]{1,0:T(8,128)(2,1)S(1)}, bf16[1040,128]{1,0:T(8,128)(2,1)S(1)}, bf16[1040,128]{1,0:T(8,128)(2,1)S(1)}) custom-call(s32[3]{0:T(128)S(1)} %pad_add_fusion.me_ref, bf16[16,128]{1,0:T(8,128)(2,1)S(1)} %bitcast.5, bf16[2,528,128]{2,1,0:T(8,128)(2,1)S(1)} %get-tuple-element.56.refs_0_, ...), custom_call_target="tpu_custom_call" | custom-call | flops 1 | bytes 1 | tf_op jit(solution)/shard_map/prefix1/pallas_call | solution.py:448
  59.5 1.2 %collective-permute-start.13 = (bf16[1040,128]{1,0:T(8,128)(2,1)S(1)}, bf16[1040,128]{1,0:T(8,128)(2,1)S(1)}, u32[]{:S(2)}, u32[]{:S(2)}) collective-permute-start(bf16[1040,128]{1,0:T(8,128)(2,1)S(1)} %get-tuple-element.72), channel_id=1, source_target_pairs={{0,16},{8,24},{16,0},{24,8},{1,17},{9,25},{17,1},{25,9},{2,18},{10... | collective-permute-start | bytes 798728 | tf_op jit(solution)/shard_map/ppermute | solution.py:364
  60.7 1.7 %collective-permute-start.14 = (bf16[1040,128]{1,0:T(8,128)(2,1)S(1)}, bf16[1040,128]{1,0:T(8,128)(2,1)S(1)}, u32[]{:S(2)}, u32[]{:S(2)}) collective-permute-start(bf16[1040,128]{1,0:T(8,128)(2,1)S(1)} %get-tuple-element.73), channel_id=1, source_target_pairs={{0,24},{8,16},{16,8},{24,0},{1,25},{9,17},{17,9},{25,1},{2,26},{10... | collective-permute-start | bytes 798728 | tf_op jit(solution)/shard_map/ppermute | solution.py:364
  62.4 2.0 %output0_0.1 = (bf16[1,128,8192]{2,1,0:T(8,128)(2,1)}, f32[8,128]{1,0:T(8,128)S(1)}) custom-call(s32[3]{0:T(128)S(1)} %pad_add_fusion.me_ref, bf16[1,128,8192]{2,1,0:T(8,128)(2,1)S(1)} %copy-done, f32[128,2048]{1,0:T(8,128)S(1)} %get-tuple-element.80.inside_ref, f32[2,128,8]{2,1,0:T(8,128)S(1)} %get-tuple-element.81.down_ref, f32[128,2048]{1,0:T(8,128)S(1)} %copy-done.6, ...), custom_call_target="tpu_custom_call" | custom-call | flops 1 | bytes 1 | tf_op jit(solution)/shard_map/output0_0/pallas_call | solution.py:505
  65.7 1.0 %collective-permute-done.18.refs_0_ = bf16[2,512,128]{2,1,0:T(8,128)(2,1)S(1)} collective-permute-done((bf16[2,512,128]{2,1,0:T(8,128)(2,1)S(1)}, bf16[2,512,128]{2,1,0:T(8,128)(2,1)S(1)}, u32[]{:S(2)}, u32[]{:S(2)}) %collective-permute-start.18) | collective-permute-done | bytes 262176 | tf_op jit(solution)/shard_map/ppermute | solution.py:533
  67.1 2.0 %output0_1.1 = (bf16[1,128,8192]{2,1,0:T(8,128)(2,1)}, f32[8,128]{1,0:T(8,128)S(1)}) custom-call(s32[3]{0:T(128)S(1)} %pad_add_fusion.me_ref, bf16[1,128,8192]{2,1,0:T(8,128)(2,1)S(1)} %copy-done, f32[128,2048]{1,0:T(8,128)S(1)} %get-tuple-element.74.inside_ref, f32[2,128,8]{2,1,0:T(8,128)S(1)} %get-tuple-element.75.down_ref, ...), custom_call_target="tpu_custom_call", output_to_operand_aliasing={{0}: (8, {})} | custom-call | flops 1 | bytes 1 | tf_op jit(solution)/shard_map/output0_1/pallas_call | solution.py:505
  70.9 2.0 %output1_0.1 = (bf16[1,128,8192]{2,1,0:T(8,128)(2,1)}, f32[8,128]{1,0:T(8,128)S(1)}) custom-call(s32[3]{0:T(128)S(1)} %pad_add_fusion.me_ref, bf16[1,128,8192]{2,1,0:T(8,128)(2,1)S(1)} %copy-done, f32[128,2048]{1,0:T(8,128)S(1)} %get-tuple-element.92.inside_ref, f32[2,128,8]{2,1,0:T(8,128)S(1)} %get-tuple-element.93.down_ref, ...), custom_call_target="tpu_custom_call", output_to_operand_aliasing={{0}: (9, {})} | custom-call | flops 20000000000 | bytes 1 | tf_op jit(solution)/shard_map/output1_0/pallas_call | solution.py:505
  73.0 2.6 %output1_1.1 = (bf16[1,128,8192]{2,1,0:T(8,128)(2,1)}, f32[8,128]{1,0:T(8,128)}) custom-call(s32[3]{0:T(128)S(1)} %pad_add_fusion.me_ref, bf16[1,128,8192]{2,1,0:T(8,128)(2,1)S(1)} %copy-done, f32[128,2048]{1,0:T(8,128)S(1)} %get-tuple-element.65.inside_ref, f32[2,128,8]{2,1,0:T(8,128)S(1)} %get-tuple-element.66.down_ref, ...), custom_call_target="tpu_custom_call", output_to_operand_aliasing={{0}: (8, {})} | custom-call | flops 1 | bytes 1 | tf_op jit(solution)/shard_map/output1_1/pallas_call | solution.py:505
  (57 shorter events, 10.1 us)
Async XLA Ops:
  0.0 12.0 %collective-permute-start = (bf16[1,128,8192]{2,1,0:T(8,128)(2,1)}, bf16[1,128,8192]{2,1,0:T(8,128)(2,1)S(1)}, u32[]{:S(2)}, u32[]{:S(2)}) collective-permute-start(bf16[1,128,8192]{2,1,0:T(8,128)(2,1)} %keys_ref.7), channel_id=1, source_target_pairs={{0,1},{1,0},{2,3},{3,2},{4,5},{5,4},{6,7},{7,6},{8,9},{9,8},{10,11... | collective-permute-start | bytes 6291464 | tf_op jit(solution)/shard_map/ppermute | solution.py:338
  0.5 11.6 %collective-permute-start.1 = (bf16[1,128,8192]{2,1,0:T(8,128)(2,1)}, bf16[1,128,8192]{2,1,0:T(8,128)(2,1)}, u32[]{:S(2)}, u32[]{:S(2)}) collective-permute-start(bf16[1,128,8192]{2,1,0:T(8,128)(2,1)} %values_ref.7), channel_id=1, source_target_pairs={{0,1},{1,0},{2,3},{3,2},{4,5},{5,4},{6,7},{7,6},{8,9},{9,8},{10,11... | collective-permute-start | bytes 6291464 | tf_op jit(solution)/shard_map/ppermute | solution.py:337
  1.9 10.1 %all-to-all-start = ((f32[8,16,128]{2,1,0:T(8,128)}), f32[8,16,128]{2,1,0:T(8,128)S(1)}, u32[]{:S(2)}, u32[]{:S(2)}) async-start(f32[8,16,128]{2,1,0:T(8,128)} %pack.1), calls=%async_computation | async-start | bytes 131072 | tf_op jit(solution)/shard_map/all_to_all | solution.py:344
  14.2 15.4 %collective-permute-start.7 = (bf16[2,528,128]{2,1,0:T(8,128)(2,1)S(1)}, bf16[2,528,128]{2,1,0:T(8,128)(2,1)S(1)}, u32[]{:S(2)}, u32[]{:S(2)}) collective-permute-start(bf16[2,528,128]{2,1,0:T(8,128)(2,1)S(1)} %get-tuple-element.61), channel_id=1, source_target_pairs={{0,24},{8,16},{16,8},{24,0},{1,25},{9,17},{17,9},{25,1},{2,26},{10... | collective-permute-start | bytes 811016 | tf_op jit(solution)/shard_map/ppermute | solution.py:364
  14.9 5.1 %copy-start = (bf16[1,128,8192]{2,1,0:T(8,128)(2,1)S(1)}, bf16[1,128,8192]{2,1,0:T(8,128)(2,1)}, u32[]{:S(2)}) copy-start(bf16[1,128,8192]{2,1,0:T(8,128)(2,1)} %queries_ref.15) | copy-start | bytes 6291460
  14.9 5.1 %copy-start.1 = (bf16[1,128,8192]{2,1,0:T(8,128)(2,1)S(1)}, bf16[1,128,8192]{2,1,0:T(8,128)(2,1)}, u32[]{:S(2)}) copy-start(bf16[1,128,8192]{2,1,0:T(8,128)(2,1)} %keys_ref.7) | copy-start | bytes 6291460
  14.9 5.1 %copy-start.3 = (bf16[1,128,8192]{2,1,0:T(8,128)(2,1)S(1)}, bf16[1,128,8192]{2,1,0:T(8,128)(2,1)}, u32[]{:S(2)}) copy-start(bf16[1,128,8192]{2,1,0:T(8,128)(2,1)} %values_ref.7) | copy-start | bytes 6291460
  14.9 15.6 %collective-permute-start.6 = (bf16[2,528,128]{2,1,0:T(8,128)(2,1)S(1)}, bf16[2,528,128]{2,1,0:T(8,128)(2,1)S(1)}, u32[]{:S(2)}, u32[]{:S(2)}) collective-permute-start(bf16[2,528,128]{2,1,0:T(8,128)(2,1)S(1)} %get-tuple-element.52.refs_4_), channel_id=1, source_target_pairs={{0,16},{8,24},{16,0},{24,8},{1,17},{9,25},{17,1},{25,9},{2,18},{10... | collective-permute-start | bytes 811016 | tf_op jit(solution)/shard_map/ppermute | solution.py:364
  18.5 12.0 %collective-permute-start.5 = (bf16[2,528,128]{2,1,0:T(8,128)(2,1)S(1)}, bf16[2,528,128]{2,1,0:T(8,128)(2,1)S(1)}, u32[]{:S(2)}, u32[]{:S(2)}) collective-permute-start(bf16[2,528,128]{2,1,0:T(8,128)(2,1)S(1)} %get-tuple-element.60), channel_id=1, source_target_pairs={{0,8},{8,0},{16,24},{24,16},{1,9},{9,1},{17,25},{25,17},{2,10},{10... | collective-permute-start | bytes 811016 | tf_op jit(solution)/shard_map/ppermute | solution.py:364
  23.4 9.5 %copy-start.2 = (bf16[1,128,8192]{2,1,0:T(8,128)(2,1)S(1)}, bf16[1,128,8192]{2,1,0:T(8,128)(2,1)}, u32[]{:S(2)}) copy-start(bf16[1,128,8192]{2,1,0:T(8,128)(2,1)} %keys_ref.7) | copy-start | bytes 6291460
  23.4 9.5 %copy-start.4 = (bf16[1,128,8192]{2,1,0:T(8,128)(2,1)S(1)}, bf16[1,128,8192]{2,1,0:T(8,128)(2,1)}, u32[]{:S(2)}) copy-start(bf16[1,128,8192]{2,1,0:T(8,128)(2,1)} %values_ref.7) | copy-start | bytes 6291460
  26.9 15.9 %collective-permute-start.2 = (bf16[2,528,128]{2,1,0:T(8,128)(2,1)S(1)}, bf16[2,528,128]{2,1,0:T(8,128)(2,1)S(1)}, u32[]{:S(2)}, u32[]{:S(2)}) collective-permute-start(bf16[2,528,128]{2,1,0:T(8,128)(2,1)S(1)} %get-tuple-element.57), channel_id=1, source_target_pairs={{0,8},{8,0},{16,24},{24,16},{1,9},{9,1},{17,25},{25,17},{2,10},{10... | collective-permute-start | bytes 811016 | tf_op jit(solution)/shard_map/ppermute | solution.py:364
  27.5 15.3 %collective-permute-start.4 = (bf16[2,528,128]{2,1,0:T(8,128)(2,1)S(1)}, bf16[2,528,128]{2,1,0:T(8,128)(2,1)S(1)}, u32[]{:S(2)}, u32[]{:S(2)}) collective-permute-start(bf16[2,528,128]{2,1,0:T(8,128)(2,1)S(1)} %get-tuple-element.59), channel_id=1, source_target_pairs={{0,24},{8,16},{16,8},{24,0},{1,25},{9,17},{17,9},{25,1},{2,26},{10... | collective-permute-start | bytes 811016 | tf_op jit(solution)/shard_map/ppermute | solution.py:364
  29.7 13.2 %collective-permute-start.3 = (bf16[2,528,128]{2,1,0:T(8,128)(2,1)S(1)}, bf16[2,528,128]{2,1,0:T(8,128)(2,1)S(1)}, u32[]{:S(2)}, u32[]{:S(2)}) collective-permute-start(bf16[2,528,128]{2,1,0:T(8,128)(2,1)S(1)} %get-tuple-element.58.refs_4_), channel_id=1, source_target_pairs={{0,16},{8,24},{16,0},{24,8},{1,17},{9,25},{17,1},{25,9},{2,18},{10... | collective-permute-start | bytes 811016 | tf_op jit(solution)/shard_map/ppermute | solution.py:364
  31.4 5.1 %collective-permute-start.8 = (bf16[528,128]{1,0:T(8,128)(2,1)S(1)}, bf16[528,128]{1,0:T(8,128)(2,1)S(1)}, u32[]{:S(2)}, u32[]{:S(2)}) collective-permute-start(bf16[528,128]{1,0:T(8,128)(2,1)S(1)} %total0.1.rest_0_.mine_ref), channel_id=1, source_target_pairs={{0,2},{2,0},{4,6},{6,4},{1,3},{3,1},{5,7},{7,5},{8,10},{10,8},{12,... | collective-permute-start | bytes 405512 | tf_op jit(solution)/shard_map/ppermute | solution.py:435
  34.7 10.7 %copy-start.8 = (bf16[2048]{0:T(1024)(128)(2,1)S(1)}, bf16[2048]{0:T(1024)(128)(2,1)}, u32[]{:S(2)}) copy-start(bf16[2048]{0:T(1024)(128)(2,1)} %param.11) | copy-start | bytes 12292
  37.1 8.3 %collective-permute-start.10 = (bf16[528,128]{1,0:T(8,128)(2,1)S(1)}, bf16[528,128]{1,0:T(8,128)(2,1)S(1)}, u32[]{:S(2)}, u32[]{:S(2)}) collective-permute-start(bf16[528,128]{1,0:T(8,128)(2,1)S(1)} %widen0_0.1.refs_0_), channel_id=1, source_target_pairs={{0,4},{2,6},{4,0},{6,2},{1,5},{3,7},{5,1},{7,3},{8,12},{10,14},{12... | collective-permute-start | bytes 405512 | tf_op jit(solution)/shard_map/ppermute | solution.py:435
  43.7 6.2 %collective-permute-start.9 = (bf16[528,128]{1,0:T(8,128)(2,1)S(1)}, bf16[528,128]{1,0:T(8,128)(2,1)S(1)}, u32[]{:S(2)}, u32[]{:S(2)}) collective-permute-start(bf16[528,128]{1,0:T(8,128)(2,1)S(1)} %total1.1.refs_6_.mine_ref), channel_id=1, source_target_pairs={{0,2},{2,0},{4,6},{6,4},{1,3},{3,1},{5,7},{7,5},{8,10},{10,8},{12,... | collective-permute-start | bytes 405512 | tf_op jit(solution)/shard_map/ppermute | solution.py:435
  46.4 14.3 %collective-permute-start.15 = (bf16[1040,128]{1,0:T(8,128)(2,1)S(1)}, bf16[1040,128]{1,0:T(8,128)(2,1)S(1)}, u32[]{:S(2)}, u32[]{:S(2)}) collective-permute-start(bf16[1040,128]{1,0:T(8,128)(2,1)S(1)} %get-tuple-element.77), channel_id=1, source_target_pairs={{0,8},{8,0},{16,24},{24,16},{1,9},{9,1},{17,25},{25,17},{2,10},{10... | collective-permute-start | bytes 798728 | tf_op jit(solution)/shard_map/ppermute | solution.py:364
  47.0 15.4 %collective-permute-start.16 = (bf16[1040,128]{1,0:T(8,128)(2,1)S(1)}, bf16[1040,128]{1,0:T(8,128)(2,1)S(1)}, u32[]{:S(2)}, u32[]{:S(2)}) collective-permute-start(bf16[1040,128]{1,0:T(8,128)(2,1)S(1)} %get-tuple-element.78), channel_id=1, source_target_pairs={{0,16},{8,24},{16,0},{24,8},{1,17},{9,25},{17,1},{25,9},{2,18},{10... | collective-permute-start | bytes 798728 | tf_op jit(solution)/shard_map/ppermute | solution.py:364
  48.2 14.2 %collective-permute-start.17 = (bf16[1040,128]{1,0:T(8,128)(2,1)S(1)}, bf16[1040,128]{1,0:T(8,128)(2,1)S(1)}, u32[]{:S(2)}, u32[]{:S(2)}) collective-permute-start(bf16[1040,128]{1,0:T(8,128)(2,1)S(1)} %get-tuple-element.79), channel_id=1, source_target_pairs={{0,24},{8,16},{16,8},{24,0},{1,25},{9,17},{17,9},{25,1},{2,26},{10... | collective-permute-start | bytes 798728 | tf_op jit(solution)/shard_map/ppermute | solution.py:364
  50.6 7.3 %collective-permute-start.11 = (bf16[528,128]{1,0:T(8,128)(2,1)S(1)}, bf16[528,128]{1,0:T(8,128)(2,1)S(1)}, u32[]{:S(2)}, u32[]{:S(2)}) collective-permute-start(bf16[528,128]{1,0:T(8,128)(2,1)S(1)} %widen1_0.1.rest_0_), channel_id=1, source_target_pairs={{0,4},{2,6},{4,0},{6,2},{1,5},{3,7},{5,1},{7,3},{8,12},{10,14},{12... | collective-permute-start | bytes 405512 | tf_op jit(solution)/shard_map/ppermute | solution.py:435
  54.2 8.2 %copy-start.6 = (f32[128,2048]{1,0:T(8,128)S(1)}, f32[128,2048]{1,0:T(8,128)}, u32[]{:S(2)}) copy-start(f32[128,2048]{1,0:T(8,128)} %get-tuple-element.82.gate_ref) | copy-start | bytes 3145732
  58.9 10.2 %collective-permute-start.12 = (bf16[1040,128]{1,0:T(8,128)(2,1)S(1)}, bf16[1040,128]{1,0:T(8,128)(2,1)S(1)}, u32[]{:S(2)}, u32[]{:S(2)}) collective-permute-start(bf16[1040,128]{1,0:T(8,128)(2,1)S(1)} %get-tuple-element.71), channel_id=1, source_target_pairs={{0,8},{8,0},{16,24},{24,16},{1,9},{9,1},{17,25},{25,17},{2,10},{10... | collective-permute-start | bytes 798728 | tf_op jit(solution)/shard_map/ppermute | solution.py:364
  59.5 10.2 %collective-permute-start.13 = (bf16[1040,128]{1,0:T(8,128)(2,1)S(1)}, bf16[1040,128]{1,0:T(8,128)(2,1)S(1)}, u32[]{:S(2)}, u32[]{:S(2)}) collective-permute-start(bf16[1040,128]{1,0:T(8,128)(2,1)S(1)} %get-tuple-element.72), channel_id=1, source_target_pairs={{0,16},{8,24},{16,0},{24,8},{1,17},{9,25},{17,1},{25,9},{2,18},{10... | collective-permute-start | bytes 798728 | tf_op jit(solution)/shard_map/ppermute | solution.py:364
  60.7 9.0 %collective-permute-start.14 = (bf16[1040,128]{1,0:T(8,128)(2,1)S(1)}, bf16[1040,128]{1,0:T(8,128)(2,1)S(1)}, u32[]{:S(2)}, u32[]{:S(2)}) collective-permute-start(bf16[1040,128]{1,0:T(8,128)(2,1)S(1)} %get-tuple-element.73), channel_id=1, source_target_pairs={{0,24},{8,16},{16,8},{24,0},{1,25},{9,17},{17,9},{25,1},{2,26},{10... | collective-permute-start | bytes 798728 | tf_op jit(solution)/shard_map/ppermute | solution.py:364
  62.4 4.6 %copy-start.7 = (f32[128,2048]{1,0:T(8,128)S(1)}, f32[128,2048]{1,0:T(8,128)}, u32[]{:S(2)}) copy-start(f32[128,2048]{1,0:T(8,128)} %get-tuple-element.76.gate_ref) | copy-start | bytes 3145732
  65.1 1.6 %collective-permute-start.18 = (bf16[2,512,128]{2,1,0:T(8,128)(2,1)S(1)}, bf16[2,512,128]{2,1,0:T(8,128)(2,1)S(1)}, u32[]{:S(2)}, u32[]{:S(2)}) collective-permute-start(bf16[2,512,128]{2,1,0:T(8,128)(2,1)S(1)} %get-tuple-element.84), channel_id=1, source_target_pairs={{0,1},{1,0},{2,3},{3,2},{4,5},{5,4},{6,7},{7,6},{8,9},{9,8},{10,11... | collective-permute-start | bytes 786440 | tf_op jit(solution)/shard_map/ppermute | solution.py:533
  65.2 1.9 %collective-permute-start.19 = (bf16[2,512,128]{2,1,0:T(8,128)(2,1)S(1)}, bf16[2,512,128]{2,1,0:T(8,128)(2,1)S(1)}, u32[]{:S(2)}, u32[]{:S(2)}) collective-permute-start(bf16[2,512,128]{2,1,0:T(8,128)(2,1)S(1)} %get-tuple-element.85), channel_id=1, source_target_pairs={{0,1},{1,0},{2,3},{3,2},{4,5},{5,4},{6,7},{7,6},{8,9},{9,8},{10,11... | collective-permute-start | bytes 786440 | tf_op jit(solution)/shard_map/ppermute | solution.py:533
  67.1 3.8 %copy-start.9 = (f32[128,2048]{1,0:T(8,128)S(1)}, f32[128,2048]{1,0:T(8,128)}, u32[]{:S(2)}) copy-start(f32[128,2048]{1,0:T(8,128)} %get-tuple-element.94.gate_ref) | copy-start | bytes 3145732
  70.4 2.6 %collective-permute-start.20 = (bf16[2,512,128]{2,1,0:T(8,128)(2,1)S(1)}, bf16[2,512,128]{2,1,0:T(8,128)(2,1)S(1)}, u32[]{:S(2)}, u32[]{:S(2)}) collective-permute-start(bf16[2,512,128]{2,1,0:T(8,128)(2,1)S(1)} %get-tuple-element.89), channel_id=1, source_target_pairs={{0,1},{1,0},{2,3},{3,2},{4,5},{5,4},{6,7},{7,6},{8,9},{9,8},{10,11... | collective-permute-start | bytes 786440 | tf_op jit(solution)/shard_map/ppermute | solution.py:533
  70.4 2.5 %collective-permute-start.21 = (bf16[2,512,128]{2,1,0:T(8,128)(2,1)S(1)}, bf16[2,512,128]{2,1,0:T(8,128)(2,1)S(1)}, u32[]{:S(2)}, u32[]{:S(2)}) collective-permute-start(bf16[2,512,128]{2,1,0:T(8,128)(2,1)S(1)} %get-tuple-element.90), channel_id=1, source_target_pairs={{0,1},{1,0},{2,3},{3,2},{4,5},{5,4},{6,7},{7,6},{8,9},{9,8},{10,11... | collective-permute-start | bytes 786440 | tf_op jit(solution)/shard_map/ppermute | solution.py:533
  (1 other events, 2.1 us)
where the time goes:
time: 76.1 us; the launch traced here: 75.7 us
  Pallas kernels  37 us (49%)
  starting transfers between devices  29 us (38%)
  waiting for transfers between devices  9.23 us (12%)
    ppermute x12, starting transfers between devices, exchange(): arrived[slot] = lax.ppermute(slots[slot], 'head', pairs)  14.3 us
    pallas_call x4, Pallas kernels, output(): kernel_call(functools.partial(output_kernel, dim, owned, half, group * sh...  8.63 us
    ppermute x4, starting transfers between devices, with_plane(): return lax.ppermute(total, 'z', pairs)  7.87 us
    pallas_call x3, Pallas kernels, on_device(): kernel_call(functools.partial(state_kernel, dim, owned, half, group * sha...  7.85 us
    pallas_call x4, Pallas kernels, inside_part(): kernel_call(functools.partial(inside_kernel, dim, half, group * share, sh...  6.72 us
    pallas_call x2, Pallas kernels, gates_of(): kernel_call(functools.partial(gate_kernel, half, group * share, share, di...  6.23 us
    all_to_all x1, starting transfers between devices, on_device(): decay = lax.all_to_all(packed, ('core', 'head'), 0, 0, tiled=True)  5.17 us
    all_to_all x1, waiting for transfers between devices, on_device(): decay = lax.all_to_all(packed, ('core', 'head'), 0, 0, tiled=True)  4.85 us
  transfers between devices with their start and end apart: 23, of which 6 were waited for; matrix products, arithmetic and copies ran while one was open for 0% of the time, Pallas kernels for 42%

commit v1 on v0

--- a/solution.py
+++ b/solution.py
@@ -268,28 +268,31 @@
         collect(me_ref[0], core, refs[:parts], prefix_ref, gain_ref)
         prefixes, gains = [prefix_ref.at[at] for at in range(parts)], gain_ref
     average = jnp.full((dim, dim), 1.0 / dim, jnp.bfloat16)
+    batch = STEP // 2
+    width = batch * dim
     moves = []
-    for turn in range(count // STEP):
-        first = (1 - core if parts is None else core) * half + begin + turn * STEP
-        gain = gains[pl.ds(pl.multiple_of(first, STEP), STEP), :]
-        down = down_ref[turn]
-        columns = [heads_at(first, head, dim) for head in range(STEP)]
+    for turn in range(count // batch):
+        first = (1 - core if parts is None else core) * half + begin + turn * batch
+        block, offset = divmod(turn * batch, STEP)
+        gain = gains[pl.ds(pl.multiple_of(first - offset, STEP), STEP), :]
+        down = down_ref[block]
+        places = [turn * batch + head for head in range(batch)]
         carried = []
-        for head, c in enumerate(columns):
-            owner, spot = divmod(turn * STEP + head, owned)
-            prefix = prefixes[owner][spot * dim : (spot + 1) * dim, :]
-            carried.append(dot(queries_ref[0, :, c], prefix, NN))
+        for place in places:
+            owner, spot = divmod(place, owned)
+            query = queries_ref[0, :, heads_at(first - turn * batch, place, dim)]
+            carried.append(dot(query, prefixes[owner][spot * dim : (spot + 1) * dim, :], NN))
         mixed, means = [], []
-        for head in range(STEP):
-            at = (turn * STEP + head) * dim
-            mixed.append(inside_ref[:, at : at + dim] + carried[head] * down[:, head : head + 1])
+        for head, place in enumerate(places):
+            c = slice(place * dim, (place + 1) * dim)
+            at = offset + head
+            mixed.append(inside_ref[:, c] + carried[head] * down[:, at : at + 1])
             means.append(dot((mixed[head] * mixed[head]).astype(jnp.bfloat16), average, NN))
-        for head in range(STEP):
-            at = (turn * STEP + head) * dim
-            factor = gain[head : head + 1, :] * gate_ref[:, at : at + dim]
+        for head, place in enumerate(places):
+            c = slice(place * dim, (place + 1) * dim)
+            factor = gain[offset + head : offset + head + 1, :] * gate_ref[:, c]
             normed = mixed[head] * lax.rsqrt(means[head] + 1e-06) * factor
             result_ref[turn, :, head * dim : (head + 1) * dim] = normed.astype(jnp.bfloat16)
-        width = STEP * dim
         moves.append(
             pltpu.make_async_copy(
                 result_ref.at[turn],
@@ -513,8 +516,8 @@
             [
                 pltpu.VMEM(part_type.shape, part_type.dtype),
                 pltpu.VMEM(gain_type.shape, gain_type.dtype),
-                pltpu.VMEM((share // STEP, length, STEP * dim), jnp.bfloat16),
-                pltpu.SemaphoreType.DMA((share // STEP,)),
+                pltpu.VMEM((2 * share // STEP, length, STEP // 2 * dim), jnp.bfloat16),
+                pltpu.SemaphoreType.DMA((2 * share // STEP,)),
             ],
             aliases={5 + len(received): 0} if out else {},
             cost=cost,
@@ -527,13 +530,10 @@
     out = ()
     for group in range(GROUPS):
         last = group == GROUPS - 1
-        if not last:
-            out, before = output(group, 0, prefixes[group], out, before)
         *others, gains = merge(group, before, 0)
         others = [lax.ppermute(other, "core", swap) for other in others]
         before = (gains,)
-        if last:
-            out, before = output(group, 0, prefixes[group], out, before, cost=20)
+        out, before = output(group, 0, prefixes[group], out, before, cost=20 if last else 0)
         out, before = output(group, 1, (*others, gains), out, before)
     return out[0]
 

time: 76.1 us -> 76.4 us (level)
    ppermute x4, waiting for transfers between devices: 1.4 us -> 0.01 us  [on_device(): others = [lax.ppermute(other, 'core', swap) for other in others]]
    ppermute x12, waiting for transfers between devices: 0.65 us -> 1.67 us  [exchange(): arrived[slot] = lax.ppermute(slots[slot], 'head', pairs)]
  transfers between devices with their start and end apart: 23 -> 23, of which waited for: 6 -> 4; matrix products, arithmetic and copies ran while one was open for 0% -> 0% of each run, Pallas kernels for 42% -> 42%
where the time goes in v1:
time: 76.4 us; the launch traced here: 76.1 us
  Pallas kernels  37.7 us (49%)
  starting transfers between devices  29 us (38%)
  waiting for transfers between devices  8.86 us (12%)
    ppermute x12, starting transfers between devices, exchange(): arrived[slot] = lax.ppermute(slots[slot], 'head', pairs)  14.3 us
    pallas_call x4, Pallas kernels, output(): kernel_call(functools.partial(output_kernel, dim, owned, half, group * sh...  9.32 us
    ppermute x4, starting transfers between devices, with_plane(): return lax.ppermute(total, 'z', pairs)  7.87 us
    pallas_call x3, Pallas kernels, on_device(): kernel_call(functools.partial(state_kernel, dim, owned, half, group * sha...  7.85 us
    pallas_call x4, Pallas kernels, inside_part(): kernel_call(functools.partial(inside_kernel, dim, half, group * share, sh...  6.72 us
    pallas_call x2, Pallas kernels, gates_of(): kernel_call(functools.partial(gate_kernel, half, group * share, share, di...  6.23 us
    all_to_all x1, starting transfers between devices, on_device(): decay = lax.all_to_all(packed, ('core', 'head'), 0, 0, tiled=True)  5.17 us
    all_to_all x1, waiting for transfers between devices, on_device(): decay = lax.all_to_all(packed, ('core', 'head'), 0, 0, tiled=True)  4.85 us
  transfers between devices with their start and end apart: 23, of which 4 were waited for; matrix products, arithmetic and copies ran while one was open for 0% of the time, Pallas kernels for 42%

profile of v1, /device:TPU:0, one launch (start us, length us, event | category | flops | bytes accessed | tf_op | source)
XLA Modules:
  0.0 76.1 jit_solution(4306943446223297789)
XLA Ops:
  0.5 1.4 %pack.1 = f32[8,16,128]{2,1,0:T(8,128)} custom-call(f32[1,16,512]{2,1,0:T(8,128)} %decay_ref.1), custom_call_target="tpu_custom_call" | custom-call | tf_op jit(solution)/shard_map/pack/pallas_call | solution.py:342
  1.9 5.2 %all-to-all-start = ((f32[8,16,128]{2,1,0:T(8,128)}), f32[8,16,128]{2,1,0:T(8,128)S(1)}, u32[]{:S(2)}, u32[]{:S(2)}) async-start(f32[8,16,128]{2,1,0:T(8,128)} %pack.1), calls=%async_computation | async-start | bytes 131072 | tf_op jit(solution)/shard_map/all_to_all | solution.py:347
  7.1 4.9 %all-to-all-done.decay_ref = f32[8,16,128]{2,1,0:T(8,128)S(1)} async-done(((f32[8,16,128]{2,1,0:T(8,128)}), f32[8,16,128]{2,1,0:T(8,128)S(1)}, u32[]{:S(2)}, u32[]{:S(2)}) %all-to-all-start) | async-done | bytes 65568 | tf_op jit(solution)/shard_map/all_to_all | solution.py:347
  12.0 2.2 %state0_1.1 = (bf16[2,528,128]{2,1,0:T(8,128)(2,1)S(1)}, bf16[2,528,128]{2,1,0:T(8,128)(2,1)S(1)}) custom-call(s32[3]{0:T(128)S(1)} %pad_add_fusion.me_ref, f32[8,16,128]{2,1,0:T(8,128)S(1)} %all-to-all-done.decay_ref, bf16[1,128,8192]{2,1,0:T(8,128)(2,1)} %keys_ref.7, bf16[1,128,8192]{2,1,0:T(8,128)(2,1)} %values_ref.7, ...), custom_call_target="tpu_custom_call" | custom-call | flops 1 | bytes 1 | tf_op jit(solution)/shard_map/state0_1/pallas_call | solution.py:413
  14.9 1.4 %collective-permute-start.6 = (bf16[2,528,128]{2,1,0:T(8,128)(2,1)S(1)}, bf16[2,528,128]{2,1,0:T(8,128)(2,1)S(1)}, u32[]{:S(2)}, u32[]{:S(2)}) collective-permute-start(bf16[2,528,128]{2,1,0:T(8,128)(2,1)S(1)} %get-tuple-element.52.refs_4_), channel_id=1, source_target_pairs={{0,16},{8,24},{16,0},{24,8},{1,17},{9,25},{17,1},{25,9},{2,18},{10... | collective-permute-start | bytes 811016 | tf_op jit(solution)/shard_map/ppermute | solution.py:367
  16.3 2.2 %state0_0.1 = (bf16[2,528,128]{2,1,0:T(8,128)(2,1)S(1)}, bf16[2,528,128]{2,1,0:T(8,128)(2,1)S(1)}) custom-call(s32[3]{0:T(128)S(1)} %pad_add_fusion.me_ref, f32[8,16,128]{2,1,0:T(8,128)S(1)} %all-to-all-done.decay_ref, bf16[1,128,8192]{2,1,0:T(8,128)(2,1)} %keys_ref.7, bf16[1,128,8192]{2,1,0:T(8,128)(2,1)} %values_ref.7, ...), custom_call_target="tpu_custom_call" | custom-call | flops 1 | bytes 1 | tf_op jit(solution)/shard_map/state0_0/pallas_call | solution.py:413
  18.5 1.5 %collective-permute-start.5 = (bf16[2,528,128]{2,1,0:T(8,128)(2,1)S(1)}, bf16[2,528,128]{2,1,0:T(8,128)(2,1)S(1)}, u32[]{:S(2)}, u32[]{:S(2)}) collective-permute-start(bf16[2,528,128]{2,1,0:T(8,128)(2,1)S(1)} %get-tuple-element.60), channel_id=1, source_target_pairs={{0,8},{8,0},{16,24},{24,16},{1,9},{9,1},{17,25},{25,17},{2,10},{10... | collective-permute-start | bytes 811016 | tf_op jit(solution)/shard_map/ppermute | solution.py:367
  20.1 1.7 %inside0_0.1 = (f32[128,2048]{1,0:T(8,128)S(1)}, f32[2,128,8]{2,1,0:T(8,128)S(1)}, f32[8,128]{1,0:T(8,128)S(1)}) custom-call(s32[3]{0:T(128)S(1)} %pad_add_fusion.me_ref, bf16[1,128,8192]{2,1,0:T(8,128)(2,1)S(1)} %copy-done, bf16[1,128,8192]{2,1,0:T(8,128)(2,1)S(1)} %copy-done.1, bf16[1,128,8192]{2,1,0:T(8,128)(2,1)S(1)} %copy-done.3, ...), custom_call_target="tpu_custom_call" | custom-call | flops 1 | bytes 1 | tf_op jit(solution)/shard_map/inside0_0/pallas_call | solution.py:378
  21.7 1.7 %inside0_1.1 = (f32[128,2048]{1,0:T(8,128)S(1)}, f32[2,128,8]{2,1,0:T(8,128)S(1)}, f32[8,128]{1,0:T(8,128)S(1)}) custom-call(s32[3]{0:T(128)S(1)} %pad_add_fusion.me_ref, bf16[1,128,8192]{2,1,0:T(8,128)(2,1)S(1)} %copy-done, bf16[1,128,8192]{2,1,0:T(8,128)(2,1)S(1)} %copy-done.1, bf16[1,128,8192]{2,1,0:T(8,128)(2,1)S(1)} %copy-done.3, ...), custom_call_target="tpu_custom_call" | custom-call | flops 1 | bytes 1 | tf_op jit(solution)/shard_map/inside0_1/pallas_call | solution.py:378
  23.5 3.5 %state1_1.1 = (bf16[2,528,128]{2,1,0:T(8,128)(2,1)S(1)}, bf16[2,528,128]{2,1,0:T(8,128)(2,1)S(1)}, bf16[2,528,128]{2,1,0:T(8,128)(2,1)S(1)}, bf16[2,528,128]{2,1,0:T(8,128)(2,1)S(1)}) custom-call(s32[3]{0:T(128)S(1)} %pad_add_fusion.me_ref, f32[8,16,128]{2,1,0:T(8,128)S(1)} %all-to-all-done.decay_ref, bf16[1,128,8192]{2,1,0:T(8,128)(2,1)} %keys_ref.7, ...), custom_call_target="tpu_custom_call" | custom-call | flops 1 | bytes 1 | tf_op jit(solution)/shard_map/state1_1/pallas_call | solution.py:413
  27.5 2.1 %collective-permute-start.4 = (bf16[2,528,128]{2,1,0:T(8,128)(2,1)S(1)}, bf16[2,528,128]{2,1,0:T(8,128)(2,1)S(1)}, u32[]{:S(2)}, u32[]{:S(2)}) collective-permute-start(bf16[2,528,128]{2,1,0:T(8,128)(2,1)S(1)} %get-tuple-element.59), channel_id=1, source_target_pairs={{0,24},{8,16},{16,8},{24,0},{1,25},{9,17},{17,9},{25,1},{2,26},{10... | collective-permute-start | bytes 811016 | tf_op jit(solution)/shard_map/ppermute | solution.py:367
  31.4 1.6 %collective-permute-start.8 = (bf16[528,128]{1,0:T(8,128)(2,1)S(1)}, bf16[528,128]{1,0:T(8,128)(2,1)S(1)}, u32[]{:S(2)}, u32[]{:S(2)}) collective-permute-start(bf16[528,128]{1,0:T(8,128)(2,1)S(1)} %total0.1.rest_0_.mine_ref), channel_id=1, source_target_pairs={{0,2},{2,0},{4,6},{6,4},{1,3},{3,1},{5,7},{7,5},{8,10},{10,8},{12,... | collective-permute-start | bytes 405512 | tf_op jit(solution)/shard_map/ppermute | solution.py:438
  33.0 1.7 %inside1_0.1 = (f32[128,2048]{1,0:T(8,128)S(1)}, f32[2,128,8]{2,1,0:T(8,128)S(1)}, f32[8,128]{1,0:T(8,128)S(1)}) custom-call(s32[3]{0:T(128)S(1)} %pad_add_fusion.me_ref, bf16[1,128,8192]{2,1,0:T(8,128)(2,1)S(1)} %copy-done, bf16[1,128,8192]{2,1,0:T(8,128)(2,1)S(1)} %copy-done.2, bf16[1,128,8192]{2,1,0:T(8,128)(2,1)S(1)} %copy-done.4, ...), custom_call_target="tpu_custom_call" | custom-call | flops 1 | bytes 1 | tf_op jit(solution)/shard_map/inside1_0/pallas_call | solution.py:378
  34.7 1.7 %collective-permute-done.8.other_ref.refs_4_ = bf16[528,128]{1,0:T(8,128)(2,1)S(1)} collective-permute-done((bf16[528,128]{1,0:T(8,128)(2,1)S(1)}, bf16[528,128]{1,0:T(8,128)(2,1)S(1)}, u32[]{:S(2)}, u32[]{:S(2)}) %collective-permute-start.8) | collective-permute-done | bytes 135200 | tf_op jit(solution)/shard_map/ppermute | solution.py:438
  37.1 2.6 %collective-permute-start.10 = (bf16[528,128]{1,0:T(8,128)(2,1)S(1)}, bf16[528,128]{1,0:T(8,128)(2,1)S(1)}, u32[]{:S(2)}, u32[]{:S(2)}) collective-permute-start(bf16[528,128]{1,0:T(8,128)(2,1)S(1)} %widen0_0.1.refs_0_), channel_id=1, source_target_pairs={{0,4},{2,6},{4,0},{6,2},{1,5},{3,7},{5,1},{7,3},{8,12},{10,14},{12... | collective-permute-start | bytes 405512 | tf_op jit(solution)/shard_map/ppermute | solution.py:438
  39.7 3.1 %gates0.1 = (f32[128,2048]{1,0:T(8,128)}, f32[128,2048]{1,0:T(8,128)}, f32[8,128]{1,0:T(8,128)S(1)}) custom-call(s32[3]{0:T(128)S(1)} %pad_add_fusion.me_ref, bf16[1,128,8192]{2,1,0:T(8,128)(2,1)} %gate_ref.3, bf16[528,128]{1,0:T(8,128)(2,1)S(1)} %widen0_0.1.refs_0_), custom_call_target="tpu_custom_call" | custom-call | flops 1 | bytes 1 | tf_op jit(solution)/shard_map/gates0/pallas_call | solution.py:396
  42.9 0.9 %total1.1.refs_6_.mine_ref = bf16[528,128]{1,0:T(8,128)(2,1)S(1)} custom-call(s32[3]{0:T(128)S(1)} %pad_add_fusion.me_ref, bf16[2,528,128]{2,1,0:T(8,128)(2,1)S(1)} %get-tuple-element.56.refs_0_, bf16[2,528,128]{2,1,0:T(8,128)(2,1)S(1)} %collective-permute-done.2.refs_1_, bf16[2,528,128]{2,1,0:T(8,128)(2,1)S(1)} %collective-permute-done.3.refs_2_, ...), custom_call_target="tpu_custom_call" | custom-call | flops 1 | bytes 1 | tf_op jit(solution)/shard_map/total1/pallas_call | solution.py:464
  43.7 1.6 %collective-permute-start.9 = (bf16[528,128]{1,0:T(8,128)(2,1)S(1)}, bf16[528,128]{1,0:T(8,128)(2,1)S(1)}, u32[]{:S(2)}, u32[]{:S(2)}) collective-permute-start(bf16[528,128]{1,0:T(8,128)(2,1)S(1)} %total1.1.refs_6_.mine_ref), channel_id=1, source_target_pairs={{0,2},{2,0},{4,6},{6,4},{1,3},{3,1},{5,7},{7,5},{8,10},{10,8},{12,... | collective-permute-start | bytes 405512 | tf_op jit(solution)/shard_map/ppermute | solution.py:438
  45.4 1.0 %prefix0.1 = (bf16[1040,128]{1,0:T(8,128)(2,1)S(1)}, bf16[1040,128]{1,0:T(8,128)(2,1)S(1)}, bf16[1040,128]{1,0:T(8,128)(2,1)S(1)}, bf16[1040,128]{1,0:T(8,128)(2,1)S(1)}) custom-call(s32[3]{0:T(128)S(1)} %pad_add_fusion.me_ref, bf16[16,128]{1,0:T(8,128)(2,1)S(1)} %bitcast.4, bf16[2,528,128]{2,1,0:T(8,128)(2,1)S(1)} %get-tuple-element.53.rest_0_.refs_0_, ...), custom_call_target="tpu_custom_call" | custom-call | flops 1 | bytes 1 | tf_op jit(solution)/shard_map/prefix0/pallas_call | solution.py:451
  47.0 1.2 %collective-permute-start.16 = (bf16[1040,128]{1,0:T(8,128)(2,1)S(1)}, bf16[1040,128]{1,0:T(8,128)(2,1)S(1)}, u32[]{:S(2)}, u32[]{:S(2)}) collective-permute-start(bf16[1040,128]{1,0:T(8,128)(2,1)S(1)} %get-tuple-element.78), channel_id=1, source_target_pairs={{0,16},{8,24},{16,0},{24,8},{1,17},{9,25},{17,1},{25,9},{2,18},{10... | collective-permute-start | bytes 798728 | tf_op jit(solution)/shard_map/ppermute | solution.py:367
  48.2 1.7 %collective-permute-start.17 = (bf16[1040,128]{1,0:T(8,128)(2,1)S(1)}, bf16[1040,128]{1,0:T(8,128)(2,1)S(1)}, u32[]{:S(2)}, u32[]{:S(2)}) collective-permute-start(bf16[1040,128]{1,0:T(8,128)(2,1)S(1)} %get-tuple-element.79), channel_id=1, source_target_pairs={{0,24},{8,16},{16,8},{24,0},{1,25},{9,17},{17,9},{25,1},{2,26},{10... | collective-permute-start | bytes 798728 | tf_op jit(solution)/shard_map/ppermute | solution.py:367
  50.6 1.9 %collective-permute-start.11 = (bf16[528,128]{1,0:T(8,128)(2,1)S(1)}, bf16[528,128]{1,0:T(8,128)(2,1)S(1)}, u32[]{:S(2)}, u32[]{:S(2)}) collective-permute-start(bf16[528,128]{1,0:T(8,128)(2,1)S(1)} %widen1_0.1.rest_0_), channel_id=1, source_target_pairs={{0,4},{2,6},{4,0},{6,2},{1,5},{3,7},{5,1},{7,3},{8,12},{10,14},{12... | collective-permute-start | bytes 405512 | tf_op jit(solution)/shard_map/ppermute | solution.py:438
  52.5 1.7 %inside1_1.1 = (f32[128,2048]{1,0:T(8,128)S(1)}, f32[2,128,8]{2,1,0:T(8,128)S(1)}, f32[8,128]{1,0:T(8,128)S(1)}) custom-call(s32[3]{0:T(128)S(1)} %pad_add_fusion.me_ref, bf16[1,128,8192]{2,1,0:T(8,128)(2,1)S(1)} %copy-done, bf16[1,128,8192]{2,1,0:T(8,128)(2,1)S(1)} %copy-done.2, bf16[1,128,8192]{2,1,0:T(8,128)(2,1)S(1)} %copy-done.4, ...), custom_call_target="tpu_custom_call" | custom-call | flops 2000000000 | bytes 1 | tf_op jit(solution)/shard_map/inside1_1/pallas_call | solution.py:378
  54.2 3.1 %gates1.1 = (f32[128,2048]{1,0:T(8,128)}, f32[128,2048]{1,0:T(8,128)}, f32[8,128]{1,0:T(8,128)S(1)}) custom-call(s32[3]{0:T(128)S(1)} %pad_add_fusion.me_ref, bf16[1,128,8192]{2,1,0:T(8,128)(2,1)} %gate_ref.3, f32[8,128]{1,0:T(8,128)S(1)} %get-tuple-element.67.refs_0_), custom_call_target="tpu_custom_call" | custom-call | flops 1 | bytes 1 | tf_op jit(solution)/shard_map/gates1/pallas_call | solution.py:396
  57.9 1.0 %prefix1.1 = (bf16[1040,128]{1,0:T(8,128)(2,1)S(1)}, bf16[1040,128]{1,0:T(8,128)(2,1)S(1)}, bf16[1040,128]{1,0:T(8,128)(2,1)S(1)}, bf16[1040,128]{1,0:T(8,128)(2,1)S(1)}) custom-call(s32[3]{0:T(128)S(1)} %pad_add_fusion.me_ref, bf16[16,128]{1,0:T(8,128)(2,1)S(1)} %bitcast.5, bf16[2,528,128]{2,1,0:T(8,128)(2,1)S(1)} %get-tuple-element.56.refs_0_, ...), custom_call_target="tpu_custom_call" | custom-call | flops 1 | bytes 1 | tf_op jit(solution)/shard_map/prefix1/pallas_call | solution.py:451
  59.5 1.2 %collective-permute-start.13 = (bf16[1040,128]{1,0:T(8,128)(2,1)S(1)}, bf16[1040,128]{1,0:T(8,128)(2,1)S(1)}, u32[]{:S(2)}, u32[]{:S(2)}) collective-permute-start(bf16[1040,128]{1,0:T(8,128)(2,1)S(1)} %get-tuple-element.72), channel_id=1, source_target_pairs={{0,16},{8,24},{16,0},{24,8},{1,17},{9,25},{17,1},{25,9},{2,18},{10... | collective-permute-start | bytes 798728 | tf_op jit(solution)/shard_map/ppermute | solution.py:367
  60.7 1.7 %collective-permute-start.14 = (bf16[1040,128]{1,0:T(8,128)(2,1)S(1)}, bf16[1040,128]{1,0:T(8,128)(2,1)S(1)}, u32[]{:S(2)}, u32[]{:S(2)}) collective-permute-start(bf16[1040,128]{1,0:T(8,128)(2,1)S(1)} %get-tuple-element.73), channel_id=1, source_target_pairs={{0,24},{8,16},{16,8},{24,0},{1,25},{9,17},{17,9},{25,1},{2,26},{10... | collective-permute-start | bytes 798728 | tf_op jit(solution)/shard_map/ppermute | solution.py:367
  63.6 2.2 %output0_0.1 = (bf16[1,128,8192]{2,1,0:T(8,128)(2,1)}, f32[8,128]{1,0:T(8,128)S(1)}) custom-call(s32[3]{0:T(128)S(1)} %pad_add_fusion.me_ref, bf16[1,128,8192]{2,1,0:T(8,128)(2,1)S(1)} %copy-done, f32[128,2048]{1,0:T(8,128)S(1)} %get-tuple-element.83.inside_ref, f32[2,128,8]{2,1,0:T(8,128)S(1)} %get-tuple-element.84.down_ref, f32[128,2048]{1,0:T(8,128)S(1)} %copy-done.7, ...), custom_call_target="tpu_custom_call" | custom-call | flops 1 | bytes 1 | tf_op jit(solution)/shard_map/output0_0/pallas_call | solution.py:508
  65.9 2.2 %output0_1.1 = (bf16[1,128,8192]{2,1,0:T(8,128)(2,1)}, f32[8,128]{1,0:T(8,128)S(1)}) custom-call(s32[3]{0:T(128)S(1)} %pad_add_fusion.me_ref, bf16[1,128,8192]{2,1,0:T(8,128)(2,1)S(1)} %copy-done, f32[128,2048]{1,0:T(8,128)S(1)} %get-tuple-element.74.inside_ref, f32[2,128,8]{2,1,0:T(8,128)S(1)} %get-tuple-element.75.down_ref, ...), custom_call_target="tpu_custom_call", output_to_operand_aliasing={{0}: (8, {})} | custom-call | flops 1 | bytes 1 | tf_op jit(solution)/shard_map/output0_1/pallas_call | solution.py:508
  68.1 1.6 %collective-permute-done.13.refs_2_ = bf16[1040,128]{1,0:T(8,128)(2,1)S(1)} collective-permute-done((bf16[1040,128]{1,0:T(8,128)(2,1)S(1)}, bf16[1040,128]{1,0:T(8,128)(2,1)S(1)}, u32[]{:S(2)}, u32[]{:S(2)}) %collective-permute-start.13) | collective-permute-done | bytes 266272 | tf_op jit(solution)/shard_map/ppermute | solution.py:367
  70.9 2.2 %output1_0.1 = (bf16[1,128,8192]{2,1,0:T(8,128)(2,1)}, f32[8,128]{1,0:T(8,128)S(1)}) custom-call(s32[3]{0:T(128)S(1)} %pad_add_fusion.me_ref, bf16[1,128,8192]{2,1,0:T(8,128)(2,1)S(1)} %copy-done, f32[128,2048]{1,0:T(8,128)S(1)} %get-tuple-element.92.inside_ref, f32[2,128,8]{2,1,0:T(8,128)S(1)} %get-tuple-element.93.down_ref, ...), custom_call_target="tpu_custom_call", output_to_operand_aliasing={{0}: (9, {})} | custom-call | flops 20000000000 | bytes 1 | tf_op jit(solution)/shard_map/output1_0/pallas_call | solution.py:508
  73.2 2.7 %output1_1.1 = (bf16[1,128,8192]{2,1,0:T(8,128)(2,1)}, f32[8,128]{1,0:T(8,128)}) custom-call(s32[3]{0:T(128)S(1)} %pad_add_fusion.me_ref, bf16[1,128,8192]{2,1,0:T(8,128)(2,1)S(1)} %copy-done, f32[128,2048]{1,0:T(8,128)S(1)} %get-tuple-element.65.inside_ref, f32[2,128,8]{2,1,0:T(8,128)S(1)} %get-tuple-element.66.down_ref, ...), custom_call_target="tpu_custom_call", output_to_operand_aliasing={{0}: (8, {})} | custom-call | flops 1 | bytes 1 | tf_op jit(solution)/shard_map/output1_1/pallas_call | solution.py:508
  (57 shorter events, 9.1 us)
Async XLA Ops:
  0.0 12.0 %collective-permute-start = (bf16[1,128,8192]{2,1,0:T(8,128)(2,1)}, bf16[1,128,8192]{2,1,0:T(8,128)(2,1)S(1)}, u32[]{:S(2)}, u32[]{:S(2)}) collective-permute-start(bf16[1,128,8192]{2,1,0:T(8,128)(2,1)} %keys_ref.7), channel_id=1, source_target_pairs={{0,1},{1,0},{2,3},{3,2},{4,5},{5,4},{6,7},{7,6},{8,9},{9,8},{10,11... | collective-permute-start | bytes 6291464 | tf_op jit(solution)/shard_map/ppermute | solution.py:341
  0.5 11.6 %collective-permute-start.1 = (bf16[1,128,8192]{2,1,0:T(8,128)(2,1)}, bf16[1,128,8192]{2,1,0:T(8,128)(2,1)}, u32[]{:S(2)}, u32[]{:S(2)}) collective-permute-start(bf16[1,128,8192]{2,1,0:T(8,128)(2,1)} %values_ref.7), channel_id=1, source_target_pairs={{0,1},{1,0},{2,3},{3,2},{4,5},{5,4},{6,7},{7,6},{8,9},{9,8},{10,11... | collective-permute-start | bytes 6291464 | tf_op jit(solution)/shard_map/ppermute | solution.py:340
  1.9 10.1 %all-to-all-start = ((f32[8,16,128]{2,1,0:T(8,128)}), f32[8,16,128]{2,1,0:T(8,128)S(1)}, u32[]{:S(2)}, u32[]{:S(2)}) async-start(f32[8,16,128]{2,1,0:T(8,128)} %pack.1), calls=%async_computation | async-start | bytes 131072 | tf_op jit(solution)/shard_map/all_to_all | solution.py:347
  14.2 15.4 %collective-permute-start.7 = (bf16[2,528,128]{2,1,0:T(8,128)(2,1)S(1)}, bf16[2,528,128]{2,1,0:T(8,128)(2,1)S(1)}, u32[]{:S(2)}, u32[]{:S(2)}) collective-permute-start(bf16[2,528,128]{2,1,0:T(8,128)(2,1)S(1)} %get-tuple-element.61), channel_id=1, source_target_pairs={{0,24},{8,16},{16,8},{24,0},{1,25},{9,17},{17,9},{25,1},{2,26},{10... | collective-permute-start | bytes 811016 | tf_op jit(solution)/shard_map/ppermute | solution.py:367
  14.9 5.1 %copy-start = (bf16[1,128,8192]{2,1,0:T(8,128)(2,1)S(1)}, bf16[1,128,8192]{2,1,0:T(8,128)(2,1)}, u32[]{:S(2)}) copy-start(bf16[1,128,8192]{2,1,0:T(8,128)(2,1)} %queries_ref.15) | copy-start | bytes 6291460
  14.9 5.1 %copy-start.1 = (bf16[1,128,8192]{2,1,0:T(8,128)(2,1)S(1)}, bf16[1,128,8192]{2,1,0:T(8,128)(2,1)}, u32[]{:S(2)}) copy-start(bf16[1,128,8192]{2,1,0:T(8,128)(2,1)} %keys_ref.7) | copy-start | bytes 6291460
  14.9 5.1 %copy-start.3 = (bf16[1,128,8192]{2,1,0:T(8,128)(2,1)S(1)}, bf16[1,128,8192]{2,1,0:T(8,128)(2,1)}, u32[]{:S(2)}) copy-start(bf16[1,128,8192]{2,1,0:T(8,128)(2,1)} %values_ref.7) | copy-start | bytes 6291460
  14.9 15.6 %collective-permute-start.6 = (bf16[2,528,128]{2,1,0:T(8,128)(2,1)S(1)}, bf16[2,528,128]{2,1,0:T(8,128)(2,1)S(1)}, u32[]{:S(2)}, u32[]{:S(2)}) collective-permute-start(bf16[2,528,128]{2,1,0:T(8,128)(2,1)S(1)} %get-tuple-element.52.refs_4_), channel_id=1, source_target_pairs={{0,16},{8,24},{16,0},{24,8},{1,17},{9,25},{17,1},{25,9},{2,18},{10... | collective-permute-start | bytes 811016 | tf_op jit(solution)/shard_map/ppermute | solution.py:367
  18.5 12.0 %collective-permute-start.5 = (bf16[2,528,128]{2,1,0:T(8,128)(2,1)S(1)}, bf16[2,528,128]{2,1,0:T(8,128)(2,1)S(1)}, u32[]{:S(2)}, u32[]{:S(2)}) collective-permute-start(bf16[2,528,128]{2,1,0:T(8,128)(2,1)S(1)} %get-tuple-element.60), channel_id=1, source_target_pairs={{0,8},{8,0},{16,24},{24,16},{1,9},{9,1},{17,25},{25,17},{2,10},{10... | collective-permute-start | bytes 811016 | tf_op jit(solution)/shard_map/ppermute | solution.py:367
  23.4 9.5 %copy-start.2 = (bf16[1,128,8192]{2,1,0:T(8,128)(2,1)S(1)}, bf16[1,128,8192]{2,1,0:T(8,128)(2,1)}, u32[]{:S(2)}) copy-start(bf16[1,128,8192]{2,1,0:T(8,128)(2,1)} %keys_ref.7) | copy-start | bytes 6291460
  23.4 9.5 %copy-start.4 = (bf16[1,128,8192]{2,1,0:T(8,128)(2,1)S(1)}, bf16[1,128,8192]{2,1,0:T(8,128)(2,1)}, u32[]{:S(2)}) copy-start(bf16[1,128,8192]{2,1,0:T(8,128)(2,1)} %values_ref.7) | copy-start | bytes 6291460
  26.9 15.9 %collective-permute-start.2 = (bf16[2,528,128]{2,1,0:T(8,128)(2,1)S(1)}, bf16[2,528,128]{2,1,0:T(8,128)(2,1)S(1)}, u32[]{:S(2)}, u32[]{:S(2)}) collective-permute-start(bf16[2,528,128]{2,1,0:T(8,128)(2,1)S(1)} %get-tuple-element.57), channel_id=1, source_target_pairs={{0,8},{8,0},{16,24},{24,16},{1,9},{9,1},{17,25},{25,17},{2,10},{10... | collective-permute-start | bytes 811016 | tf_op jit(solution)/shard_map/ppermute | solution.py:367
  27.5 15.3 %collective-permute-start.4 = (bf16[2,528,128]{2,1,0:T(8,128)(2,1)S(1)}, bf16[2,528,128]{2,1,0:T(8,128)(2,1)S(1)}, u32[]{:S(2)}, u32[]{:S(2)}) collective-permute-start(bf16[2,528,128]{2,1,0:T(8,128)(2,1)S(1)} %get-tuple-element.59), channel_id=1, source_target_pairs={{0,24},{8,16},{16,8},{24,0},{1,25},{9,17},{17,9},{25,1},{2,26},{10... | collective-permute-start | bytes 811016 | tf_op jit(solution)/shard_map/ppermute | solution.py:367
  29.7 13.2 %collective-permute-start.3 = (bf16[2,528,128]{2,1,0:T(8,128)(2,1)S(1)}, bf16[2,528,128]{2,1,0:T(8,128)(2,1)S(1)}, u32[]{:S(2)}, u32[]{:S(2)}) collective-permute-start(bf16[2,528,128]{2,1,0:T(8,128)(2,1)S(1)} %get-tuple-element.58.refs_4_), channel_id=1, source_target_pairs={{0,16},{8,24},{16,0},{24,8},{1,17},{9,25},{17,1},{25,9},{2,18},{10... | collective-permute-start | bytes 811016 | tf_op jit(solution)/shard_map/ppermute | solution.py:367
  31.4 5.1 %collective-permute-start.8 = (bf16[528,128]{1,0:T(8,128)(2,1)S(1)}, bf16[528,128]{1,0:T(8,128)(2,1)S(1)}, u32[]{:S(2)}, u32[]{:S(2)}) collective-permute-start(bf16[528,128]{1,0:T(8,128)(2,1)S(1)} %total0.1.rest_0_.mine_ref), channel_id=1, source_target_pairs={{0,2},{2,0},{4,6},{6,4},{1,3},{3,1},{5,7},{7,5},{8,10},{10,8},{12,... | collective-permute-start | bytes 405512 | tf_op jit(solution)/shard_map/ppermute | solution.py:438
  34.7 10.7 %copy-start.8 = (bf16[2048]{0:T(1024)(128)(2,1)S(1)}, bf16[2048]{0:T(1024)(128)(2,1)}, u32[]{:S(2)}) copy-start(bf16[2048]{0:T(1024)(128)(2,1)} %param.11) | copy-start | bytes 12292
  37.1 8.3 %collective-permute-start.10 = (bf16[528,128]{1,0:T(8,128)(2,1)S(1)}, bf16[528,128]{1,0:T(8,128)(2,1)S(1)}, u32[]{:S(2)}, u32[]{:S(2)}) collective-permute-start(bf16[528,128]{1,0:T(8,128)(2,1)S(1)} %widen0_0.1.refs_0_), channel_id=1, source_target_pairs={{0,4},{2,6},{4,0},{6,2},{1,5},{3,7},{5,1},{7,3},{8,12},{10,14},{12... | collective-permute-start | bytes 405512 | tf_op jit(solution)/shard_map/ppermute | solution.py:438
  43.7 6.2 %collective-permute-start.9 = (bf16[528,128]{1,0:T(8,128)(2,1)S(1)}, bf16[528,128]{1,0:T(8,128)(2,1)S(1)}, u32[]{:S(2)}, u32[]{:S(2)}) collective-permute-start(bf16[528,128]{1,0:T(8,128)(2,1)S(1)} %total1.1.refs_6_.mine_ref), channel_id=1, source_target_pairs={{0,2},{2,0},{4,6},{6,4},{1,3},{3,1},{5,7},{7,5},{8,10},{10,8},{12,... | collective-permute-start | bytes 405512 | tf_op jit(solution)/shard_map/ppermute | solution.py:438
  46.4 14.3 %collective-permute-start.15 = (bf16[1040,128]{1,0:T(8,128)(2,1)S(1)}, bf16[1040,128]{1,0:T(8,128)(2,1)S(1)}, u32[]{:S(2)}, u32[]{:S(2)}) collective-permute-start(bf16[1040,128]{1,0:T(8,128)(2,1)S(1)} %get-tuple-element.77), channel_id=1, source_target_pairs={{0,8},{8,0},{16,24},{24,16},{1,9},{9,1},{17,25},{25,17},{2,10},{10... | collective-permute-start | bytes 798728 | tf_op jit(solution)/shard_map/ppermute | solution.py:367
  47.0 15.4 %collective-permute-start.16 = (bf16[1040,128]{1,0:T(8,128)(2,1)S(1)}, bf16[1040,128]{1,0:T(8,128)(2,1)S(1)}, u32[]{:S(2)}, u32[]{:S(2)}) collective-permute-start(bf16[1040,128]{1,0:T(8,128)(2,1)S(1)} %get-tuple-element.78), channel_id=1, source_target_pairs={{0,16},{8,24},{16,0},{24,8},{1,17},{9,25},{17,1},{25,9},{2,18},{10... | collective-permute-start | bytes 798728 | tf_op jit(solution)/shard_map/ppermute | solution.py:367
  48.2 14.2 %collective-permute-start.17 = (bf16[1040,128]{1,0:T(8,128)(2,1)S(1)}, bf16[1040,128]{1,0:T(8,128)(2,1)S(1)}, u32[]{:S(2)}, u32[]{:S(2)}) collective-permute-start(bf16[1040,128]{1,0:T(8,128)(2,1)S(1)} %get-tuple-element.79), channel_id=1, source_target_pairs={{0,24},{8,16},{16,8},{24,0},{1,25},{9,17},{17,9},{25,1},{2,26},{10... | collective-permute-start | bytes 798728 | tf_op jit(solution)/shard_map/ppermute | solution.py:367
  50.6 7.3 %collective-permute-start.11 = (bf16[528,128]{1,0:T(8,128)(2,1)S(1)}, bf16[528,128]{1,0:T(8,128)(2,1)S(1)}, u32[]{:S(2)}, u32[]{:S(2)}) collective-permute-start(bf16[528,128]{1,0:T(8,128)(2,1)S(1)} %widen1_0.1.rest_0_), channel_id=1, source_target_pairs={{0,4},{2,6},{4,0},{6,2},{1,5},{3,7},{5,1},{7,3},{8,12},{10,14},{12... | collective-permute-start | bytes 405512 | tf_op jit(solution)/shard_map/ppermute | solution.py:438
  54.2 9.4 %copy-start.7 = (f32[128,2048]{1,0:T(8,128)S(1)}, f32[128,2048]{1,0:T(8,128)}, u32[]{:S(2)}) copy-start(f32[128,2048]{1,0:T(8,128)} %get-tuple-element.85.gate_ref) | copy-start | bytes 3145732
  58.9 9.2 %collective-permute-start.12 = (bf16[1040,128]{1,0:T(8,128)(2,1)S(1)}, bf16[1040,128]{1,0:T(8,128)(2,1)S(1)}, u32[]{:S(2)}, u32[]{:S(2)}) collective-permute-start(bf16[1040,128]{1,0:T(8,128)(2,1)S(1)} %get-tuple-element.71), channel_id=1, source_target_pairs={{0,8},{8,0},{16,24},{24,16},{1,9},{9,1},{17,25},{25,17},{2,10},{10... | collective-permute-start | bytes 798728 | tf_op jit(solution)/shard_map/ppermute | solution.py:367
  59.5 10.2 %collective-permute-start.13 = (bf16[1040,128]{1,0:T(8,128)(2,1)S(1)}, bf16[1040,128]{1,0:T(8,128)(2,1)S(1)}, u32[]{:S(2)}, u32[]{:S(2)}) collective-permute-start(bf16[1040,128]{1,0:T(8,128)(2,1)S(1)} %get-tuple-element.72), channel_id=1, source_target_pairs={{0,16},{8,24},{16,0},{24,8},{1,17},{9,25},{17,1},{25,9},{2,18},{10... | collective-permute-start | bytes 798728 | tf_op jit(solution)/shard_map/ppermute | solution.py:367
  60.7 9.0 %collective-permute-start.14 = (bf16[1040,128]{1,0:T(8,128)(2,1)S(1)}, bf16[1040,128]{1,0:T(8,128)(2,1)S(1)}, u32[]{:S(2)}, u32[]{:S(2)}) collective-permute-start(bf16[1040,128]{1,0:T(8,128)(2,1)S(1)} %get-tuple-element.73), channel_id=1, source_target_pairs={{0,24},{8,16},{16,8},{24,0},{1,25},{9,17},{17,9},{25,1},{2,26},{10... | collective-permute-start | bytes 798728 | tf_op jit(solution)/shard_map/ppermute | solution.py:367
  63.1 2.8 %collective-permute-start.18 = (bf16[2,512,128]{2,1,0:T(8,128)(2,1)S(1)}, bf16[2,512,128]{2,1,0:T(8,128)(2,1)S(1)}, u32[]{:S(2)}, u32[]{:S(2)}) collective-permute-start(bf16[2,512,128]{2,1,0:T(8,128)(2,1)S(1)} %get-tuple-element.80), channel_id=1, source_target_pairs={{0,1},{1,0},{2,3},{3,2},{4,5},{5,4},{6,7},{7,6},{8,9},{9,8},{10,11... | collective-permute-start | bytes 786440 | tf_op jit(solution)/shard_map/ppermute | solution.py:534
  63.1 2.7 %collective-permute-start.19 = (bf16[2,512,128]{2,1,0:T(8,128)(2,1)S(1)}, bf16[2,512,128]{2,1,0:T(8,128)(2,1)S(1)}, u32[]{:S(2)}, u32[]{:S(2)}) collective-permute-start(bf16[2,512,128]{2,1,0:T(8,128)(2,1)S(1)} %get-tuple-element.81), channel_id=1, source_target_pairs={{0,1},{1,0},{2,3},{3,2},{4,5},{5,4},{6,7},{7,6},{8,9},{9,8},{10,11... | collective-permute-start | bytes 786440 | tf_op jit(solution)/shard_map/ppermute | solution.py:534
  63.6 2.2 %copy-start.5 = (f32[128,2048]{1,0:T(8,128)S(1)}, f32[128,2048]{1,0:T(8,128)}, u32[]{:S(2)}) copy-start(f32[128,2048]{1,0:T(8,128)} %get-tuple-element.76.gate_ref) | copy-start | bytes 3145732
  65.9 5.0 %copy-start.9 = (f32[128,2048]{1,0:T(8,128)S(1)}, f32[128,2048]{1,0:T(8,128)}, u32[]{:S(2)}) copy-start(f32[128,2048]{1,0:T(8,128)} %get-tuple-element.94.gate_ref) | copy-start | bytes 3145732
  70.4 2.8 %collective-permute-start.20 = (bf16[2,512,128]{2,1,0:T(8,128)(2,1)S(1)}, bf16[2,512,128]{2,1,0:T(8,128)(2,1)S(1)}, u32[]{:S(2)}, u32[]{:S(2)}) collective-permute-start(bf16[2,512,128]{2,1,0:T(8,128)(2,1)S(1)} %get-tuple-element.89), channel_id=1, source_target_pairs={{0,1},{1,0},{2,3},{3,2},{4,5},{5,4},{6,7},{7,6},{8,9},{9,8},{10,11... | collective-permute-start | bytes 786440 | tf_op jit(solution)/shard_map/ppermute | solution.py:534
  70.4 2.7 %collective-permute-start.21 = (bf16[2,512,128]{2,1,0:T(8,128)(2,1)S(1)}, bf16[2,512,128]{2,1,0:T(8,128)(2,1)S(1)}, u32[]{:S(2)}, u32[]{:S(2)}) collective-permute-start(bf16[2,512,128]{2,1,0:T(8,128)(2,1)S(1)} %get-tuple-element.90), channel_id=1, source_target_pairs={{0,1},{1,0},{2,3},{3,2},{4,5},{5,4},{6,7},{7,6},{8,9},{9,8},{10,11... | collective-permute-start | bytes 786440 | tf_op jit(solution)/shard_map/ppermute | solution.py:534
  (1 other events, 2.2 us)

commit v2 on v0

--- a/solution.py
+++ b/solution.py
@@ -267,7 +267,8 @@
     else:
         collect(me_ref[0], core, refs[:parts], prefix_ref, gain_ref)
         prefixes, gains = [prefix_ref.at[at] for at in range(parts)], gain_ref
-    average = jnp.full((dim, dim), 1.0 / dim, jnp.bfloat16)
+    blocks = [lax.broadcasted_iota(jnp.int32, (2 * dim, 2 * dim), axis) // dim for axis in (0, 1)]
+    average = jnp.where(blocks[0] == blocks[1], 1.0 / dim, 0.0).astype(jnp.bfloat16)
     moves = []
     for turn in range(count // STEP):
         first = (1 - core if parts is None else core) * half + begin + turn * STEP
@@ -283,7 +284,10 @@
         for head in range(STEP):
             at = (turn * STEP + head) * dim
             mixed.append(inside_ref[:, at : at + dim] + carried[head] * down[:, head : head + 1])
-            means.append(dot((mixed[head] * mixed[head]).astype(jnp.bfloat16), average, NN))
+        for head in range(0, STEP, 2):
+            squares = [(mixed[at] * mixed[at]).astype(jnp.bfloat16) for at in (head, head + 1)]
+            both = dot(jnp.concatenate(squares, axis=1), average, NN)
+            means += [both[:, :dim], both[:, dim:]]
         for head in range(STEP):
             at = (turn * STEP + head) * dim
             factor = gain[head : head + 1, :] * gate_ref[:, at : at + dim]
@@ -423,8 +427,7 @@
             for at, array in enumerate(state):
                 slots[2 * masks[at // 2] + at % 2] = array
         held.append(exchange([slots[slot] for slot in range(parts)]))
-        if group == 0:
-            before = inside_part(inside_part(before))
+    before = inside_part(inside_part(before))
 
     arrived = []
     stacked = pltpu.VMEM((count, rows, dim), jnp.bfloat16)
@@ -527,13 +530,10 @@
     out = ()
     for group in range(GROUPS):
         last = group == GROUPS - 1
-        if not last:
-            out, before = output(group, 0, prefixes[group], out, before)
         *others, gains = merge(group, before, 0)
         others = [lax.ppermute(other, "core", swap) for other in others]
         before = (gains,)
-        if last:
-            out, before = output(group, 0, prefixes[group], out, before, cost=20)
+        out, before = output(group, 0, prefixes[group], out, before, cost=20 if last else 0)
         out, before = output(group, 1, (*others, gains), out, before)
     return out[0]
 

time: 76.1 us -> 75.9 us (level)
  waiting for transfers between devices: 9.23 us -> 10.3 us
    ppermute x12, waiting for transfers between devices: 0.65 us -> 2.4 us  [exchange(): arrived[slot] = lax.ppermute(slots[slot], 'head', pairs)]
    ppermute x4, waiting for transfers between devices: 1.4 us -> 0.01 us  [on_device(): others = [lax.ppermute(other, 'core', swap) for other in others]]
  transfers between devices with their start and end apart: 23 -> 23, of which waited for: 6 -> 4; matrix products, arithmetic and copies ran while one was open for 0% -> 0% of each run, Pallas kernels for 42% -> 41%
where the time goes in v2:
time: 75.9 us; the launch traced here: 75.6 us
  Pallas kernels  36.6 us (48%)
  starting transfers between devices  28.3 us (37%)
  waiting for transfers between devices  10.3 us (14%)
    ppermute x12, starting transfers between devices, exchange(): arrived[slot] = lax.ppermute(slots[slot], 'head', pairs)  14.3 us
    pallas_call x4, Pallas kernels, output(): kernel_call(functools.partial(output_kernel, dim, owned, half, group * sh...  8.62 us
    pallas_call x3, Pallas kernels, on_device(): kernel_call(functools.partial(state_kernel, dim, owned, half, group * sha...  7.48 us
    ppermute x4, starting transfers between devices, with_plane(): return lax.ppermute(total, 'z', pairs)  7.19 us
    pallas_call x4, Pallas kernels, inside_part(): kernel_call(functools.partial(inside_kernel, dim, half, group * share, sh...  6.74 us
    pallas_call x2, Pallas kernels, gates_of(): kernel_call(functools.partial(gate_kernel, half, group * share, share, di...  6.25 us
    all_to_all x1, starting transfers between devices, on_device(): decay = lax.all_to_all(packed, ('core', 'head'), 0, 0, tiled=True)  5.17 us
    all_to_all x1, waiting for transfers between devices, on_device(): decay = lax.all_to_all(packed, ('core', 'head'), 0, 0, tiled=True)  4.85 us
  transfers between devices with their start and end apart: 23, of which 4 were waited for; matrix products, arithmetic and copies ran while one was open for 0% of the time, Pallas kernels for 41%

profile of v2, /device:TPU:0, one launch (start us, length us, event | category | flops | bytes accessed | tf_op | source)
XLA Modules:
  0.0 75.6 jit_solution(4365135612622958325)
XLA Ops:
  0.5 1.4 %pack.1 = f32[8,16,128]{2,1,0:T(8,128)} custom-call(f32[1,16,512]{2,1,0:T(8,128)} %decay_ref.1), custom_call_target="tpu_custom_call" | custom-call | tf_op jit(solution)/shard_map/pack/pallas_call | solution.py:343
  1.9 5.2 %all-to-all-start = ((f32[8,16,128]{2,1,0:T(8,128)}), f32[8,16,128]{2,1,0:T(8,128)S(1)}, u32[]{:S(2)}, u32[]{:S(2)}) async-start(f32[8,16,128]{2,1,0:T(8,128)} %pack.1), calls=%async_computation | async-start | bytes 131072 | tf_op jit(solution)/shard_map/all_to_all | solution.py:348
  7.1 4.9 %all-to-all-done.decay_ref = f32[8,16,128]{2,1,0:T(8,128)S(1)} async-done(((f32[8,16,128]{2,1,0:T(8,128)}), f32[8,16,128]{2,1,0:T(8,128)S(1)}, u32[]{:S(2)}, u32[]{:S(2)}) %all-to-all-start) | async-done | bytes 65568 | tf_op jit(solution)/shard_map/all_to_all | solution.py:348
  12.0 2.2 %state0_1.1 = (bf16[2,528,128]{2,1,0:T(8,128)(2,1)S(1)}, bf16[2,528,128]{2,1,0:T(8,128)(2,1)S(1)}) custom-call(s32[3]{0:T(128)S(1)} %pad_add_fusion.me_ref, f32[8,16,128]{2,1,0:T(8,128)S(1)} %all-to-all-done.decay_ref, bf16[1,128,8192]{2,1,0:T(8,128)(2,1)} %keys_ref.7, bf16[1,128,8192]{2,1,0:T(8,128)(2,1)} %values_ref.7, ...), custom_call_target="tpu_custom_call" | custom-call | flops 1 | bytes 1 | tf_op jit(solution)/shard_map/state0_1/pallas_call | solution.py:414
  14.9 1.4 %collective-permute-start.6 = (bf16[2,528,128]{2,1,0:T(8,128)(2,1)S(1)}, bf16[2,528,128]{2,1,0:T(8,128)(2,1)S(1)}, u32[]{:S(2)}, u32[]{:S(2)}) collective-permute-start(bf16[2,528,128]{2,1,0:T(8,128)(2,1)S(1)} %get-tuple-element.52.refs_4_), channel_id=1, source_target_pairs={{0,16},{8,24},{16,0},{24,8},{1,17},{9,25},{17,1},{25,9},{2,18},{10... | collective-permute-start | bytes 811016 | tf_op jit(solution)/shard_map/ppermute | solution.py:368
  16.3 2.2 %state0_0.1 = (bf16[2,528,128]{2,1,0:T(8,128)(2,1)S(1)}, bf16[2,528,128]{2,1,0:T(8,128)(2,1)S(1)}) custom-call(s32[3]{0:T(128)S(1)} %pad_add_fusion.me_ref, f32[8,16,128]{2,1,0:T(8,128)S(1)} %all-to-all-done.decay_ref, bf16[1,128,8192]{2,1,0:T(8,128)(2,1)} %keys_ref.7, bf16[1,128,8192]{2,1,0:T(8,128)(2,1)} %values_ref.7, ...), custom_call_target="tpu_custom_call" | custom-call | flops 1 | bytes 1 | tf_op jit(solution)/shard_map/state0_0/pallas_call | solution.py:414
  18.5 1.5 %collective-permute-start.5 = (bf16[2,528,128]{2,1,0:T(8,128)(2,1)S(1)}, bf16[2,528,128]{2,1,0:T(8,128)(2,1)S(1)}, u32[]{:S(2)}, u32[]{:S(2)}) collective-permute-start(bf16[2,528,128]{2,1,0:T(8,128)(2,1)S(1)} %get-tuple-element.58), channel_id=1, source_target_pairs={{0,8},{8,0},{16,24},{24,16},{1,9},{9,1},{17,25},{25,17},{2,10},{10... | collective-permute-start | bytes 811016 | tf_op jit(solution)/shard_map/ppermute | solution.py:368
  20.0 3.1 %state1_1.1 = (bf16[2,528,128]{2,1,0:T(8,128)(2,1)S(1)}, bf16[2,528,128]{2,1,0:T(8,128)(2,1)S(1)}, bf16[2,528,128]{2,1,0:T(8,128)(2,1)S(1)}, bf16[2,528,128]{2,1,0:T(8,128)(2,1)S(1)}) custom-call(s32[3]{0:T(128)S(1)} %pad_add_fusion.me_ref, f32[8,16,128]{2,1,0:T(8,128)S(1)} %all-to-all-done.decay_ref, bf16[1,128,8192]{2,1,0:T(8,128)(2,1)} %keys_ref.7, ...), custom_call_target="tpu_custom_call" | custom-call | flops 1 | bytes 1 | tf_op jit(solution)/shard_map/state1_1/pallas_call | solution.py:414
  23.8 1.6 %collective-permute-start.4 = (bf16[2,528,128]{2,1,0:T(8,128)(2,1)S(1)}, bf16[2,528,128]{2,1,0:T(8,128)(2,1)S(1)}, u32[]{:S(2)}, u32[]{:S(2)}) collective-permute-start(bf16[2,528,128]{2,1,0:T(8,128)(2,1)S(1)} %get-tuple-element.57), channel_id=1, source_target_pairs={{0,24},{8,16},{16,8},{24,0},{1,25},{9,17},{17,9},{25,1},{2,26},{10... | collective-permute-start | bytes 811016 | tf_op jit(solution)/shard_map/ppermute | solution.py:368
  25.3 1.4 %collective-permute-start.3 = (bf16[2,528,128]{2,1,0:T(8,128)(2,1)S(1)}, bf16[2,528,128]{2,1,0:T(8,128)(2,1)S(1)}, u32[]{:S(2)}, u32[]{:S(2)}) collective-permute-start(bf16[2,528,128]{2,1,0:T(8,128)(2,1)S(1)} %get-tuple-element.56.rest_0_), channel_id=1, source_target_pairs={{0,16},{8,24},{16,0},{24,8},{1,17},{9,25},{17,1},{25,9},{2,18},{10... | collective-permute-start | bytes 811016 | tf_op jit(solution)/shard_map/ppermute | solution.py:368
  26.7 1.7 %inside0_0.1 = (f32[128,2048]{1,0:T(8,128)S(1)}, f32[2,128,8]{2,1,0:T(8,128)S(1)}, f32[8,128]{1,0:T(8,128)S(1)}) custom-call(s32[3]{0:T(128)S(1)} %pad_add_fusion.me_ref, bf16[1,128,8192]{2,1,0:T(8,128)(2,1)S(1)} %copy-done.2, bf16[1,128,8192]{2,1,0:T(8,128)(2,1)S(1)} %copy-done, bf16[1,128,8192]{2,1,0:T(8,128)(2,1)S(1)} %copy-done.1, ...), custom_call_target="tpu_custom_call" | custom-call | flops 1 | bytes 1 | tf_op jit(solution)/shard_map/inside0_0/pallas_call | solution.py:379
  28.4 1.7 %inside0_1.1 = (f32[128,2048]{1,0:T(8,128)S(1)}, f32[2,128,8]{2,1,0:T(8,128)S(1)}, f32[8,128]{1,0:T(8,128)S(1)}) custom-call(s32[3]{0:T(128)S(1)} %pad_add_fusion.me_ref, bf16[1,128,8192]{2,1,0:T(8,128)(2,1)S(1)} %copy-done.2, bf16[1,128,8192]{2,1,0:T(8,128)(2,1)S(1)} %copy-done, bf16[1,128,8192]{2,1,0:T(8,128)(2,1)S(1)} %copy-done.1, ...), custom_call_target="tpu_custom_call" | custom-call | flops 1 | bytes 1 | tf_op jit(solution)/shard_map/inside0_1/pallas_call | solution.py:379
  30.1 0.9 %total0.1.rest_0_.mine_ref = bf16[528,128]{1,0:T(8,128)(2,1)S(1)} custom-call(s32[3]{0:T(128)S(1)} %pad_add_fusion.me_ref, bf16[2,528,128]{2,1,0:T(8,128)(2,1)S(1)} %get-tuple-element.53.refs_4_.refs_0_, bf16[2,528,128]{2,1,0:T(8,128)(2,1)S(1)} %collective-permute-done.5.refs_1_, bf16[2,528,128]{2,1,0:T(8,128)(2,1)S(1)} %collective-permute-done.6.refs_2_, ...), custom_call_target="tpu_custom_call" | custom-call | flops 1 | bytes 1 | tf_op jit(solution)/shard_map/total0/pallas_call | solution.py:464
  31.0 1.6 %collective-permute-start.8 = (bf16[528,128]{1,0:T(8,128)(2,1)S(1)}, bf16[528,128]{1,0:T(8,128)(2,1)S(1)}, u32[]{:S(2)}, u32[]{:S(2)}) collective-permute-start(bf16[528,128]{1,0:T(8,128)(2,1)S(1)} %total0.1.rest_0_.mine_ref), channel_id=1, source_target_pairs={{0,2},{2,0},{4,6},{6,4},{1,3},{3,1},{5,7},{7,5},{8,10},{10,8},{12,... | collective-permute-start | bytes 405512 | tf_op jit(solution)/shard_map/ppermute | solution.py:438
  32.6 1.7 %inside1_0.1 = (f32[128,2048]{1,0:T(8,128)S(1)}, f32[2,128,8]{2,1,0:T(8,128)S(1)}, f32[8,128]{1,0:T(8,128)S(1)}) custom-call(s32[3]{0:T(128)S(1)} %pad_add_fusion.me_ref, bf16[1,128,8192]{2,1,0:T(8,128)(2,1)S(1)} %copy-done.2, bf16[1,128,8192]{2,1,0:T(8,128)(2,1)S(1)} %copy-done, bf16[1,128,8192]{2,1,0:T(8,128)(2,1)S(1)} %copy-done.1, ...), custom_call_target="tpu_custom_call" | custom-call | flops 1 | bytes 1 | tf_op jit(solution)/shard_map/inside1_0/pallas_call | solution.py:379
  34.3 1.7 %collective-permute-done.8.other_ref.refs_4_ = bf16[528,128]{1,0:T(8,128)(2,1)S(1)} collective-permute-done((bf16[528,128]{1,0:T(8,128)(2,1)S(1)}, bf16[528,128]{1,0:T(8,128)(2,1)S(1)}, u32[]{:S(2)}, u32[]{:S(2)}) %collective-permute-start.8) | collective-permute-done | bytes 135200 | tf_op jit(solution)/shard_map/ppermute | solution.py:438
  36.7 2.7 %collective-permute-start.10 = (bf16[528,128]{1,0:T(8,128)(2,1)S(1)}, bf16[528,128]{1,0:T(8,128)(2,1)S(1)}, u32[]{:S(2)}, u32[]{:S(2)}) collective-permute-start(bf16[528,128]{1,0:T(8,128)(2,1)S(1)} %widen0_0.1.refs_0_), channel_id=1, source_target_pairs={{0,4},{2,6},{4,0},{6,2},{1,5},{3,7},{5,1},{7,3},{8,12},{10,14},{12... | collective-permute-start | bytes 405512 | tf_op jit(solution)/shard_map/ppermute | solution.py:438
  39.3 3.1 %gates0.1 = (f32[128,2048]{1,0:T(8,128)}, f32[128,2048]{1,0:T(8,128)}, f32[8,128]{1,0:T(8,128)S(1)}) custom-call(s32[3]{0:T(128)S(1)} %pad_add_fusion.me_ref, bf16[1,128,8192]{2,1,0:T(8,128)(2,1)} %gate_ref.3, bf16[528,128]{1,0:T(8,128)(2,1)S(1)} %widen0_0.1.refs_0_), custom_call_target="tpu_custom_call" | custom-call | flops 1 | bytes 1 | tf_op jit(solution)/shard_map/gates0/pallas_call | solution.py:397
  43.4 1.6 %collective-permute-start.9 = (bf16[528,128]{1,0:T(8,128)(2,1)S(1)}, bf16[528,128]{1,0:T(8,128)(2,1)S(1)}, u32[]{:S(2)}, u32[]{:S(2)}) collective-permute-start(bf16[528,128]{1,0:T(8,128)(2,1)S(1)} %total1.1.refs_6_.mine_ref), channel_id=1, source_target_pairs={{0,2},{2,0},{4,6},{6,4},{1,3},{3,1},{5,7},{7,5},{8,10},{10,8},{12,... | collective-permute-start | bytes 405512 | tf_op jit(solution)/shard_map/ppermute | solution.py:438
  45.0 1.0 %prefix0.1 = (bf16[1040,128]{1,0:T(8,128)(2,1)S(1)}, bf16[1040,128]{1,0:T(8,128)(2,1)S(1)}, bf16[1040,128]{1,0:T(8,128)(2,1)S(1)}, bf16[1040,128]{1,0:T(8,128)(2,1)S(1)}) custom-call(s32[3]{0:T(128)S(1)} %pad_add_fusion.me_ref, bf16[16,128]{1,0:T(8,128)(2,1)S(1)} %bitcast.4, bf16[2,528,128]{2,1,0:T(8,128)(2,1)S(1)} %get-tuple-element.53.refs_4_.refs_0_, ...), custom_call_target="tpu_custom_call" | custom-call | flops 1 | bytes 1 | tf_op jit(solution)/shard_map/prefix0/pallas_call | solution.py:451
  47.4 2.1 %collective-permute-start.17 = (bf16[1040,128]{1,0:T(8,128)(2,1)S(1)}, bf16[1040,128]{1,0:T(8,128)(2,1)S(1)}, u32[]{:S(2)}, u32[]{:S(2)}) collective-permute-start(bf16[1040,128]{1,0:T(8,128)(2,1)S(1)} %get-tuple-element.79), channel_id=1, source_target_pairs={{0,24},{8,16},{16,8},{24,0},{1,25},{9,17},{17,9},{25,1},{2,26},{10... | collective-permute-start | bytes 798728 | tf_op jit(solution)/shard_map/ppermute | solution.py:368
  50.2 1.2 %collective-permute-start.11 = (bf16[528,128]{1,0:T(8,128)(2,1)S(1)}, bf16[528,128]{1,0:T(8,128)(2,1)S(1)}, u32[]{:S(2)}, u32[]{:S(2)}) collective-permute-start(bf16[528,128]{1,0:T(8,128)(2,1)S(1)} %widen1_0.1.rest_0_), channel_id=1, source_target_pairs={{0,4},{2,6},{4,0},{6,2},{1,5},{3,7},{5,1},{7,3},{8,12},{10,14},{12... | collective-permute-start | bytes 405512 | tf_op jit(solution)/shard_map/ppermute | solution.py:438
  51.4 1.7 %inside1_1.1 = (f32[128,2048]{1,0:T(8,128)S(1)}, f32[2,128,8]{2,1,0:T(8,128)S(1)}, f32[8,128]{1,0:T(8,128)S(1)}) custom-call(s32[3]{0:T(128)S(1)} %pad_add_fusion.me_ref, bf16[1,128,8192]{2,1,0:T(8,128)(2,1)S(1)} %copy-done.2, bf16[1,128,8192]{2,1,0:T(8,128)(2,1)S(1)} %copy-done, bf16[1,128,8192]{2,1,0:T(8,128)(2,1)S(1)} %copy-done.1, ...), custom_call_target="tpu_custom_call" | custom-call | flops 2000000000 | bytes 1 | tf_op jit(solution)/shard_map/inside1_1/pallas_call | solution.py:379
  53.1 3.1 %gates1.1 = (f32[128,2048]{1,0:T(8,128)}, f32[128,2048]{1,0:T(8,128)}, f32[8,128]{1,0:T(8,128)S(1)}) custom-call(s32[3]{0:T(128)S(1)} %pad_add_fusion.me_ref, bf16[1,128,8192]{2,1,0:T(8,128)(2,1)} %gate_ref.3, f32[8,128]{1,0:T(8,128)S(1)} %get-tuple-element.67.refs_0_), custom_call_target="tpu_custom_call" | custom-call | flops 1 | bytes 1 | tf_op jit(solution)/shard_map/gates1/pallas_call | solution.py:397
  56.3 1.3 %collective-permute-done.11.refs_5_ = bf16[528,128]{1,0:T(8,128)(2,1)S(1)} collective-permute-done((bf16[528,128]{1,0:T(8,128)(2,1)S(1)}, bf16[528,128]{1,0:T(8,128)(2,1)S(1)}, u32[]{:S(2)}, u32[]{:S(2)}) %collective-permute-start.11) | collective-permute-done | bytes 135200 | tf_op jit(solution)/shard_map/ppermute | solution.py:438
  57.5 1.0 %prefix1.1 = (bf16[1040,128]{1,0:T(8,128)(2,1)S(1)}, bf16[1040,128]{1,0:T(8,128)(2,1)S(1)}, bf16[1040,128]{1,0:T(8,128)(2,1)S(1)}, bf16[1040,128]{1,0:T(8,128)(2,1)S(1)}) custom-call(s32[3]{0:T(128)S(1)} %pad_add_fusion.me_ref, bf16[16,128]{1,0:T(8,128)(2,1)S(1)} %bitcast.5, bf16[2,528,128]{2,1,0:T(8,128)(2,1)S(1)} %get-tuple-element.54.refs_0_, ...), custom_call_target="tpu_custom_call" | custom-call | flops 1 | bytes 1 | tf_op jit(solution)/shard_map/prefix1/pallas_call | solution.py:451
  59.9 2.1 %collective-permute-start.14 = (bf16[1040,128]{1,0:T(8,128)(2,1)S(1)}, bf16[1040,128]{1,0:T(8,128)(2,1)S(1)}, u32[]{:S(2)}, u32[]{:S(2)}) collective-permute-start(bf16[1040,128]{1,0:T(8,128)(2,1)S(1)} %get-tuple-element.73), channel_id=1, source_target_pairs={{0,24},{8,16},{16,8},{24,0},{1,25},{9,17},{17,9},{25,1},{2,26},{10... | collective-permute-start | bytes 798728 | tf_op jit(solution)/shard_map/ppermute | solution.py:368
  63.3 2.0 %output0_0.1 = (bf16[1,128,8192]{2,1,0:T(8,128)(2,1)}, f32[8,128]{1,0:T(8,128)S(1)}) custom-call(s32[3]{0:T(128)S(1)} %pad_add_fusion.me_ref, bf16[1,128,8192]{2,1,0:T(8,128)(2,1)S(1)} %copy-done.2, f32[128,2048]{1,0:T(8,128)S(1)} %get-tuple-element.83.inside_ref, f32[2,128,8]{2,1,0:T(8,128)S(1)} %get-tuple-element.84.down_ref, f32[128,2048]{1,0:T(8,128)S(1)} %copy-done.5, ...), custom_call_target="tpu_custom_call" | custom-call | flops 1 | bytes 1 | tf_op jit(solution)/shard_map/output0_0/pallas_call | solution.py:508
  65.3 2.0 %output0_1.1 = (bf16[1,128,8192]{2,1,0:T(8,128)(2,1)}, f32[8,128]{1,0:T(8,128)S(1)}) custom-call(s32[3]{0:T(128)S(1)} %pad_add_fusion.me_ref, bf16[1,128,8192]{2,1,0:T(8,128)(2,1)S(1)} %copy-done.2, f32[128,2048]{1,0:T(8,128)S(1)} %get-tuple-element.74.inside_ref, f32[2,128,8]{2,1,0:T(8,128)S(1)} %get-tuple-element.75.down_ref, ...), custom_call_target="tpu_custom_call", output_to_operand_aliasing={{0}: (8, {})} | custom-call | flops 1 | bytes 1 | tf_op jit(solution)/shard_map/output0_1/pallas_call | solution.py:508
  67.4 2.4 %collective-permute-done.13.refs_2_ = bf16[1040,128]{1,0:T(8,128)(2,1)S(1)} collective-permute-done((bf16[1040,128]{1,0:T(8,128)(2,1)S(1)}, bf16[1040,128]{1,0:T(8,128)(2,1)S(1)}, u32[]{:S(2)}, u32[]{:S(2)}) %collective-permute-start.13) | collective-permute-done | bytes 266272 | tf_op jit(solution)/shard_map/ppermute | solution.py:368
  70.9 2.0 %output1_0.1 = (bf16[1,128,8192]{2,1,0:T(8,128)(2,1)}, f32[8,128]{1,0:T(8,128)S(1)}) custom-call(s32[3]{0:T(128)S(1)} %pad_add_fusion.me_ref, bf16[1,128,8192]{2,1,0:T(8,128)(2,1)S(1)} %copy-done.2, f32[128,2048]{1,0:T(8,128)S(1)} %get-tuple-element.92.inside_ref, f32[2,128,8]{2,1,0:T(8,128)S(1)} %get-tuple-element.93.down_ref, ...), custom_call_target="tpu_custom_call", output_to_operand_aliasing={{0}: (9, {})} | custom-call | flops 20000000000 | bytes 1 | tf_op jit(solution)/shard_map/output1_0/pallas_call | solution.py:508
  73.0 2.6 %output1_1.1 = (bf16[1,128,8192]{2,1,0:T(8,128)(2,1)}, f32[8,128]{1,0:T(8,128)}) custom-call(s32[3]{0:T(128)S(1)} %pad_add_fusion.me_ref, bf16[1,128,8192]{2,1,0:T(8,128)(2,1)S(1)} %copy-done.2, f32[128,2048]{1,0:T(8,128)S(1)} %get-tuple-element.65.inside_ref, f32[2,128,8]{2,1,0:T(8,128)S(1)} %get-tuple-element.66.down_ref, ...), custom_call_target="tpu_custom_call", output_to_operand_aliasing={{0}: (8, {})} | custom-call | flops 1 | bytes 1 | tf_op jit(solution)/shard_map/output1_1/pallas_call | solution.py:508
  (53 shorter events, 9.3 us)
Async XLA Ops:
  0.0 12.0 %collective-permute-start = (bf16[1,128,8192]{2,1,0:T(8,128)(2,1)}, bf16[1,128,8192]{2,1,0:T(8,128)(2,1)S(1)}, u32[]{:S(2)}, u32[]{:S(2)}) collective-permute-start(bf16[1,128,8192]{2,1,0:T(8,128)(2,1)} %keys_ref.7), channel_id=1, source_target_pairs={{0,1},{1,0},{2,3},{3,2},{4,5},{5,4},{6,7},{7,6},{8,9},{9,8},{10,11... | collective-permute-start | bytes 6291464 | tf_op jit(solution)/shard_map/ppermute | solution.py:342
  0.5 11.6 %collective-permute-start.1 = (bf16[1,128,8192]{2,1,0:T(8,128)(2,1)}, bf16[1,128,8192]{2,1,0:T(8,128)(2,1)}, u32[]{:S(2)}, u32[]{:S(2)}) collective-permute-start(bf16[1,128,8192]{2,1,0:T(8,128)(2,1)} %values_ref.7), channel_id=1, source_target_pairs={{0,1},{1,0},{2,3},{3,2},{4,5},{5,4},{6,7},{7,6},{8,9},{9,8},{10,11... | collective-permute-start | bytes 6291464 | tf_op jit(solution)/shard_map/ppermute | solution.py:341
  1.9 10.1 %all-to-all-start = ((f32[8,16,128]{2,1,0:T(8,128)}), f32[8,16,128]{2,1,0:T(8,128)S(1)}, u32[]{:S(2)}, u32[]{:S(2)}) async-start(f32[8,16,128]{2,1,0:T(8,128)} %pack.1), calls=%async_computation | async-start | bytes 131072 | tf_op jit(solution)/shard_map/all_to_all | solution.py:348
  14.2 11.1 %collective-permute-start.7 = (bf16[2,528,128]{2,1,0:T(8,128)(2,1)S(1)}, bf16[2,528,128]{2,1,0:T(8,128)(2,1)S(1)}, u32[]{:S(2)}, u32[]{:S(2)}) collective-permute-start(bf16[2,528,128]{2,1,0:T(8,128)(2,1)S(1)} %get-tuple-element.59), channel_id=1, source_target_pairs={{0,24},{8,16},{16,8},{24,0},{1,25},{9,17},{17,9},{25,1},{2,26},{10... | collective-permute-start | bytes 811016 | tf_op jit(solution)/shard_map/ppermute | solution.py:368
  14.9 15.2 %collective-permute-start.6 = (bf16[2,528,128]{2,1,0:T(8,128)(2,1)S(1)}, bf16[2,528,128]{2,1,0:T(8,128)(2,1)S(1)}, u32[]{:S(2)}, u32[]{:S(2)}) collective-permute-start(bf16[2,528,128]{2,1,0:T(8,128)(2,1)S(1)} %get-tuple-element.52.refs_4_), channel_id=1, source_target_pairs={{0,16},{8,24},{16,0},{24,8},{1,17},{9,25},{17,1},{25,9},{2,18},{10... | collective-permute-start | bytes 811016 | tf_op jit(solution)/shard_map/ppermute | solution.py:368
  18.5 11.6 %collective-permute-start.5 = (bf16[2,528,128]{2,1,0:T(8,128)(2,1)S(1)}, bf16[2,528,128]{2,1,0:T(8,128)(2,1)S(1)}, u32[]{:S(2)}, u32[]{:S(2)}) collective-permute-start(bf16[2,528,128]{2,1,0:T(8,128)(2,1)S(1)} %get-tuple-element.58), channel_id=1, source_target_pairs={{0,8},{8,0},{16,24},{24,16},{1,9},{9,1},{17,25},{25,17},{2,10},{10... | collective-permute-start | bytes 811016 | tf_op jit(solution)/shard_map/ppermute | solution.py:368
  20.0 6.7 %copy-start = (bf16[1,128,8192]{2,1,0:T(8,128)(2,1)S(1)}, bf16[1,128,8192]{2,1,0:T(8,128)(2,1)}, u32[]{:S(2)}) copy-start(bf16[1,128,8192]{2,1,0:T(8,128)(2,1)} %keys_ref.7) | copy-start | bytes 6291460
  20.0 6.7 %copy-start.1 = (bf16[1,128,8192]{2,1,0:T(8,128)(2,1)S(1)}, bf16[1,128,8192]{2,1,0:T(8,128)(2,1)}, u32[]{:S(2)}) copy-start(bf16[1,128,8192]{2,1,0:T(8,128)(2,1)} %values_ref.7) | copy-start | bytes 6291460
  20.0 6.7 %copy-start.2 = (bf16[1,128,8192]{2,1,0:T(8,128)(2,1)S(1)}, bf16[1,128,8192]{2,1,0:T(8,128)(2,1)}, u32[]{:S(2)}) copy-start(bf16[1,128,8192]{2,1,0:T(8,128)(2,1)} %queries_ref.15) | copy-start | bytes 6291460
  23.1 19.3 %collective-permute-start.2 = (bf16[2,528,128]{2,1,0:T(8,128)(2,1)S(1)}, bf16[2,528,128]{2,1,0:T(8,128)(2,1)S(1)}, u32[]{:S(2)}, u32[]{:S(2)}) collective-permute-start(bf16[2,528,128]{2,1,0:T(8,128)(2,1)S(1)} %get-tuple-element.55), channel_id=1, source_target_pairs={{0,8},{8,0},{16,24},{24,16},{1,9},{9,1},{17,25},{25,17},{2,10},{10... | collective-permute-start | bytes 811016 | tf_op jit(solution)/shard_map/ppermute | solution.py:368
  23.8 18.7 %collective-permute-start.4 = (bf16[2,528,128]{2,1,0:T(8,128)(2,1)S(1)}, bf16[2,528,128]{2,1,0:T(8,128)(2,1)S(1)}, u32[]{:S(2)}, u32[]{:S(2)}) collective-permute-start(bf16[2,528,128]{2,1,0:T(8,128)(2,1)S(1)} %get-tuple-element.57), channel_id=1, source_target_pairs={{0,24},{8,16},{16,8},{24,0},{1,25},{9,17},{17,9},{25,1},{2,26},{10... | collective-permute-start | bytes 811016 | tf_op jit(solution)/shard_map/ppermute | solution.py:368
  25.3 17.2 %collective-permute-start.3 = (bf16[2,528,128]{2,1,0:T(8,128)(2,1)S(1)}, bf16[2,528,128]{2,1,0:T(8,128)(2,1)S(1)}, u32[]{:S(2)}, u32[]{:S(2)}) collective-permute-start(bf16[2,528,128]{2,1,0:T(8,128)(2,1)S(1)} %get-tuple-element.56.rest_0_), channel_id=1, source_target_pairs={{0,16},{8,24},{16,0},{24,8},{1,17},{9,25},{17,1},{25,9},{2,18},{10... | collective-permute-start | bytes 811016 | tf_op jit(solution)/shard_map/ppermute | solution.py:368
  31.0 5.1 %collective-permute-start.8 = (bf16[528,128]{1,0:T(8,128)(2,1)S(1)}, bf16[528,128]{1,0:T(8,128)(2,1)S(1)}, u32[]{:S(2)}, u32[]{:S(2)}) collective-permute-start(bf16[528,128]{1,0:T(8,128)(2,1)S(1)} %total0.1.rest_0_.mine_ref), channel_id=1, source_target_pairs={{0,2},{2,0},{4,6},{6,4},{1,3},{3,1},{5,7},{7,5},{8,10},{10,8},{12,... | collective-permute-start | bytes 405512 | tf_op jit(solution)/shard_map/ppermute | solution.py:438
  34.3 10.7 %copy-start.6 = (bf16[2048]{0:T(1024)(128)(2,1)S(1)}, bf16[2048]{0:T(1024)(128)(2,1)}, u32[]{:S(2)}) copy-start(bf16[2048]{0:T(1024)(128)(2,1)} %param.11) | copy-start | bytes 12292
  36.7 8.3 %collective-permute-start.10 = (bf16[528,128]{1,0:T(8,128)(2,1)S(1)}, bf16[528,128]{1,0:T(8,128)(2,1)S(1)}, u32[]{:S(2)}, u32[]{:S(2)}) collective-permute-start(bf16[528,128]{1,0:T(8,128)(2,1)S(1)} %widen0_0.1.refs_0_), channel_id=1, source_target_pairs={{0,4},{2,6},{4,0},{6,2},{1,5},{3,7},{5,1},{7,3},{8,12},{10,14},{12... | collective-permute-start | bytes 405512 | tf_op jit(solution)/shard_map/ppermute | solution.py:438
  43.4 6.2 %collective-permute-start.9 = (bf16[528,128]{1,0:T(8,128)(2,1)S(1)}, bf16[528,128]{1,0:T(8,128)(2,1)S(1)}, u32[]{:S(2)}, u32[]{:S(2)}) collective-permute-start(bf16[528,128]{1,0:T(8,128)(2,1)S(1)} %total1.1.refs_6_.mine_ref), channel_id=1, source_target_pairs={{0,2},{2,0},{4,6},{6,4},{1,3},{3,1},{5,7},{7,5},{8,10},{10,8},{12,... | collective-permute-start | bytes 405512 | tf_op jit(solution)/shard_map/ppermute | solution.py:438
  46.0 13.9 %collective-permute-start.15 = (bf16[1040,128]{1,0:T(8,128)(2,1)S(1)}, bf16[1040,128]{1,0:T(8,128)(2,1)S(1)}, u32[]{:S(2)}, u32[]{:S(2)}) collective-permute-start(bf16[1040,128]{1,0:T(8,128)(2,1)S(1)} %get-tuple-element.77), channel_id=1, source_target_pairs={{0,8},{8,0},{16,24},{24,16},{1,9},{9,1},{17,25},{25,17},{2,10},{10... | collective-permute-start | bytes 798728 | tf_op jit(solution)/shard_map/ppermute | solution.py:368
  46.6 15.5 %collective-permute-start.16 = (bf16[1040,128]{1,0:T(8,128)(2,1)S(1)}, bf16[1040,128]{1,0:T(8,128)(2,1)S(1)}, u32[]{:S(2)}, u32[]{:S(2)}) collective-permute-start(bf16[1040,128]{1,0:T(8,128)(2,1)S(1)} %get-tuple-element.78), channel_id=1, source_target_pairs={{0,16},{8,24},{16,0},{24,8},{1,17},{9,25},{17,1},{25,9},{2,18},{10... | collective-permute-start | bytes 798728 | tf_op jit(solution)/shard_map/ppermute | solution.py:368
  47.4 14.6 %collective-permute-start.17 = (bf16[1040,128]{1,0:T(8,128)(2,1)S(1)}, bf16[1040,128]{1,0:T(8,128)(2,1)S(1)}, u32[]{:S(2)}, u32[]{:S(2)}) collective-permute-start(bf16[1040,128]{1,0:T(8,128)(2,1)S(1)} %get-tuple-element.79), channel_id=1, source_target_pairs={{0,24},{8,16},{16,8},{24,0},{1,25},{9,17},{17,9},{25,1},{2,26},{10... | collective-permute-start | bytes 798728 | tf_op jit(solution)/shard_map/ppermute | solution.py:368
  50.2 7.3 %collective-permute-start.11 = (bf16[528,128]{1,0:T(8,128)(2,1)S(1)}, bf16[528,128]{1,0:T(8,128)(2,1)S(1)}, u32[]{:S(2)}, u32[]{:S(2)}) collective-permute-start(bf16[528,128]{1,0:T(8,128)(2,1)S(1)} %widen1_0.1.rest_0_), channel_id=1, source_target_pairs={{0,4},{2,6},{4,0},{6,2},{1,5},{3,7},{5,1},{7,3},{8,12},{10,14},{12... | collective-permute-start | bytes 405512 | tf_op jit(solution)/shard_map/ppermute | solution.py:438
  53.1 10.1 %copy-start.5 = (f32[128,2048]{1,0:T(8,128)S(1)}, f32[128,2048]{1,0:T(8,128)}, u32[]{:S(2)}) copy-start(f32[128,2048]{1,0:T(8,128)} %get-tuple-element.85.gate_ref) | copy-start | bytes 3145732
  58.5 8.9 %collective-permute-start.12 = (bf16[1040,128]{1,0:T(8,128)(2,1)S(1)}, bf16[1040,128]{1,0:T(8,128)(2,1)S(1)}, u32[]{:S(2)}, u32[]{:S(2)}) collective-permute-start(bf16[1040,128]{1,0:T(8,128)(2,1)S(1)} %get-tuple-element.71), channel_id=1, source_target_pairs={{0,8},{8,0},{16,24},{24,16},{1,9},{9,1},{17,25},{25,17},{2,10},{10... | collective-permute-start | bytes 798728 | tf_op jit(solution)/shard_map/ppermute | solution.py:368
  59.2 10.5 %collective-permute-start.13 = (bf16[1040,128]{1,0:T(8,128)(2,1)S(1)}, bf16[1040,128]{1,0:T(8,128)(2,1)S(1)}, u32[]{:S(2)}, u32[]{:S(2)}) collective-permute-start(bf16[1040,128]{1,0:T(8,128)(2,1)S(1)} %get-tuple-element.72), channel_id=1, source_target_pairs={{0,16},{8,24},{16,0},{24,8},{1,17},{9,25},{17,1},{25,9},{2,18},{10... | collective-permute-start | bytes 798728 | tf_op jit(solution)/shard_map/ppermute | solution.py:368
  59.9 9.8 %collective-permute-start.14 = (bf16[1040,128]{1,0:T(8,128)(2,1)S(1)}, bf16[1040,128]{1,0:T(8,128)(2,1)S(1)}, u32[]{:S(2)}, u32[]{:S(2)}) collective-permute-start(bf16[1040,128]{1,0:T(8,128)(2,1)S(1)} %get-tuple-element.73), channel_id=1, source_target_pairs={{0,24},{8,16},{16,8},{24,0},{1,25},{9,17},{17,9},{25,1},{2,26},{10... | collective-permute-start | bytes 798728 | tf_op jit(solution)/shard_map/ppermute | solution.py:368
  62.7 2.6 %collective-permute-start.18 = (bf16[2,512,128]{2,1,0:T(8,128)(2,1)S(1)}, bf16[2,512,128]{2,1,0:T(8,128)(2,1)S(1)}, u32[]{:S(2)}, u32[]{:S(2)}) collective-permute-start(bf16[2,512,128]{2,1,0:T(8,128)(2,1)S(1)} %get-tuple-element.80), channel_id=1, source_target_pairs={{0,1},{1,0},{2,3},{3,2},{4,5},{5,4},{6,7},{7,6},{8,9},{9,8},{10,11... | collective-permute-start | bytes 786440 | tf_op jit(solution)/shard_map/ppermute | solution.py:534
  62.8 2.5 %collective-permute-start.19 = (bf16[2,512,128]{2,1,0:T(8,128)(2,1)S(1)}, bf16[2,512,128]{2,1,0:T(8,128)(2,1)S(1)}, u32[]{:S(2)}, u32[]{:S(2)}) collective-permute-start(bf16[2,512,128]{2,1,0:T(8,128)(2,1)S(1)} %get-tuple-element.81), channel_id=1, source_target_pairs={{0,1},{1,0},{2,3},{3,2},{4,5},{5,4},{6,7},{7,6},{8,9},{9,8},{10,11... | collective-permute-start | bytes 786440 | tf_op jit(solution)/shard_map/ppermute | solution.py:534
  63.3 2.1 %copy-start.3 = (f32[128,2048]{1,0:T(8,128)S(1)}, f32[128,2048]{1,0:T(8,128)}, u32[]{:S(2)}) copy-start(f32[128,2048]{1,0:T(8,128)} %get-tuple-element.76.gate_ref) | copy-start | bytes 3145732
  65.3 5.6 %copy-start.7 = (f32[128,2048]{1,0:T(8,128)S(1)}, f32[128,2048]{1,0:T(8,128)}, u32[]{:S(2)}) copy-start(f32[128,2048]{1,0:T(8,128)} %get-tuple-element.94.gate_ref) | copy-start | bytes 3145732
  70.4 2.6 %collective-permute-start.20 = (bf16[2,512,128]{2,1,0:T(8,128)(2,1)S(1)}, bf16[2,512,128]{2,1,0:T(8,128)(2,1)S(1)}, u32[]{:S(2)}, u32[]{:S(2)}) collective-permute-start(bf16[2,512,128]{2,1,0:T(8,128)(2,1)S(1)} %get-tuple-element.89), channel_id=1, source_target_pairs={{0,1},{1,0},{2,3},{3,2},{4,5},{5,4},{6,7},{7,6},{8,9},{9,8},{10,11... | collective-permute-start | bytes 786440 | tf_op jit(solution)/shard_map/ppermute | solution.py:534
  70.4 2.5 %collective-permute-start.21 = (bf16[2,512,128]{2,1,0:T(8,128)(2,1)S(1)}, bf16[2,512,128]{2,1,0:T(8,128)(2,1)S(1)}, u32[]{:S(2)}, u32[]{:S(2)}) collective-permute-start(bf16[2,512,128]{2,1,0:T(8,128)(2,1)S(1)} %get-tuple-element.90), channel_id=1, source_target_pairs={{0,1},{1,0},{2,3},{3,2},{4,5},{5,4},{6,7},{7,6},{8,9},{9,8},{10,11... | collective-permute-start | bytes 786440 | tf_op jit(solution)/shard_map/ppermute | solution.py:534
  70.9 2.1 %copy-start.4 = (f32[128,2048]{1,0:T(8,128)S(1)}, f32[128,2048]{1,0:T(8,128)}, u32[]{:S(2)}) copy-start(f32[128,2048]{1,0:T(8,128)} %get-tuple-element.68.gate_ref) | copy-start | bytes 3145732

commit v3 on v2

--- a/solution.py
+++ b/solution.py
@@ -91,39 +91,64 @@
     return decay_ref[block * parts + first // local, rows, :]
 
 
-def state_kernel(dim, owned, half, begin, masks, me_ref, decay_ref, *refs):
-    arrays, slots = refs[:4], refs[-3 - 2 * len(masks) : -3]
-    stacked_ref, copy_ref, done = refs[-3:]
+def load_kernel(half, begin, count, dim, me_ref, *refs):
+    sources, copies, done = refs[:4], refs[-5:-1], refs[-1]
+    width = count * dim
+    columns = pl.ds(pl.multiple_of((me_ref[1] * half + begin) * dim, width), width)
+    moves = [
+        pltpu.make_async_copy(source.at[0, :, columns], copy, done.at[at])
+        for at, (source, copy) in enumerate(zip(sources, copies))
+    ]
+    for move in moves:
+        move.start()
+    for move in moves:
+        move.wait()
+
+
+def state_kernel(dim, owned, half, begin, masks, loaded, me_ref, decay_ref, *refs):
+    arrays = refs[:4]
+    outs = refs[len(refs) - (1 if loaded else 3) - 2 * len(masks) :]
+    slots, stacked_ref = outs[: 2 * len(masks)], outs[2 * len(masks)]
     part, core = me_ref[0], me_ref[1]
-    firsts = [core * half + begin + ((part >> 1) ^ mask) * STEP for mask in masks]
+    turns = [(part >> 1) ^ mask for mask in masks]
+    firsts = [core * half + begin + turn * STEP for turn in turns]
     width = STEP * dim
-    moves = [
-        [
-            pltpu.make_async_copy(
-                ref.at[0, :, pl.ds(pl.multiple_of(first * dim, width), width)],
-                copy_ref.at[turn, at],
-                done.at[turn, at],
-            )
-            for at, ref in enumerate(arrays)
+    moves = []
+    if not loaded:
+        copy_ref, done = outs[-2:]
+        moves = [
+            [
+                pltpu.make_async_copy(
+                    ref.at[0, :, pl.ds(pl.multiple_of(first * dim, width), width)],
+                    copy_ref.at[turn, at],
+                    done.at[turn, at],
+                )
+                for at, ref in enumerate(arrays)
+            ]
+            for turn, first in enumerate(firsts)
         ]
-        for turn, first in enumerate(firsts)
-    ]
     for move in sum(moves, []):
         move.start()
+
+    def piece(turn, at, head):
+        if loaded:
+            return arrays[at][:, heads_at(turns[turn] * STEP, head, dim)]
+        return copy_ref[turn, at, :, head * dim : (head + 1) * dim]
+
     for turn, first in enumerate(firsts):
         for source in range(2):
             block = core if source == 0 else 1 - core
             decay = decays_at(decay_ref, block, first)
             weight = jnp.exp(sums_over(decay, lambda u, s: u > s))
             whole = jnp.broadcast_to(jnp.sum(decay, axis=1, keepdims=True), (STEP, dim))
-            for move in moves[turn][2 * source : 2 * source + 2]:
-                move.wait()
+            if moves:
+                for move in moves[turn][2 * source : 2 * source + 2]:
+                    move.wait()
             states = []
             for head in range(STEP):
-                c = slice(head * dim, (head + 1) * dim)
-                decayed = copy_ref[turn, 2 * source, :, c].T.astype(jnp.float32)
+                decayed = piece(turn, 2 * source, head).T.astype(jnp.float32)
                 decayed = (decayed * weight[head : head + 1, :]).astype(jnp.bfloat16)
-                states.append(dot(decayed, copy_ref[turn, 2 * source + 1, :, c], NN))
+                states.append(dot(decayed, piece(turn, 2 * source + 1, head), NN))
             for head in range(STEP):
                 owner, spot = divmod(head, owned)
                 span = slice(spot * dim, (spot + 1) * dim)
@@ -233,72 +258,76 @@
             result_ref[block * size : (block + 1) * size, :] = prefix_ref[
                 block * parts + (me_ref[0] ^ slot)
             ]
-        result_ref[2 * size :, :] = gain_ref[...]
-
-
-def collect(part, block, slots, prefix_ref, gain_ref):
-    parts, size, _ = prefix_ref.shape
+        if result_ref.shape[0] > 2 * size:
+            result_ref[2 * size :, :] = gain_ref[...]
+
+
+def merge_kernel(parts, me_ref, *refs):
+    slots, gain_ref, prefix_ref = refs[:parts], refs[-2], refs[-1]
+    others = refs[-4:-2]
+    size = prefix_ref.shape[1]
     local = gain_ref.shape[0] // parts
+    block = 1 - me_ref[1]
     for slot, slot_ref in enumerate(slots):
-        owner = part ^ slot
+        owner = me_ref[0] ^ slot
         prefix_ref[owner] = slot_ref[pl.ds(pl.multiple_of(block * size, size), size), :]
-        rows = pl.ds(pl.multiple_of(owner * local, local), local)
-        gain_ref[rows, :] = slot_ref[2 * size :, :].astype(jnp.float32)
-
-
-def merge_kernel(parts, me_ref, *refs):
-    *others, gain_ref, prefix_ref = refs[parts:] if len(refs) == parts + 4 else refs[parts + 1 :]
-    collect(me_ref[0], 1 - me_ref[1], refs[:parts], prefix_ref, gain_ref)
+        if slot_ref.shape[0] > 2 * size:
+            rows = pl.ds(pl.multiple_of(owner * local, local), local)
+            gain_ref[rows, :] = slot_ref[2 * size :, :].astype(jnp.float32)
+    if slots[0].shape[0] == 2 * size:
+        gain_ref[...] = jnp.zeros_like(gain_ref)
     each = parts // len(others)
     for turn, other_ref in enumerate(others):
         other_ref[...] = prefix_ref[turn * each : (turn + 1) * each]
 
 
 def output_kernel(
-    dim, owned, half, begin, count, parts, me_ref,
-    queries_ref, inside_ref, down_ref, gate_ref, *refs,
+    dim, owned, half, begin, masks, other, me_ref,
+    queries_ref, inside_ref, down_ref, gate_ref, gains, *refs,
 ):
-    out_ref, done_ref, prefix_ref, gain_ref, result_ref, sent = refs[-6:]
-    core = me_ref[1]
-    if parts is None:
-        *others, gains = refs[:3]
-        each = others[0].shape[0]
-        prefixes = [others[at // each].at[at % each] for at in range(each * len(others))]
+    out_ref, done_ref, prefix_ref, result_ref, sent = refs[-5:]
+    part, core = me_ref[0], me_ref[1]
+    size = owned * dim
+    if other:
+        turns, prefixes = [0, 1], [refs[0], refs[1]]
     else:
-        collect(me_ref[0], core, refs[:parts], prefix_ref, gain_ref)
-        prefixes, gains = [prefix_ref.at[at] for at in range(parts)], gain_ref
+        turns = [(part >> 1) ^ mask for mask in masks]
+        prefixes = [prefix_ref.at[turn] for turn in range(len(masks))]
+        rows = pl.ds(pl.multiple_of(core * size, size), size)
+        for turn in range(len(masks)):
+            for at in range(2):
+                prefix_ref[turn, (part & 1) ^ at] = refs[2 * turn + at][rows, :]
     blocks = [lax.broadcasted_iota(jnp.int32, (2 * dim, 2 * dim), axis) // dim for axis in (0, 1)]
     average = jnp.where(blocks[0] == blocks[1], 1.0 / dim, 0.0).astype(jnp.bfloat16)
     moves = []
-    for turn in range(count // STEP):
-        first = (1 - core if parts is None else core) * half + begin + turn * STEP
+    for at, turn in enumerate(turns):
+        first = (1 - core if other else core) * half + begin + turn * STEP
         gain = gains[pl.ds(pl.multiple_of(first, STEP), STEP), :]
         down = down_ref[turn]
         columns = [heads_at(first, head, dim) for head in range(STEP)]
+        here = [heads_at(turn * STEP, head, dim) for head in range(STEP)]
         carried = []
         for head, c in enumerate(columns):
-            owner, spot = divmod(turn * STEP + head, owned)
-            prefix = prefixes[owner][spot * dim : (spot + 1) * dim, :]
+            owner, spot = divmod(head, owned)
+            prefix = prefixes[at][owner, spot * dim : (spot + 1) * dim, :]
             carried.append(dot(queries_ref[0, :, c], prefix, NN))
         mixed, means = [], []
         for head in range(STEP):
-            at = (turn * STEP + head) * dim
-            mixed.append(inside_ref[:, at : at + dim] + carried[head] * down[:, head : head + 1])
+            mixed.append(inside_ref[:, here[head]] + carried[head] * down[:, head : head + 1])
         for head in range(0, STEP, 2):
-            squares = [(mixed[at] * mixed[at]).astype(jnp.bfloat16) for at in (head, head + 1)]
+            squares = [(value * value).astype(jnp.bfloat16) for value in mixed[head : head + 2]]
             both = dot(jnp.concatenate(squares, axis=1), average, NN)
             means += [both[:, :dim], both[:, dim:]]
         for head in range(STEP):
-            at = (turn * STEP + head) * dim
-            factor = gain[head : head + 1, :] * gate_ref[:, at : at + dim]
+            factor = gain[head : head + 1, :] * gate_ref[:, here[head]]
             normed = mixed[head] * lax.rsqrt(means[head] + 1e-06) * factor
-            result_ref[turn, :, head * dim : (head + 1) * dim] = normed.astype(jnp.bfloat16)
+            result_ref[at, :, head * dim : (head + 1) * dim] = normed.astype(jnp.bfloat16)
         width = STEP * dim
         moves.append(
             pltpu.make_async_copy(
-                result_ref.at[turn],
+                result_ref.at[at],
                 out_ref.at[0, :, pl.ds(pl.multiple_of(first * dim, width), width)],
-                sent.at[turn],
+                sent.at[at],
             )
         )
         moves[-1].start()
@@ -408,21 +437,34 @@
         )(me, in_hbm(gate), *before)
         return (made,)
 
+    slices = (*own, keys_other, values_other)
+    first_slices = kernel_call(
+        functools.partial(load_kernel, half, 0, share, dim),
+        "load",
+        [hbm] * 4,
+        [vmem] * 4,
+        [pltpu.VMEM((length, share * dim), jnp.bfloat16)] * 4,
+        [pltpu.SemaphoreType.DMA((4,))],
+    )(me, *slices)
+    first_slices = [in_vmem(array) for array in first_slices]
     for group in range(GROUPS):
         slots = {}
-        for masks in ((1,), (0,)) if group == 0 else ((1, 0),):
+        for masks in ((1, 0),):
+            loaded = group == 0
+            scratch = [pltpu.VMEM((len(masks), 2) + state_type.shape, jnp.bfloat16)]
+            if not loaded:
+                scratch += [
+                    pltpu.VMEM((len(masks), 4, length, STEP * dim), jnp.bfloat16),
+                    pltpu.SemaphoreType.DMA((len(masks), 4)),
+                ]
             state = kernel_call(
-                functools.partial(state_kernel, dim, owned, half, group * share, masks),
+                functools.partial(state_kernel, dim, owned, half, group * share, masks, loaded),
                 f"state{group}_{masks[0]}",
-                [vmem] + [hbm] * (4 + len(before)),
+                [vmem] + [vmem if loaded else hbm] * 4 + [hbm] * len(before),
                 [vmem] * (2 * len(masks)),
                 [state_type] * (2 * len(masks)),
-                [
-                    pltpu.VMEM((len(masks), 2) + state_type.shape, jnp.bfloat16),
-                    pltpu.VMEM((len(masks), 4, length, STEP * dim), jnp.bfloat16),
-                    pltpu.SemaphoreType.DMA((len(masks), 4)),
-                ],
-            )(me, decay, *own, keys_other, values_other, *before)
+                scratch,
+            )(me, decay, *(first_slices if loaded else slices), *before)
             before = tuple(state[:1])
             for at, array in enumerate(state):
                 slots[2 * masks[at // 2] + at % 2] = array
@@ -504,37 +546,42 @@
             cost=cost,
         )(me, *prefixes[group], *before)
 
-    def output(group, other, received, out, before, cost=0):
+    def output(group, other, masks, received, out, before, cost=0):
         *out, made = kernel_call(
-            functools.partial(
-                output_kernel, dim, owned, half, group * share, share, None if other else parts
-            ),
-            f"output{group}_{other}",
-            [vmem] * (4 + len(received)) + [hbm] * (len(out) + len(before)),
+            functools.partial(output_kernel, dim, owned, half, group * share, masks, other),
+            f"output{group}_{other}_{masks[0]}",
+            [vmem] * (5 + len(received)) + [hbm] * (len(out) + len(before)),
             [hbm, vmem],
             [pltpu.HBM((1, length, width), jnp.bfloat16), token],
             [
-                pltpu.VMEM(part_type.shape, part_type.dtype),
-                pltpu.VMEM(gain_type.shape, gain_type.dtype),
-                pltpu.VMEM((share // STEP, length, STEP * dim), jnp.bfloat16),
-                pltpu.SemaphoreType.DMA((share // STEP,)),
+                pltpu.VMEM((len(masks), 2, size, dim), jnp.bfloat16),
+                pltpu.VMEM((len(masks), length, STEP * dim), jnp.bfloat16),
+                pltpu.SemaphoreType.DMA((len(masks),)),
             ],
-            aliases={5 + len(received): 0} if out else {},
+            aliases={6 + len(received): 0} if out else {},
             cost=cost,
         )(
             me, queries, in_vmem(inside[group, other][0]), inside[group, other][1],
-            in_vmem(gates[group, other]), *received, *out, *before,
+            in_vmem(gates[group, other]), gains, *received, *out, *before,
         )
         return out, (made,)
 
     out = ()
     for group in range(GROUPS):
         last = group == GROUPS - 1
-        *others, gains = merge(group, before, 0)
+        slots = prefixes[group]
+        if last:
+            out, before = output(group, 0, (0,), slots[:2], out, before)
+        *others, came = merge(group, before, 0)
+        if group == 0:
+            gains = came
         others = [lax.ppermute(other, "core", swap) for other in others]
-        before = (gains,)
-        out, before = output(group, 0, prefixes[group], out, before, cost=20 if last else 0)
-        out, before = output(group, 1, (*others, gains), out, before)
+        before = (came,)
+        if last:
+            out, before = output(group, 0, (1,), slots[2:], out, before, cost=20)
+        else:
+            out, before = output(group, 0, (0, 1), slots, out, before)
+        out, before = output(group, 1, (0, 1), others, out, before)
     return out[0]
 
 

time: 75.9 us -> 78.6 us (1.036)
  waiting for transfers between devices: 10.3 us -> 5.64 us
  local copies, waits for them, and re-layouts: 0.04 us -> 3.7 us
  starting transfers between devices: 28.3 us -> 31.1 us
  Pallas kernels: 36.6 us -> 37.4 us
    all_to_all x1, waiting for transfers between devices: 4.85 us -> 0.86 us  [on_device(): decay = lax.all_to_all(packed, ('core', 'head'), 0, 0, tiled=True)]
    unnamed x16 -> x24, local copies, waits for them, and re-layouts: 0.04 us -> 3.7 us
    pallas_call x3 -> x2, Pallas kernels: 7.48 us -> 4.87 us  [on_device(): kernel_call(functools.partial(state_kernel, dim, owned, half, group * sha...]
    ppermute x12, starting transfers between devices: 14.3 us -> 16.4 us  [exchange(): arrived[slot] = lax.ppermute(slots[slot], 'head', pairs)]
    pallas_call x0 -> x1, Pallas kernels: none -> 1.95 us  [on_device(): kernel_call(functools.partial(load_kernel, half, 0, share, dim), 'load',...]
    pallas_call x4 -> x5, Pallas kernels: 8.62 us -> 10.1 us  [output(): kernel_call(functools.partial(output_kernel, dim, owned, half, group * sh...]
  transfers between devices with their start and end apart: 23 -> 23, of which waited for: 4 -> 7; matrix products, arithmetic and copies ran while one was open for 0% -> 0% of each run, Pallas kernels for 41% -> 41%
where the time goes in v3:
time: 78.6 us; the launch traced here: 78.2 us
  Pallas kernels  37.4 us (48%)
  starting transfers between devices  31.1 us (40%)
  waiting for transfers between devices  5.64 us (7%)
  local copies, waits for them, and re-layouts  3.7 us (5%)
    ppermute x12, starting transfers between devices, exchange(): arrived[slot] = lax.ppermute(slots[slot], 'head', pairs)  16.4 us
    pallas_call x5, Pallas kernels, output(): kernel_call(functools.partial(output_kernel, dim, owned, half, group * sh...  10.1 us
    ppermute x4, starting transfers between devices, with_plane(): return lax.ppermute(total, 'z', pairs)  7.91 us
    pallas_call x4, Pallas kernels, inside_part(): kernel_call(functools.partial(inside_kernel, dim, half, group * share, sh...  6.73 us
    pallas_call x2, Pallas kernels, gates_of(): kernel_call(functools.partial(gate_kernel, half, group * share, share, di...  6.22 us
    all_to_all x1, starting transfers between devices, on_device(): decay = lax.all_to_all(packed, ('core', 'head'), 0, 0, tiled=True)  5.17 us
    pallas_call x2, Pallas kernels, on_device(): kernel_call(functools.partial(state_kernel, dim, owned, half, group * sha...  4.87 us
    unnamed x24, local copies, waits for them, and re-layouts  3.7 us
  transfers between devices with their start and end apart: 23, of which 7 were waited for; matrix products, arithmetic and copies ran while one was open for 0% of the time, Pallas kernels for 41%

profile of v3, /device:TPU:0, one launch (start us, length us, event | category | flops | bytes accessed | tf_op | source)
XLA Modules:
  0.0 78.2 jit_solution(4856093140304282955)
XLA Ops:
  0.5 1.4 %pack.1 = f32[8,16,128]{2,1,0:T(8,128)} custom-call(f32[1,16,512]{2,1,0:T(8,128)} %decay_ref.1), custom_call_target="tpu_custom_call" | custom-call | tf_op jit(solution)/shard_map/pack/pallas_call | solution.py:372
  1.9 5.2 %all-to-all-start = ((f32[8,16,128]{2,1,0:T(8,128)}), f32[8,16,128]{2,1,0:T(8,128)S(1)}, u32[]{:S(2)}, u32[]{:S(2)}) async-start(f32[8,16,128]{2,1,0:T(8,128)} %pack.1), calls=%async_computation | async-start | bytes 131072 | tf_op jit(solution)/shard_map/all_to_all | solution.py:377
  7.6 1.9 %load.1 = (bf16[128,2048]{1,0:T(8,128)(2,1)S(1)}, bf16[128,2048]{1,0:T(8,128)(2,1)S(1)}, bf16[128,2048]{1,0:T(8,128)(2,1)S(1)}, bf16[128,2048]{1,0:T(8,128)(2,1)S(1)}) custom-call(s32[3]{0:T(128)S(1)} %pad_add_fusion.me_ref, bf16[1,128,8192]{2,1,0:T(8,128)(2,1)} %keys_ref.7, bf16[1,128,8192]{2,1,0:T(8,128)(2,1)} %values_ref.7, ...), custom_call_target="tpu_custom_call" | custom-call | flops 1 | bytes 1 | tf_op jit(solution)/shard_map/load/pallas_call | solution.py:441
  12.0 1.0 %copy-done.8 = bf16[128,2048]{1,0:T(8,128)(2,1)S(1)} copy-done((bf16[128,2048]{1,0:T(8,128)(2,1)S(1)}, bf16[128,2048]{1,0:T(8,128)(2,1)}, u32[]{:S(2)}) %copy-start.8) | copy-done | bytes 524312
  13.0 1.0 %copy-done.10 = bf16[128,2048]{1,0:T(8,128)(2,1)S(1)} copy-done((bf16[128,2048]{1,0:T(8,128)(2,1)S(1)}, bf16[128,2048]{1,0:T(8,128)(2,1)}, u32[]{:S(2)}) %copy-start.10) | copy-done | bytes 524312
  14.1 1.8 %state0_1.1 = (bf16[2,528,128]{2,1,0:T(8,128)(2,1)S(1)}, bf16[2,528,128]{2,1,0:T(8,128)(2,1)S(1)}, bf16[2,528,128]{2,1,0:T(8,128)(2,1)S(1)}, bf16[2,528,128]{2,1,0:T(8,128)(2,1)S(1)}) custom-call(s32[3]{0:T(128)S(1)} %pad_add_fusion.me_ref, f32[8,16,128]{2,1,0:T(8,128)S(1)} %all-to-all-done.decay_ref, bf16[128,2048]{1,0:T(8,128)(2,1)S(1)} %get-tuple-element.58.refs_0_, ...), custom_call_target="tpu_custom_call" | custom-call | flops 1 | bytes 1 | tf_op jit(solution)/shard_map/state0_1/pallas_call | solution.py:460
  15.8 2.1 %collective-permute-start.5 = (bf16[2,528,128]{2,1,0:T(8,128)(2,1)S(1)}, bf16[2,528,128]{2,1,0:T(8,128)(2,1)S(1)}, u32[]{:S(2)}, u32[]{:S(2)}) collective-permute-start(bf16[2,528,128]{2,1,0:T(8,128)(2,1)S(1)} %get-tuple-element.68), channel_id=1, source_target_pairs={{0,8},{8,0},{16,24},{24,16},{1,9},{9,1},{17,25},{25,17},{2,10},{10... | collective-permute-start | bytes 811016 | tf_op jit(solution)/shard_map/ppermute | solution.py:397
  17.9 1.5 %collective-permute-start.6 = (bf16[2,528,128]{2,1,0:T(8,128)(2,1)S(1)}, bf16[2,528,128]{2,1,0:T(8,128)(2,1)S(1)}, u32[]{:S(2)}, u32[]{:S(2)}) collective-permute-start(bf16[2,528,128]{2,1,0:T(8,128)(2,1)S(1)} %get-tuple-element.62.refs_4_), channel_id=1, source_target_pairs={{0,16},{8,24},{16,0},{24,8},{1,17},{9,25},{17,1},{25,9},{2,18},{10... | collective-permute-start | bytes 811016 | tf_op jit(solution)/shard_map/ppermute | solution.py:397
  19.5 3.1 %state1_1.1 = (bf16[2,528,128]{2,1,0:T(8,128)(2,1)S(1)}, bf16[2,528,128]{2,1,0:T(8,128)(2,1)S(1)}, bf16[2,528,128]{2,1,0:T(8,128)(2,1)S(1)}, bf16[2,528,128]{2,1,0:T(8,128)(2,1)S(1)}) custom-call(s32[3]{0:T(128)S(1)} %pad_add_fusion.me_ref, f32[8,16,128]{2,1,0:T(8,128)S(1)} %all-to-all-done.decay_ref, bf16[1,128,8192]{2,1,0:T(8,128)(2,1)} %keys_ref.7, ...), custom_call_target="tpu_custom_call" | custom-call | flops 1 | bytes 1 | tf_op jit(solution)/shard_map/state1_1/pallas_call | solution.py:460
  22.6 1.7 %collective-permute-start.2 = (bf16[2,528,128]{2,1,0:T(8,128)(2,1)S(1)}, bf16[2,528,128]{2,1,0:T(8,128)(2,1)S(1)}, u32[]{:S(2)}, u32[]{:S(2)}) collective-permute-start(bf16[2,528,128]{2,1,0:T(8,128)(2,1)S(1)} %get-tuple-element.64), channel_id=1, source_target_pairs={{0,8},{8,0},{16,24},{24,16},{1,9},{9,1},{17,25},{25,17},{2,10},{10... | collective-permute-start | bytes 811016 | tf_op jit(solution)/shard_map/ppermute | solution.py:397
  24.3 1.5 %collective-permute-start.3 = (bf16[2,528,128]{2,1,0:T(8,128)(2,1)S(1)}, bf16[2,528,128]{2,1,0:T(8,128)(2,1)S(1)}, u32[]{:S(2)}, u32[]{:S(2)}) collective-permute-start(bf16[2,528,128]{2,1,0:T(8,128)(2,1)S(1)} %get-tuple-element.65.rest_0_), channel_id=1, source_target_pairs={{0,16},{8,24},{16,0},{24,8},{1,17},{9,25},{17,1},{25,9},{2,18},{10... | collective-permute-start | bytes 811016 | tf_op jit(solution)/shard_map/ppermute | solution.py:397
  25.8 2.4 %collective-permute-start.4 = (bf16[2,528,128]{2,1,0:T(8,128)(2,1)S(1)}, bf16[2,528,128]{2,1,0:T(8,128)(2,1)S(1)}, u32[]{:S(2)}, u32[]{:S(2)}) collective-permute-start(bf16[2,528,128]{2,1,0:T(8,128)(2,1)S(1)} %get-tuple-element.66), channel_id=1, source_target_pairs={{0,24},{8,16},{16,8},{24,0},{1,25},{9,17},{17,9},{25,1},{2,26},{10... | collective-permute-start | bytes 811016 | tf_op jit(solution)/shard_map/ppermute | solution.py:397
  28.2 1.7 %inside0_0.1 = (f32[128,2048]{1,0:T(8,128)S(1)}, f32[2,128,8]{2,1,0:T(8,128)S(1)}, f32[8,128]{1,0:T(8,128)S(1)}) custom-call(s32[3]{0:T(128)S(1)} %pad_add_fusion.me_ref, bf16[1,128,8192]{2,1,0:T(8,128)(2,1)S(1)} %copy-done, bf16[1,128,8192]{2,1,0:T(8,128)(2,1)S(1)} %copy-done.1, bf16[1,128,8192]{2,1,0:T(8,128)(2,1)S(1)} %copy-done.2, ...), custom_call_target="tpu_custom_call" | custom-call | flops 1 | bytes 1 | tf_op jit(solution)/shard_map/inside0_0/pallas_call | solution.py:408
  29.9 1.7 %inside0_1.1 = (f32[128,2048]{1,0:T(8,128)S(1)}, f32[2,128,8]{2,1,0:T(8,128)S(1)}, f32[8,128]{1,0:T(8,128)S(1)}) custom-call(s32[3]{0:T(128)S(1)} %pad_add_fusion.me_ref, bf16[1,128,8192]{2,1,0:T(8,128)(2,1)S(1)} %copy-done, bf16[1,128,8192]{2,1,0:T(8,128)(2,1)S(1)} %copy-done.1, bf16[1,128,8192]{2,1,0:T(8,128)(2,1)S(1)} %copy-done.2, ...), custom_call_target="tpu_custom_call" | custom-call | flops 1 | bytes 1 | tf_op jit(solution)/shard_map/inside0_1/pallas_call | solution.py:408
  33.4 1.6 %collective-permute-start.8 = (bf16[528,128]{1,0:T(8,128)(2,1)S(1)}, bf16[528,128]{1,0:T(8,128)(2,1)S(1)}, u32[]{:S(2)}, u32[]{:S(2)}) collective-permute-start(bf16[528,128]{1,0:T(8,128)(2,1)S(1)} %total0.1.rest_0_.mine_ref), channel_id=1, source_target_pairs={{0,2},{2,0},{4,6},{6,4},{1,3},{3,1},{5,7},{7,5},{8,10},{10,8},{12,... | collective-permute-start | bytes 405512 | tf_op jit(solution)/shard_map/ppermute | solution.py:480
  35.0 1.7 %inside1_0.1 = (f32[128,2048]{1,0:T(8,128)S(1)}, f32[2,128,8]{2,1,0:T(8,128)S(1)}, f32[8,128]{1,0:T(8,128)S(1)}) custom-call(s32[3]{0:T(128)S(1)} %pad_add_fusion.me_ref, bf16[1,128,8192]{2,1,0:T(8,128)(2,1)S(1)} %copy-done, bf16[1,128,8192]{2,1,0:T(8,128)(2,1)S(1)} %copy-done.1, bf16[1,128,8192]{2,1,0:T(8,128)(2,1)S(1)} %copy-done.2, ...), custom_call_target="tpu_custom_call" | custom-call | flops 1 | bytes 1 | tf_op jit(solution)/shard_map/inside1_0/pallas_call | solution.py:408
  36.8 1.7 %collective-permute-done.8.other_ref.refs_4_ = bf16[528,128]{1,0:T(8,128)(2,1)S(1)} collective-permute-done((bf16[528,128]{1,0:T(8,128)(2,1)S(1)}, bf16[528,128]{1,0:T(8,128)(2,1)S(1)}, u32[]{:S(2)}, u32[]{:S(2)}) %collective-permute-start.8) | collective-permute-done | bytes 135200 | tf_op jit(solution)/shard_map/ppermute | solution.py:480
  39.1 2.7 %collective-permute-start.10 = (bf16[528,128]{1,0:T(8,128)(2,1)S(1)}, bf16[528,128]{1,0:T(8,128)(2,1)S(1)}, u32[]{:S(2)}, u32[]{:S(2)}) collective-permute-start(bf16[528,128]{1,0:T(8,128)(2,1)S(1)} %widen0_0.1.refs_0_), channel_id=1, source_target_pairs={{0,4},{2,6},{4,0},{6,2},{1,5},{3,7},{5,1},{7,3},{8,12},{10,14},{12... | collective-permute-start | bytes 405512 | tf_op jit(solution)/shard_map/ppermute | solution.py:480
  41.8 3.1 %gates0.1 = (f32[128,2048]{1,0:T(8,128)}, f32[128,2048]{1,0:T(8,128)}, f32[8,128]{1,0:T(8,128)S(1)}) custom-call(s32[3]{0:T(128)S(1)} %pad_add_fusion.me_ref, bf16[1,128,8192]{2,1,0:T(8,128)(2,1)} %gate_ref.3, bf16[528,128]{1,0:T(8,128)(2,1)S(1)} %widen0_0.1.refs_0_), custom_call_target="tpu_custom_call" | custom-call | flops 1 | bytes 1 | tf_op jit(solution)/shard_map/gates0/pallas_call | solution.py:426
  45.8 1.6 %collective-permute-start.9 = (bf16[528,128]{1,0:T(8,128)(2,1)S(1)}, bf16[528,128]{1,0:T(8,128)(2,1)S(1)}, u32[]{:S(2)}, u32[]{:S(2)}) collective-permute-start(bf16[528,128]{1,0:T(8,128)(2,1)S(1)} %total1.1.refs_6_.mine_ref), channel_id=1, source_target_pairs={{0,2},{2,0},{4,6},{6,4},{1,3},{3,1},{5,7},{7,5},{8,10},{10,8},{12,... | collective-permute-start | bytes 405512 | tf_op jit(solution)/shard_map/ppermute | solution.py:480
  48.4 1.6 %collective-permute-start.11 = (bf16[1040,128]{1,0:T(8,128)(2,1)S(1)}, bf16[1040,128]{1,0:T(8,128)(2,1)S(1)}, u32[]{:S(2)}, u32[]{:S(2)}) collective-permute-start(bf16[1040,128]{1,0:T(8,128)(2,1)S(1)} %get-tuple-element.79), channel_id=1, source_target_pairs={{0,8},{8,0},{16,24},{24,16},{1,9},{9,1},{17,25},{25,17},{2,10},{10... | collective-permute-start | bytes 798728 | tf_op jit(solution)/shard_map/ppermute | solution.py:397
  50.6 1.4 %collective-permute-start.13 = (bf16[1040,128]{1,0:T(8,128)(2,1)S(1)}, bf16[1040,128]{1,0:T(8,128)(2,1)S(1)}, u32[]{:S(2)}, u32[]{:S(2)}) collective-permute-start(bf16[1040,128]{1,0:T(8,128)(2,1)S(1)} %get-tuple-element.81), channel_id=1, source_target_pairs={{0,24},{8,16},{16,8},{24,0},{1,25},{9,17},{17,9},{25,1},{2,26},{10... | collective-permute-start | bytes 798728 | tf_op jit(solution)/shard_map/ppermute | solution.py:397
  52.7 2.0 %collective-permute-start.14 = (bf16[528,128]{1,0:T(8,128)(2,1)S(1)}, bf16[528,128]{1,0:T(8,128)(2,1)S(1)}, u32[]{:S(2)}, u32[]{:S(2)}) collective-permute-start(bf16[528,128]{1,0:T(8,128)(2,1)S(1)} %widen1_0.1.rest_0_), channel_id=1, source_target_pairs={{0,4},{2,6},{4,0},{6,2},{1,5},{3,7},{5,1},{7,3},{8,12},{10,14},{12... | collective-permute-start | bytes 405512 | tf_op jit(solution)/shard_map/ppermute | solution.py:480
  54.6 1.7 %inside1_1.1 = (f32[128,2048]{1,0:T(8,128)S(1)}, f32[2,128,8]{2,1,0:T(8,128)S(1)}, f32[8,128]{1,0:T(8,128)S(1)}) custom-call(s32[3]{0:T(128)S(1)} %pad_add_fusion.me_ref, bf16[1,128,8192]{2,1,0:T(8,128)(2,1)S(1)} %copy-done, bf16[1,128,8192]{2,1,0:T(8,128)(2,1)S(1)} %copy-done.1, bf16[1,128,8192]{2,1,0:T(8,128)(2,1)S(1)} %copy-done.2, ...), custom_call_target="tpu_custom_call" | custom-call | flops 2000000000 | bytes 1 | tf_op jit(solution)/shard_map/inside1_1/pallas_call | solution.py:408
  56.3 3.1 %gates1.1 = (f32[128,2048]{1,0:T(8,128)}, f32[128,2048]{1,0:T(8,128)}, f32[8,128]{1,0:T(8,128)S(1)}) custom-call(s32[3]{0:T(128)S(1)} %pad_add_fusion.me_ref, bf16[1,128,8192]{2,1,0:T(8,128)(2,1)} %gate_ref.3, f32[8,128]{1,0:T(8,128)S(1)} %get-tuple-element.77.refs_0_), custom_call_target="tpu_custom_call" | custom-call | flops 1 | bytes 1 | tf_op jit(solution)/shard_map/gates1/pallas_call | solution.py:426
  61.1 1.4 %collective-permute-start.15 = (bf16[1040,128]{1,0:T(8,128)(2,1)S(1)}, bf16[1040,128]{1,0:T(8,128)(2,1)S(1)}, u32[]{:S(2)}, u32[]{:S(2)}) collective-permute-start(bf16[1040,128]{1,0:T(8,128)(2,1)S(1)} %get-tuple-element.85), channel_id=1, source_target_pairs={{0,8},{8,0},{16,24},{24,16},{1,9},{9,1},{17,25},{25,17},{2,10},{10... | collective-permute-start | bytes 798728 | tf_op jit(solution)/shard_map/ppermute | solution.py:397
  63.2 1.4 %collective-permute-start.17 = (bf16[1040,128]{1,0:T(8,128)(2,1)S(1)}, bf16[1040,128]{1,0:T(8,128)(2,1)S(1)}, u32[]{:S(2)}, u32[]{:S(2)}) collective-permute-start(bf16[1040,128]{1,0:T(8,128)(2,1)S(1)} %get-tuple-element.87), channel_id=1, source_target_pairs={{0,24},{8,16},{16,8},{24,0},{1,25},{9,17},{17,9},{25,1},{2,26},{10... | collective-permute-start | bytes 798728 | tf_op jit(solution)/shard_map/ppermute | solution.py:397
  65.8 2.0 %output0_0_0.1 = (bf16[1,128,8192]{2,1,0:T(8,128)(2,1)}, f32[8,128]{1,0:T(8,128)S(1)}) custom-call(s32[3]{0:T(128)S(1)} %pad_add_fusion.me_ref, bf16[1,128,8192]{2,1,0:T(8,128)(2,1)S(1)} %copy-done, f32[128,2048]{1,0:T(8,128)S(1)} %get-tuple-element.96.inside_ref, f32[2,128,8]{2,1,0:T(8,128)S(1)} %get-tuple-element.97.down_ref, f32[128,2048]{1,0:T(8,128)S(1)} %copy-done.6, ...), custom_call_target="tpu_custom_call" | custom-call | flops 1 | bytes 1 | tf_op jit(solution)/shard_map/output0_0_0/pallas_call | solution.py:550
  67.9 2.0 %output0_1_0.1 = (bf16[1,128,8192]{2,1,0:T(8,128)(2,1)}, f32[8,128]{1,0:T(8,128)S(1)}) custom-call(s32[3]{0:T(128)S(1)} %pad_add_fusion.me_ref, bf16[1,128,8192]{2,1,0:T(8,128)(2,1)S(1)} %copy-done, f32[128,2048]{1,0:T(8,128)S(1)} %get-tuple-element.91.inside_ref, f32[2,128,8]{2,1,0:T(8,128)S(1)} %get-tuple-element.92.down_ref, ...), custom_call_target="tpu_custom_call", output_to_operand_aliasing={{0}: (8, {})} | custom-call | flops 1 | bytes 1 | tf_op jit(solution)/shard_map/output0_1_0/pallas_call | solution.py:550
  69.9 1.7 %output1_0_0.1 = (bf16[1,128,8192]{2,1,0:T(8,128)(2,1)}, f32[8,128]{1,0:T(8,128)S(1)}) custom-call(s32[3]{0:T(128)S(1)} %pad_add_fusion.me_ref, bf16[1,128,8192]{2,1,0:T(8,128)(2,1)S(1)} %copy-done, f32[128,2048]{1,0:T(8,128)S(1)} %get-tuple-element.88.inside_ref, f32[2,128,8]{2,1,0:T(8,128)S(1)} %get-tuple-element.89.down_ref, ...), custom_call_target="tpu_custom_call", output_to_operand_aliasing={{0}: (8, {})} | custom-call | flops 1 | bytes 1 | tf_op jit(solution)/shard_map/output1_0_0/pallas_call | solution.py:550
  73.8 1.7 %output1_0_1.1 = (bf16[1,128,8192]{2,1,0:T(8,128)(2,1)}, f32[8,128]{1,0:T(8,128)S(1)}) custom-call(s32[3]{0:T(128)S(1)} %pad_add_fusion.me_ref, bf16[1,128,8192]{2,1,0:T(8,128)(2,1)S(1)} %copy-done, f32[128,2048]{1,0:T(8,128)S(1)} %get-tuple-element.88.inside_ref, f32[2,128,8]{2,1,0:T(8,128)S(1)} %get-tuple-element.89.down_ref, ...), custom_call_target="tpu_custom_call", output_to_operand_aliasing={{0}: (8, {})} | custom-call | flops 20000000000 | bytes 1 | tf_op jit(solution)/shard_map/output1_0_1/pallas_call | solution.py:550
  75.6 2.6 %output1_1_0.1 = (bf16[1,128,8192]{2,1,0:T(8,128)(2,1)}, f32[8,128]{1,0:T(8,128)}) custom-call(s32[3]{0:T(128)S(1)} %pad_add_fusion.me_ref, bf16[1,128,8192]{2,1,0:T(8,128)(2,1)S(1)} %copy-done, f32[128,2048]{1,0:T(8,128)S(1)} %get-tuple-element.75.inside_ref, f32[2,128,8]{2,1,0:T(8,128)S(1)} %get-tuple-element.76.down_ref, ...), custom_call_target="tpu_custom_call", output_to_operand_aliasing={{0}: (8, {})} | custom-call | flops 1 | bytes 1 | tf_op jit(solution)/shard_map/output1_1_0/pallas_call | solution.py:550
  (62 shorter events, 14.8 us)
Async XLA Ops:
  0.0 7.1 %collective-permute-start = (bf16[1,128,8192]{2,1,0:T(8,128)(2,1)}, bf16[1,128,8192]{2,1,0:T(8,128)(2,1)S(1)}, u32[]{:S(2)}, u32[]{:S(2)}) collective-permute-start(bf16[1,128,8192]{2,1,0:T(8,128)(2,1)} %keys_ref.7), channel_id=1, source_target_pairs={{0,1},{1,0},{2,3},{3,2},{4,5},{5,4},{6,7},{7,6},{8,9},{9,8},{10,11... | collective-permute-start | bytes 6291464 | tf_op jit(solution)/shard_map/ppermute | solution.py:371
  0.5 7.1 %collective-permute-start.1 = (bf16[1,128,8192]{2,1,0:T(8,128)(2,1)}, bf16[1,128,8192]{2,1,0:T(8,128)(2,1)}, u32[]{:S(2)}, u32[]{:S(2)}) collective-permute-start(bf16[1,128,8192]{2,1,0:T(8,128)(2,1)} %values_ref.7), channel_id=1, source_target_pairs={{0,1},{1,0},{2,3},{3,2},{4,5},{5,4},{6,7},{7,6},{8,9},{9,8},{10,11... | collective-permute-start | bytes 6291464 | tf_op jit(solution)/shard_map/ppermute | solution.py:370
  1.9 10.1 %all-to-all-start = ((f32[8,16,128]{2,1,0:T(8,128)}), f32[8,16,128]{2,1,0:T(8,128)S(1)}, u32[]{:S(2)}, u32[]{:S(2)}) async-start(f32[8,16,128]{2,1,0:T(8,128)} %pack.1), calls=%async_computation | async-start | bytes 131072 | tf_op jit(solution)/shard_map/all_to_all | solution.py:377
  12.0 1.0 %copy-start.8 = (bf16[128,2048]{1,0:T(8,128)(2,1)S(1)}, bf16[128,2048]{1,0:T(8,128)(2,1)}, u32[]{:S(2)}) copy-start(bf16[128,2048]{1,0:T(8,128)(2,1)} %copy-done.7) | copy-start | bytes 1572868
  15.8 10.0 %collective-permute-start.5 = (bf16[2,528,128]{2,1,0:T(8,128)(2,1)S(1)}, bf16[2,528,128]{2,1,0:T(8,128)(2,1)S(1)}, u32[]{:S(2)}, u32[]{:S(2)}) collective-permute-start(bf16[2,528,128]{2,1,0:T(8,128)(2,1)S(1)} %get-tuple-element.68), channel_id=1, source_target_pairs={{0,8},{8,0},{16,24},{24,16},{1,9},{9,1},{17,25},{25,17},{2,10},{10... | collective-permute-start | bytes 811016 | tf_op jit(solution)/shard_map/ppermute | solution.py:397
  17.9 14.4 %collective-permute-start.6 = (bf16[2,528,128]{2,1,0:T(8,128)(2,1)S(1)}, bf16[2,528,128]{2,1,0:T(8,128)(2,1)S(1)}, u32[]{:S(2)}, u32[]{:S(2)}) collective-permute-start(bf16[2,528,128]{2,1,0:T(8,128)(2,1)S(1)} %get-tuple-element.62.refs_4_), channel_id=1, source_target_pairs={{0,16},{8,24},{16,0},{24,8},{1,17},{9,25},{17,1},{25,9},{2,18},{10... | collective-permute-start | bytes 811016 | tf_op jit(solution)/shard_map/ppermute | solution.py:397
  19.4 8.8 %copy-start = (bf16[1,128,8192]{2,1,0:T(8,128)(2,1)S(1)}, bf16[1,128,8192]{2,1,0:T(8,128)(2,1)}, u32[]{:S(2)}) copy-start(bf16[1,128,8192]{2,1,0:T(8,128)(2,1)} %queries_ref.17) | copy-start | bytes 6291460
  19.4 8.8 %copy-start.1 = (bf16[1,128,8192]{2,1,0:T(8,128)(2,1)S(1)}, bf16[1,128,8192]{2,1,0:T(8,128)(2,1)}, u32[]{:S(2)}) copy-start(bf16[1,128,8192]{2,1,0:T(8,128)(2,1)} %keys_ref.7) | copy-start | bytes 6291460
  19.4 8.8 %copy-start.2 = (bf16[1,128,8192]{2,1,0:T(8,128)(2,1)S(1)}, bf16[1,128,8192]{2,1,0:T(8,128)(2,1)}, u32[]{:S(2)}) copy-start(bf16[1,128,8192]{2,1,0:T(8,128)(2,1)} %values_ref.7) | copy-start | bytes 6291460
  19.4 13.1 %collective-permute-start.7 = (bf16[2,528,128]{2,1,0:T(8,128)(2,1)S(1)}, bf16[2,528,128]{2,1,0:T(8,128)(2,1)S(1)}, u32[]{:S(2)}, u32[]{:S(2)}) collective-permute-start(bf16[2,528,128]{2,1,0:T(8,128)(2,1)S(1)} %get-tuple-element.69), channel_id=1, source_target_pairs={{0,24},{8,16},{16,8},{24,0},{1,25},{9,17},{17,9},{25,1},{2,26},{10... | collective-permute-start | bytes 811016 | tf_op jit(solution)/shard_map/ppermute | solution.py:397
  22.6 22.3 %collective-permute-start.2 = (bf16[2,528,128]{2,1,0:T(8,128)(2,1)S(1)}, bf16[2,528,128]{2,1,0:T(8,128)(2,1)S(1)}, u32[]{:S(2)}, u32[]{:S(2)}) collective-permute-start(bf16[2,528,128]{2,1,0:T(8,128)(2,1)S(1)} %get-tuple-element.64), channel_id=1, source_target_pairs={{0,8},{8,0},{16,24},{24,16},{1,9},{9,1},{17,25},{25,17},{2,10},{10... | collective-permute-start | bytes 811016 | tf_op jit(solution)/shard_map/ppermute | solution.py:397
  24.3 20.6 %collective-permute-start.3 = (bf16[2,528,128]{2,1,0:T(8,128)(2,1)S(1)}, bf16[2,528,128]{2,1,0:T(8,128)(2,1)S(1)}, u32[]{:S(2)}, u32[]{:S(2)}) collective-permute-start(bf16[2,528,128]{2,1,0:T(8,128)(2,1)S(1)} %get-tuple-element.65.rest_0_), channel_id=1, source_target_pairs={{0,16},{8,24},{16,0},{24,8},{1,17},{9,25},{17,1},{25,9},{2,18},{10... | collective-permute-start | bytes 811016 | tf_op jit(solution)/shard_map/ppermute | solution.py:397
  25.8 19.1 %collective-permute-start.4 = (bf16[2,528,128]{2,1,0:T(8,128)(2,1)S(1)}, bf16[2,528,128]{2,1,0:T(8,128)(2,1)S(1)}, u32[]{:S(2)}, u32[]{:S(2)}) collective-permute-start(bf16[2,528,128]{2,1,0:T(8,128)(2,1)S(1)} %get-tuple-element.66), channel_id=1, source_target_pairs={{0,24},{8,16},{16,8},{24,0},{1,25},{9,17},{17,9},{25,1},{2,26},{10... | collective-permute-start | bytes 811016 | tf_op jit(solution)/shard_map/ppermute | solution.py:397
  33.4 5.1 %collective-permute-start.8 = (bf16[528,128]{1,0:T(8,128)(2,1)S(1)}, bf16[528,128]{1,0:T(8,128)(2,1)S(1)}, u32[]{:S(2)}, u32[]{:S(2)}) collective-permute-start(bf16[528,128]{1,0:T(8,128)(2,1)S(1)} %total0.1.rest_0_.mine_ref), channel_id=1, source_target_pairs={{0,2},{2,0},{4,6},{6,4},{1,3},{3,1},{5,7},{7,5},{8,10},{10,8},{12,... | collective-permute-start | bytes 405512 | tf_op jit(solution)/shard_map/ppermute | solution.py:480
  36.7 10.7 %copy-start.11 = (bf16[2048]{0:T(1024)(128)(2,1)S(1)}, bf16[2048]{0:T(1024)(128)(2,1)}, u32[]{:S(2)}) copy-start(bf16[2048]{0:T(1024)(128)(2,1)} %param.11) | copy-start | bytes 12292
  39.1 8.3 %collective-permute-start.10 = (bf16[528,128]{1,0:T(8,128)(2,1)S(1)}, bf16[528,128]{1,0:T(8,128)(2,1)S(1)}, u32[]{:S(2)}, u32[]{:S(2)}) collective-permute-start(bf16[528,128]{1,0:T(8,128)(2,1)S(1)} %widen0_0.1.refs_0_), channel_id=1, source_target_pairs={{0,4},{2,6},{4,0},{6,2},{1,5},{3,7},{5,1},{7,3},{8,12},{10,14},{12... | collective-permute-start | bytes 405512 | tf_op jit(solution)/shard_map/ppermute | solution.py:480
  45.8 6.2 %collective-permute-start.9 = (bf16[528,128]{1,0:T(8,128)(2,1)S(1)}, bf16[528,128]{1,0:T(8,128)(2,1)S(1)}, u32[]{:S(2)}, u32[]{:S(2)}) collective-permute-start(bf16[528,128]{1,0:T(8,128)(2,1)S(1)} %total1.1.refs_6_.mine_ref), channel_id=1, source_target_pairs={{0,2},{2,0},{4,6},{6,4},{1,3},{3,1},{5,7},{7,5},{8,10},{10,8},{12,... | collective-permute-start | bytes 405512 | tf_op jit(solution)/shard_map/ppermute | solution.py:480
  48.4 14.8 %collective-permute-start.11 = (bf16[1040,128]{1,0:T(8,128)(2,1)S(1)}, bf16[1040,128]{1,0:T(8,128)(2,1)S(1)}, u32[]{:S(2)}, u32[]{:S(2)}) collective-permute-start(bf16[1040,128]{1,0:T(8,128)(2,1)S(1)} %get-tuple-element.79), channel_id=1, source_target_pairs={{0,8},{8,0},{16,24},{24,16},{1,9},{9,1},{17,25},{25,17},{2,10},{10... | collective-permute-start | bytes 798728 | tf_op jit(solution)/shard_map/ppermute | solution.py:397
  50.0 14.6 %collective-permute-start.12 = (bf16[1040,128]{1,0:T(8,128)(2,1)S(1)}, bf16[1040,128]{1,0:T(8,128)(2,1)S(1)}, u32[]{:S(2)}, u32[]{:S(2)}) collective-permute-start(bf16[1040,128]{1,0:T(8,128)(2,1)S(1)} %get-tuple-element.80), channel_id=1, source_target_pairs={{0,16},{8,24},{16,0},{24,8},{1,17},{9,25},{17,1},{25,9},{2,18},{10... | collective-permute-start | bytes 798728 | tf_op jit(solution)/shard_map/ppermute | solution.py:397
  50.6 14.0 %collective-permute-start.13 = (bf16[1040,128]{1,0:T(8,128)(2,1)S(1)}, bf16[1040,128]{1,0:T(8,128)(2,1)S(1)}, u32[]{:S(2)}, u32[]{:S(2)}) collective-permute-start(bf16[1040,128]{1,0:T(8,128)(2,1)S(1)} %get-tuple-element.81), channel_id=1, source_target_pairs={{0,24},{8,16},{16,8},{24,0},{1,25},{9,17},{17,9},{25,1},{2,26},{10... | collective-permute-start | bytes 798728 | tf_op jit(solution)/shard_map/ppermute | solution.py:397
  52.7 7.4 %collective-permute-start.14 = (bf16[528,128]{1,0:T(8,128)(2,1)S(1)}, bf16[528,128]{1,0:T(8,128)(2,1)S(1)}, u32[]{:S(2)}, u32[]{:S(2)}) collective-permute-start(bf16[528,128]{1,0:T(8,128)(2,1)S(1)} %widen1_0.1.rest_0_), channel_id=1, source_target_pairs={{0,4},{2,6},{4,0},{6,2},{1,5},{3,7},{5,1},{7,3},{8,12},{10,14},{12... | collective-permute-start | bytes 405512 | tf_op jit(solution)/shard_map/ppermute | solution.py:480
  56.3 9.5 %copy-start.6 = (f32[128,2048]{1,0:T(8,128)S(1)}, f32[128,2048]{1,0:T(8,128)}, u32[]{:S(2)}) copy-start(f32[128,2048]{1,0:T(8,128)} %get-tuple-element.98.gate_ref) | copy-start | bytes 3145732
  61.1 8.9 %collective-permute-start.15 = (bf16[1040,128]{1,0:T(8,128)(2,1)S(1)}, bf16[1040,128]{1,0:T(8,128)(2,1)S(1)}, u32[]{:S(2)}, u32[]{:S(2)}) collective-permute-start(bf16[1040,128]{1,0:T(8,128)(2,1)S(1)} %get-tuple-element.85), channel_id=1, source_target_pairs={{0,8},{8,0},{16,24},{24,16},{1,9},{9,1},{17,25},{25,17},{2,10},{10... | collective-permute-start | bytes 798728 | tf_op jit(solution)/shard_map/ppermute | solution.py:397
  62.5 10.2 %collective-permute-start.16 = (bf16[1040,128]{1,0:T(8,128)(2,1)S(1)}, bf16[1040,128]{1,0:T(8,128)(2,1)S(1)}, u32[]{:S(2)}, u32[]{:S(2)}) collective-permute-start(bf16[1040,128]{1,0:T(8,128)(2,1)S(1)} %get-tuple-element.86), channel_id=1, source_target_pairs={{0,16},{8,24},{16,0},{24,8},{1,17},{9,25},{17,1},{25,9},{2,18},{10... | collective-permute-start | bytes 798728 | tf_op jit(solution)/shard_map/ppermute | solution.py:397
  63.2 9.4 %collective-permute-start.17 = (bf16[1040,128]{1,0:T(8,128)(2,1)S(1)}, bf16[1040,128]{1,0:T(8,128)(2,1)S(1)}, u32[]{:S(2)}, u32[]{:S(2)}) collective-permute-start(bf16[1040,128]{1,0:T(8,128)(2,1)S(1)} %get-tuple-element.87), channel_id=1, source_target_pairs={{0,24},{8,16},{16,8},{24,0},{1,25},{9,17},{17,9},{25,1},{2,26},{10... | collective-permute-start | bytes 798728 | tf_op jit(solution)/shard_map/ppermute | solution.py:397
  65.2 2.6 %collective-permute-start.18 = (bf16[2,512,128]{2,1,0:T(8,128)(2,1)S(1)}, bf16[2,512,128]{2,1,0:T(8,128)(2,1)S(1)}, u32[]{:S(2)}, u32[]{:S(2)}) collective-permute-start(bf16[2,512,128]{2,1,0:T(8,128)(2,1)S(1)} %get-tuple-element.94), channel_id=1, source_target_pairs={{0,1},{1,0},{2,3},{3,2},{4,5},{5,4},{6,7},{7,6},{8,9},{9,8},{10,11... | collective-permute-start | bytes 786440 | tf_op jit(solution)/shard_map/ppermute | solution.py:578
  65.3 2.6 %collective-permute-start.19 = (bf16[2,512,128]{2,1,0:T(8,128)(2,1)S(1)}, bf16[2,512,128]{2,1,0:T(8,128)(2,1)S(1)}, u32[]{:S(2)}, u32[]{:S(2)}) collective-permute-start(bf16[2,512,128]{2,1,0:T(8,128)(2,1)S(1)} %get-tuple-element.95), channel_id=1, source_target_pairs={{0,1},{1,0},{2,3},{3,2},{4,5},{5,4},{6,7},{7,6},{8,9},{9,8},{10,11... | collective-permute-start | bytes 786440 | tf_op jit(solution)/shard_map/ppermute | solution.py:578
  65.8 2.1 %copy-start.4 = (f32[128,2048]{1,0:T(8,128)S(1)}, f32[128,2048]{1,0:T(8,128)}, u32[]{:S(2)}) copy-start(f32[128,2048]{1,0:T(8,128)} %get-tuple-element.93.gate_ref) | copy-start | bytes 3145732
  67.9 2.0 %copy-start.5 = (f32[128,2048]{1,0:T(8,128)S(1)}, f32[128,2048]{1,0:T(8,128)}, u32[]{:S(2)}) copy-start(f32[128,2048]{1,0:T(8,128)} %get-tuple-element.90.gate_ref) | copy-start | bytes 3145732
  73.3 2.3 %collective-permute-start.20 = (bf16[2,512,128]{2,1,0:T(8,128)(2,1)S(1)}, bf16[2,512,128]{2,1,0:T(8,128)(2,1)S(1)}, u32[]{:S(2)}, u32[]{:S(2)}) collective-permute-start(bf16[2,512,128]{2,1,0:T(8,128)(2,1)S(1)} %get-tuple-element.104), channel_id=1, source_target_pairs={{0,1},{1,0},{2,3},{3,2},{4,5},{5,4},{6,7},{7,6},{8,9},{9,8},{10,11... | collective-permute-start | bytes 786440 | tf_op jit(solution)/shard_map/ppermute | solution.py:578
  73.3 2.2 %collective-permute-start.21 = (bf16[2,512,128]{2,1,0:T(8,128)(2,1)S(1)}, bf16[2,512,128]{2,1,0:T(8,128)(2,1)S(1)}, u32[]{:S(2)}, u32[]{:S(2)}) collective-permute-start(bf16[2,512,128]{2,1,0:T(8,128)(2,1)S(1)} %get-tuple-element.105), channel_id=1, source_target_pairs={{0,1},{1,0},{2,3},{3,2},{4,5},{5,4},{6,7},{7,6},{8,9},{9,8},{10,11... | collective-permute-start | bytes 786440 | tf_op jit(solution)/shard_map/ppermute | solution.py:578
  73.8 1.8 %copy-start.3 = (f32[128,2048]{1,0:T(8,128)S(1)}, f32[128,2048]{1,0:T(8,128)}, u32[]{:S(2)}) copy-start(f32[128,2048]{1,0:T(8,128)} %get-tuple-element.78.gate_ref) | copy-start | bytes 3145732
  (3 other events, 2.6 us)
